TPU v7x, 32 devices: a whole 2x2x4 slice. The times are simulated.
32 devices in a mesh: dp: 2 (over x), context: 4 (over y, core), tensor: 4 (over z).
Axes of the slice: x: 2, y: 2, z: 4, core: 2. Of those that a mesh axis runs over, the one named last changes fastest.
Arguments:
- tokens: bfloat16 [2, 2048, 5376], P('dp', ('context', 'tensor')), may hold values from -48 to 48
- output_gradient: bfloat16 [2, 2048, 5376], P('dp', ('context', 'tensor')), may hold values from -48 to 48
- document_index: int32 [2, 2048], P('dp'), may hold values from 0 to 3, never falling along the last dimension, each value on 1 to 1024 neighbouring positions
- query_weight: bfloat16 [5376, 4096], P(None, 'tensor'), may hold values from -1 to 1
- key_value_weight: bfloat16 [2, 5376, 2048], P(None, None, 'tensor'), may hold values from -1 to 1
- output_weight: bfloat16 [4096, 5376], P('tensor'), may hold values from -0.09375 to 0.09375
- adapter_down_projections: bfloat16 [3, 16, 5376], replicated, may hold values from -0.078125 to 0.078125
- adapter_up_query: bfloat16 [16, 4096], P(None, 'tensor'), may hold values from -0.29882812 to 0.29882812
- adapter_up_key_value: bfloat16 [2, 16, 2048], P(None, None, 'tensor'), may hold values from -0.29882812 to 0.29882812
- adapter_down_output: bfloat16 [16, 4096], P(None, 'tensor'), may hold values from -0.09375 to 0.09375
- adapter_up_output: bfloat16 [16, 5376], replicated, may hold values from -0.29882812 to 0.29882812
Outputs:
- grad_input: bfloat16 [2, 2048, 5376], P('dp', ('context', 'tensor'))
- grad_down_qkv: float32 [3, 16, 5376], replicated
- query_up_gradient: float32 [16, 4096], P(None, 'tensor')
- grad_up_keyvalue: float32 [2, 16, 2048], P(None, None, 'tensor')
- grad_down_out: float32 [16, 4096], P(None, 'tensor')
- output_up_gradient: float32 [16, 5376], replicated
Inputs may be any that keep to these rules, and one draw needn't show every extreme that they name: `document_index`: ids never fall along a sequence; each document holds 1 to half of 2048 tokens, and one holds exactly that many.
All inputs are finite; a program needn't handle non-finite values.
Results may differ from a plain program's by a relative error of at most 0.03.
Values may be sent and summed in bfloat16 or wider, within the bound.
A program may use at most 192 MiB of HBM per device.

v0:
```python
import jax
import jax.numpy as jnp
from jax import lax
from jax.sharding import PartitionSpec as P

HEAD_SIZE = 128
WINDOW = 1024


adapter_scale = 2.0
attn_scale = 168.0 ** (-0.5)
rope_base = 10000.0


def passed_along(block, axis, distance):
    devices = range(lax.axis_size(axis))
    route = [(i - distance, i) for i in devices if i - distance in devices]
    return lax.ppermute(block, axis, route)


def rope_tables(positions, head_width):
    half_width = head_width // 2
    inverse = rope_base ** (-(jnp.arange(half_width, dtype=jnp.float32) * 2.0 / head_width))
    angle = positions[:, None] * inverse[None, :]
    return (jnp.cos(angle), jnp.sin(angle))


def apply_rotation(vectors, cosine_table, sine_values):
    half_width = vectors.shape[-1] // 2
    front_half = vectors[..., :half_width]
    back_half = vectors[..., half_width:]
    cosine_table = cosine_table[:, None, :]
    sine_values = sine_values[:, None, :]
    return jnp.concatenate(
        [
            front_half * cosine_table - back_half * sine_values,
            back_half * cosine_table + front_half * sine_values,
        ],
        -1,
    )


def undo_rotation(grads, cosine_table, sine_values):
    half_width = grads.shape[-1] // 2
    front_half = grads[..., :half_width]
    back_half = grads[..., half_width:]
    cosine_table = cosine_table[:, None, :]
    sine_values = sine_values[:, None, :]
    return jnp.concatenate(
        [
            front_half * cosine_table + back_half * sine_values,
            back_half * cosine_table - front_half * sine_values,
        ],
        -1,
    )


def band_block(queries, key_rows, value_rows, attention_output_gradient, allowed):
    row_count, heads_q, head_width = queries.shape
    heads_kv = key_rows.shape[1]
    group_size = heads_q // heads_kv
    query_groups = queries.reshape(row_count, heads_kv, group_size, head_width)
    grad_groups = attention_output_gradient.reshape(row_count, heads_kv, group_size, head_width)
    scores = (
        jnp.einsum("chgd,khd->hgck", query_groups, key_rows, preferred_element_type=jnp.float32)
        * attn_scale
    )
    scores = jnp.where(allowed[None, None], scores, -1e30)
    row_max = jnp.max(scores, -1, keepdims=True)
    exponent = jnp.exp(scores - row_max)
    weights = exponent / jnp.sum(exponent, -1, keepdims=True)
    weights_low = weights.astype(jnp.bfloat16)
    attention_output = jnp.einsum(
        "hgck,khd->chgd", weights_low, value_rows, preferred_element_type=jnp.float32
    ).astype(jnp.bfloat16)
    grad_weights = jnp.einsum(
        "chgd,khd->hgck", grad_groups, value_rows, preferred_element_type=jnp.float32
    )
    row_dot = jnp.einsum(
        "chgd,chgd->hgc", grad_groups.astype(jnp.float32), attention_output.astype(jnp.float32)
    )
    grad_scores = (weights * (grad_weights - row_dot[..., None]) * attn_scale).astype(jnp.bfloat16)
    query_gradient = jnp.einsum(
        "hgck,khd->chgd", grad_scores, key_rows, preferred_element_type=jnp.float32
    )
    key_gradient = jnp.einsum(
        "hgck,chgd->khd", grad_scores, query_groups, preferred_element_type=jnp.float32
    )
    value_gradient = jnp.einsum(
        "hgck,chgd->khd", weights_low, grad_groups, preferred_element_type=jnp.float32
    )
    return (
        attention_output.reshape(row_count, heads_q, head_width),
        query_gradient.reshape(row_count, heads_q, head_width),
        key_gradient,
        value_gradient,
    )


def local(
    tokens,
    output_gradient,
    document_index,
    query_weight,
    key_value_weight,
    output_weight,
    adapter_down_projections,
    adapter_up_query,
    adapter_up_key_value,
    adapter_down_output,
    adapter_up_output,
):
    tensor_size = lax.axis_size("tensor")
    context_at = lax.axis_index("context")
    local_count = tokens.shape[1]
    model_width_size = tokens.shape[2]
    shard_len = local_count * tensor_size
    halo_count = (WINDOW - 1) // shard_len + 1
    rank_width_size = adapter_down_projections.shape[1]
    heads_q = query_weight.shape[1] // HEAD_SIZE
    heads_kv = key_value_weight.shape[2] // HEAD_SIZE
    gathered, incoming_gradient = (
        lax.all_gather(tokens[0], "tensor", axis=0, tiled=True),
        lax.all_gather(output_gradient[0], "tensor", axis=0, tiled=True),
    )
    down_factors_all = adapter_down_projections.reshape(3 * rank_width_size, model_width_size)
    adapted = jnp.einsum(
        "ja,ma->jm", gathered, down_factors_all, preferred_element_type=jnp.float32
    ).astype(jnp.bfloat16)
    adapted_query = adapted[:, :rank_width_size]
    adapted_key = adapted[:, rank_width_size : 2 * rank_width_size]
    adapted_value = adapted[:, 2 * rank_width_size :]
    query_linear = jnp.dot(
        gathered, query_weight, preferred_element_type=jnp.float32
    ) + adapter_scale * jnp.dot(adapted_query, adapter_up_query, preferred_element_type=jnp.float32)
    key_linear = jnp.dot(
        gathered, key_value_weight[0], preferred_element_type=jnp.float32
    ) + adapter_scale * jnp.dot(
        adapted_key, adapter_up_key_value[0], preferred_element_type=jnp.float32
    )
    value_linear = jnp.dot(
        gathered, key_value_weight[1], preferred_element_type=jnp.float32
    ) + adapter_scale * jnp.dot(
        adapted_value, adapter_up_key_value[1], preferred_element_type=jnp.float32
    )
    positions = (context_at * shard_len + jnp.arange(shard_len, dtype=jnp.int32)).astype(
        jnp.float32
    )
    cosine_table, sine_values = rope_tables(positions, HEAD_SIZE)
    queries = apply_rotation(
        query_linear.reshape(shard_len, heads_q, HEAD_SIZE), cosine_table, sine_values
    ).astype(jnp.bfloat16)
    key_local = apply_rotation(
        key_linear.reshape(shard_len, heads_kv, HEAD_SIZE), cosine_table, sine_values
    ).astype(jnp.bfloat16)
    value_local = value_linear.reshape(shard_len, heads_kv, HEAD_SIZE).astype(jnp.bfloat16)
    pair_local = jnp.stack([key_local, value_local], 0)
    earlier = [
        passed_along(pair_local, "context", distance) for distance in range(halo_count, 0, -1)
    ]
    pairs = jnp.concatenate(earlier + [pair_local], 1)
    segment_row = document_index[0]
    segment_pad = jnp.concatenate(
        [jnp.full((halo_count * shard_len,), -1, jnp.int32), segment_row], 0
    )
    key_seg = lax.dynamic_slice_in_dim(
        segment_pad, context_at * shard_len, (halo_count + 1) * shard_len, 0
    )
    query_seg = lax.dynamic_slice_in_dim(segment_row, context_at * shard_len, shard_len, 0)
    query_pos = context_at * shard_len + jnp.arange(shard_len, dtype=jnp.int32)
    key_pos = (context_at - halo_count) * shard_len + jnp.arange(
        (halo_count + 1) * shard_len, dtype=jnp.int32
    )
    offset = query_pos[:, None] - key_pos[None, :]
    allowed = (
        (key_pos >= 0)[None, :]
        & (offset >= 0)
        & (offset < WINDOW)
        & (query_seg[:, None] == key_seg[None, :])
    )
    up_gradient = (
        adapter_scale
        * jnp.einsum(
            "ja,ma->jm", incoming_gradient, adapter_up_output, preferred_element_type=jnp.float32
        )
    ).astype(jnp.bfloat16)
    attention_output_gradient = (
        jnp.einsum(
            "td,hd->th", incoming_gradient, output_weight, preferred_element_type=jnp.float32
        )
        + jnp.dot(up_gradient, adapter_down_output, preferred_element_type=jnp.float32)
    ).astype(jnp.bfloat16)
    attention_output, grad_query_rot, grad_keys_all, grad_values_all = band_block(
        queries,
        pairs[0],
        pairs[1],
        attention_output_gradient.reshape(shard_len, heads_q, HEAD_SIZE),
        allowed,
    )
    grad_pairs = jnp.stack([grad_keys_all, grad_values_all], 0)

    def share_for(distance):
        return lax.slice_in_dim(
            grad_pairs,
            (halo_count - distance) * shard_len,
            (halo_count - distance + 1) * shard_len,
            axis=1,
        )

    combined = share_for(0)
    for distance in range(1, halo_count + 1):
        combined = combined + passed_along(
            share_for(distance).astype(jnp.bfloat16), "context", -distance
        ).astype(jnp.float32)
    attention_output_flat = attention_output.reshape(shard_len, heads_q * HEAD_SIZE)
    query_gradient = (
        undo_rotation(grad_query_rot, cosine_table, sine_values)
        .reshape(shard_len, heads_q * HEAD_SIZE)
        .astype(jnp.bfloat16)
    )
    key_gradient = (
        undo_rotation(combined[0], cosine_table, sine_values)
        .reshape(shard_len, heads_kv * HEAD_SIZE)
        .astype(jnp.bfloat16)
    )
    value_gradient = combined[1].reshape(shard_len, heads_kv * HEAD_SIZE).astype(jnp.bfloat16)
    query_hidden = (
        adapter_scale
        * jnp.einsum(
            "kn,pn->kp", query_gradient, adapter_up_query, preferred_element_type=jnp.float32
        )
    ).astype(jnp.bfloat16)
    key_hidden = (
        adapter_scale
        * jnp.einsum(
            "kn,pn->kp", key_gradient, adapter_up_key_value[0], preferred_element_type=jnp.float32
        )
    ).astype(jnp.bfloat16)
    value_hidden = (
        adapter_scale
        * jnp.einsum(
            "kn,pn->kp", value_gradient, adapter_up_key_value[1], preferred_element_type=jnp.float32
        )
    ).astype(jnp.bfloat16)
    hidden_all = jnp.concatenate([query_hidden, key_hidden, value_hidden], 1)
    grad_down_part = jnp.einsum(
        "tr,td->rd", hidden_all, gathered, preferred_element_type=jnp.float32
    ).reshape(3, rank_width_size, model_width_size)
    query_up_gradient_piece = adapter_scale * jnp.einsum(
        "tr,th->rh", adapted_query, query_gradient, preferred_element_type=jnp.float32
    )
    grad_up_kv_part = jnp.stack(
        [
            adapter_scale
            * jnp.einsum(
                "tr,th->rh", adapted_key, key_gradient, preferred_element_type=jnp.float32
            ),
            adapter_scale
            * jnp.einsum(
                "tr,th->rh", adapted_value, value_gradient, preferred_element_type=jnp.float32
            ),
        ],
        0,
    )
    grad_down_out_part = jnp.einsum(
        "tr,th->rh", up_gradient, attention_output_flat, preferred_element_type=jnp.float32
    )
    factor_part = jnp.einsum(
        "kn,pn->kp", attention_output_flat, adapter_down_output, preferred_element_type=jnp.float32
    )
    factor_value = lax.psum(factor_part.astype(jnp.bfloat16), "tensor")
    output_up_gradient_piece = adapter_scale * jnp.einsum(
        "tr,td->rd", factor_value, incoming_gradient, preferred_element_type=jnp.float32
    )
    grad_down_qkv = lax.psum(grad_down_part, ("dp", "context", "tensor"))
    query_up_gradient, grad_up_keyvalue, grad_down_out, output_up_gradient = (
        lax.psum(query_up_gradient_piece.astype(jnp.bfloat16), ("dp", "context")).astype(
            jnp.float32
        ),
        lax.psum(grad_up_kv_part.astype(jnp.bfloat16), ("dp", "context")).astype(jnp.float32),
        lax.psum(grad_down_out_part.astype(jnp.bfloat16), ("dp", "context")).astype(jnp.float32),
        lax.psum(output_up_gradient_piece.astype(jnp.bfloat16), ("dp", "context")).astype(
            jnp.float32
        ),
    )
    term = jnp.einsum("th,dh->td", query_gradient, query_weight, preferred_element_type=jnp.float32)
    term = term + jnp.einsum(
        "th,dh->td", key_gradient, key_value_weight[0], preferred_element_type=jnp.float32
    )
    term = term + jnp.einsum(
        "th,dh->td", value_gradient, key_value_weight[1], preferred_element_type=jnp.float32
    )
    mine = lax.psum_scatter(
        (term + jnp.dot(hidden_all, down_factors_all, preferred_element_type=jnp.float32)).astype(
            jnp.bfloat16
        ),
        "tensor",
        scatter_dimension=0,
        tiled=True,
    )
    grad_input = mine[None]
    return (
        grad_input,
        grad_down_qkv,
        query_up_gradient,
        grad_up_keyvalue,
        grad_down_out,
        output_up_gradient,
    )


def solution(mesh):
    in_specs = (
        P("dp", ("context", "tensor"), None),
        P("dp", ("context", "tensor"), None),
        P("dp", None),
        P(None, "tensor"),
        P(None, None, "tensor"),
        P("tensor", None),
        P(),
        P(None, "tensor"),
        P(None, None, "tensor"),
        P(None, "tensor"),
        P(),
    )
    out_specs = (
        P("dp", ("context", "tensor"), None),
        P(),
        P(None, "tensor"),
        P(None, None, "tensor"),
        P(None, "tensor"),
        P(),
    )
    return jax.shard_map(local, mesh=mesh, in_specs=in_specs, out_specs=out_specs, check_vma=False)
```

profile of v0, /device:TPU:9, one launch (start us, length us, event | category | flops | bytes accessed | tf_op | source)
XLA Modules:
  0.0 723.8 jit_solution(9939112087460040280)
XLA Ops:
  13.9 96.6 %all-gather.5.cloned.1.call-done = bf16[1,512,5376]{2,1,0:T(8,128)(2,1)} async-done(((bf16[1,128,5376]{2,1,0:T(8,128)(2,1)}), bf16[1,512,5376]{2,1,0:T(8,128)(2,1)}) %all-gather.5.cloned.1.call-update) | async-done | bytes 5505040 | tf_op jit(solution)/shard_map/all_gather | solution.py:123
  110.5 4.4 fusion.49
  114.9 5.1 fusion.18
  120.7 7.6 %fusion.22 = f32[512,512]{0,1:T(8,128)S(1)} fusion(bf16[1,512,5376]{2,1,0:T(8,128)(2,1)} %all-gather.5.cloned.1.call-done, bf16[2,5376,512]{2,1,0:T(8,128)(2,1)} %param.15), kind=kOutput, calls=%fused_computation.31 | convolution fusion | flops 2818572288 | bytes 12058624 | tf_op jit(solution)/shard_map/dot_general | solution.py:136
  136.0 3.7 collective-permute-start.1
  142.4 70.4 %all-gather.7.cloned.1.call-done = bf16[1,512,5376]{2,1,0:T(8,128)(2,1)} async-done(((bf16[1,128,5376]{2,1,0:T(8,128)(2,1)}), bf16[1,512,5376]{2,1,0:T(8,128)(2,1)}) %all-gather.7.cloned.1.call-update) | async-done | bytes 5505040 | tf_op jit(solution)/shard_map/all_gather | solution.py:124
  212.8 4.2 fusion.56
  217.0 10.4 %fusion.14 = f32[512,1024]{1,0:T(8,128)S(1)} fusion(bf16[1024,5376]{1,0:T(8,128)(2,1)} %param.16, bf16[1,512,5376]{2,1,0:T(8,128)(2,1)} %all-gather.7.cloned.1.call-done), kind=kOutput, calls=%fused_computation.23 | convolution fusion | flops 5637144576 | bytes 18612224 | tf_op jit(solution)/shard_map/td,hd->th/dot_general | solution.py:188
  227.6 7.2 fusion.26
  249.0 3.4 maximum_maximum_fusion
  252.4 16.3 %fusion.97 = (f32[4,2,512]{2,1,0:T(2,128)S(1)}, f32[4,2,512,1536]{2,3,1,0:T(8,128)}) fusion(pred[512,1536]{0,1:T(8,128)(4,1)} %fusion.40, bf16[2,1536,4,128]{3,1,2,0:T(8,128)(2,1)} %maximum_maximum_fusion, bf16[512,4,2,64]{3,0,2,1:T(8,128)(2,1)} %bitcast.187, bf16[512,4,2,64]{3,0,2,1:T(8,128)(2,1)} %bitcast.185), kind=kOutput, calls=%fused_computation.145 | convolution fusion | flops 1637877248 | bytes 29638656 | tf_op jit(solution)/shard_map/sub | solution.py:70
  268.7 10.3 %fusion.8 = bf16[4,2,512,1536]{2,3,1,0:T(8,128)(2,1)S(1)} fusion(f32[4,2,512,1536]{2,3,1,0:T(8,128)} %get-tuple-element.26, f32[4,2,512]{2,1,0:T(2,128)S(1)} %get-tuple-element.25), kind=kLoop, calls=%fused_computation.13 | loop fusion | flops 12582912 | bytes 37765120 | tf_op jit(solution)/shard_map/convert_element_type | solution.py:72
  279.1 3.1 multiply_reduce_fusion
  282.2 5.1 convolution_bitcast_fusion.1
  287.3 14.9 %fusion.3 = bf16[4,2,512,1536]{2,3,1,0:T(8,128)(2,1)} fusion(bf16[512,4,2,128]{0,3,2,1:T(8,128)(2,1)S(1)} %copy-done.16, f32[4,2,512]{2,1,0:T(2,128)S(1)} %get-tuple-element.27, f32[4,2,512,1536]{2,3,1,0:T(8,128)} %get-tuple-element.26, f32[4,2,512]{2,1,0:T(2,128)S(1)} %get-tuple-element.25, bf16[2,1536,4,128]{3,1,2,0:T(8,128)(2,1)} %maximum_maximum_fusion), kind=kOutput, calls=%fused_computation.4 | convolution fusion | flops 1642070016 | bytes 40402944 | tf_op jit(solution)/shard_map/chgd,khd->hgck/dot_general | solution.py:76
  302.3 7.1 fusion.48
  311.4 5.3 convolution_bitcast_fusion
  321.8 3.2 copy.80
  329.1 15.8 %psum.46 = bf16[512,16]{1,0:T(8,128)(2,1)S(1)} all-reduce(bf16[512,16]{1,0:T(8,128)(2,1)S(1)} %convolution_convert_fusion.1), channel_id=1, replica_groups=mesh['dp'=2,'context'=4,'tensor'=4] {'tensor'}, use_global_device_ids=true, to_apply=%region_7.8 | all-reduce | flops 8192 | bytes 32768 | tf_op jit(solution)/shard_map/psum | solution.py:271
  344.9 4.1 fusion.9
  349.0 3.4 fusion.10
  353.6 5.6 collective-permute-start.2
  360.8 13.0 %fusion.68 = f32[512,5376]{1,0:T(8,128)} fusion(bf16[5376,1024]{1,0:T(8,128)(2,1)} %param.14, bf16[64,8,8,128]{3,2,1,0:T(8,128)(2,1)S(1)} %bitcast.191), kind=kOutput, calls=%fused_computation.95 | convolution fusion | flops 5637144576 | bytes 23068672 | tf_op jit(solution)/shard_map/th,dh->td/dot_general | solution.py:286
  373.8 9.1 %collective-permute-done.2 = bf16[2,512,4,128]{3,1,2,0:T(8,128)(2,1)S(1)} collective-permute-done((bf16[2,512,4,128]{3,1,2,0:T(8,128)(2,1)}, bf16[2,512,4,128]{3,1,2,0:T(8,128)(2,1)S(1)}, u32[]{:S(2)}, u32[]{:S(2)}) %collective-permute-start.2) | collective-permute-done | bytes 1048608 | tf_op jit(solution)/shard_map/ppermute | solution.py:18
  382.9 4.8 collective-permute-done.3
  399.7 10.0 %fusion.20 = f32[512,5376]{1,0:T(8,128)} fusion(bf16[512,512]{0,1:T(8,128)(2,1)} %bitcast.183, bf16[2,5376,512]{2,1,0:T(8,128)(2,1)} %param.15), kind=kOutput, calls=%fused_computation.29 | convolution fusion | flops 2818572288 | bytes 17039360 | tf_op jit(solution)/shard_map/th,dh->td/dot_general | solution.py:287
  409.7 5.7 fusion.16
  416.1 4.6 fusion.24
  420.8 13.9 %add_convert_fusion = bf16[512,5376]{1,0:T(8,128)(2,1)} fusion(f32[512,5376]{1,0:T(8,128)} %fusion.16, f32[512,5376]{1,0:T(8,128)} %fusion.68, f32[512,5376]{1,0:T(8,128)} %fusion.20, bf16[48,5376]{1,0:T(8,128)(2,1)S(1)} %bitcast.172, bf16[512,16]{0,1:T(8,128)(2,1)S(1)} %fusion.63, bf16[512,16]{0,1:T(8,128)(2,1)S(1)} %fusion.62, bf16[512,16]{0,1:T(8,128)(2,1)S(1)} %fusion.59), kind=kOutput, calls=%fused_computation.12 | convolution fusion | flops 275398656 | bytes 39100416 | tf_op jit(solution)/shard_map/dot_general | solution.py:294
  436.5 41.8 %all-reduce.10.cloned.1.call-done = (bf16[16,1024]{1,0:T(8,128)(2,1)}, bf16[2,16,512]{2,1,0:T(8,128)(2,1)}, bf16[16,1024]{1,0:T(8,128)(2,1)}) async-done(((bf16[16,1024]{1,0:T(8,128)(2,1)}, bf16[2,16,512]{2,1,0:T(8,128)(2,1)}, bf16[16,1024]{1,0:T(8,128)(2,1)}), (bf16[16,1024]{1,0:T(8,128)(2,1)}, bf16[2,16,512]{2,1,0:T(8,128)(2,1)}, bf16[16,1024]{1,0:T(8,128)(2,1)})) %all-reduce.10.cloned.1.call-update) | async-done | bytes 98320 | tf_op jit(solution)/shard_map/psum | solution.py:277
  482.5 130.0 %all-reduce.6.cloned.1.call-done = f32[3,16,5376]{2,1,0:T(8,128)} async-done(((f32[3,16,5376]{2,1,0:T(8,128)}), f32[3,16,5376]{2,1,0:T(8,128)}) %all-reduce.6.cloned.1.call-update) | async-done | bytes 1032208 | tf_op jit(solution)/shard_map/psum | solution.py:275
  612.5 101.7 %reduce-scatter.2.cloned.1.call-done = bf16[128,5376]{1,0:T(8,128)(2,1)} async-done(((bf16[512,5376]{1,0:T(8,128)(2,1)}), bf16[128,5376]{1,0:T(8,128)(2,1)}) %reduce-scatter.2.cloned.1.call-update) | async-done | bytes 1376272 | tf_op jit(solution)/shard_map/reduce_scatter | solution.py:293
  (136 shorter events, 66.4 us)
Async XLA Ops:
  7.2 103.3 %copy-start = (bf16[3,16,5376]{2,1,0:T(8,128)(2,1)S(1)}, bf16[3,16,5376]{2,1,0:T(8,128)(2,1)}, u32[]{:S(2)}) copy-start(bf16[3,16,5376]{2,1,0:T(8,128)(2,1)} %param.17) | copy-start | bytes 1548292
  7.2 103.3 %all-gather.5.cloned.1.call-start = ((), (), s32[]{:S(2)}) async-start(), calls=%async_computation.4 | async-start | bytes 6881280 | tf_op jit(solution)/shard_map/all_gather | solution.py:123
  7.9 204.9 %all-gather.7.cloned.1.call-start = ((), (), s32[]{:S(2)}) async-start(), calls=%async_computation.5 | async-start | bytes 6881280 | tf_op jit(solution)/shard_map/all_gather | solution.py:124
  8.7 426.1 %all-reduce.8.cloned.1.call-start = ((), (), s32[]{:S(2)}) async-start(), calls=%async_computation.3 | async-start | bytes 344064 | tf_op jit(solution)/shard_map/psum | solution.py:282
  11.2 313.8 %copy-start.8 = (f32[512,64]{1,0:T(8,128)}, f32[512,64]{1,0:T(8,128)S(1)}, u32[]{:S(2)}) copy-start(f32[512,64]{1,0:T(8,128)S(1)} %get-tuple-element.24) | copy-start | bytes 393220
  120.6 13.2 %copy-start.13 = (bf16[1,512,4,128]{3,1,2,0:T(8,128)(2,1)}, bf16[1,512,4,128]{3,1,2,0:T(8,128)(2,1)S(1)}, u32[]{:S(2)}) copy-start(bf16[1,512,4,128]{3,1,2,0:T(8,128)(2,1)S(1)} %copy.37) | copy-start | bytes 1572868
  128.7 84.1 %copy-start.20 = (bf16[16,5376]{1,0:T(8,128)(2,1)S(1)}, bf16[16,5376]{1,0:T(8,128)(2,1)}, u32[]{:S(2)}) copy-start(bf16[16,5376]{1,0:T(8,128)(2,1)} %param.21) | copy-start | bytes 516100
  136.0 113.0 %collective-permute-start.1 = (bf16[2,512,4,128]{3,1,2,0:T(8,128)(2,1)}, bf16[2,512,4,128]{3,1,2,0:T(8,128)(2,1)}, u32[]{:S(2)}, u32[]{:S(2)}) collective-permute-start(bf16[2,512,4,128]{3,1,2,0:T(8,128)(2,1)} %pad_maximum_fusion.1), channel_id=1, source_target_pairs={{0,4},{4,8},{8,12},{1,5},{5,9},{9,13},{2,6},{6,10},{10,14},{3,7},{... | collective-permute-start | bytes 3145736 | tf_op jit(solution)/shard_map/ppermute | solution.py:18
  139.7 109.3 %collective-permute-start = (bf16[2,512,4,128]{3,1,2,0:T(8,128)(2,1)}, bf16[2,512,4,128]{3,1,2,0:T(8,128)(2,1)}, u32[]{:S(2)}, u32[]{:S(2)}) collective-permute-start(bf16[2,512,4,128]{3,1,2,0:T(8,128)(2,1)} %pad_maximum_fusion.1), channel_id=1, source_target_pairs={{0,8},{4,12},{1,9},{5,13},{2,10},{6,14},{3,11},{7,15},{16,24},{20,... | collective-permute-start | bytes 3145736 | tf_op jit(solution)/shard_map/ppermute | solution.py:18
  212.8 14.7 %slice-start = ((s8[5505024]{0:T(1024)(128)(4,1)}), s8[4194304]{0:T(1024)(128)(4,1)S(1)}, s32[]{:S(2)}) async-start(s8[5505024]{0:T(1024)(128)(4,1)} %bitcast.173), calls=%async_computation.7 | async-start | bytes 8388608
  212.8 14.7 %slice-start.5 = ((s8[11010048]{0:T(1024)(128)(4,1)}), s8[4194304]{0:T(1024)(128)(4,1)S(1)}, s32[]{:S(2)}) async-start(s8[11010048]{0:T(1024)(128)(4,1)} %bitcast.199), calls=%async_computation.12 | async-start | bytes 8388608
  217.0 10.5 %slice-start.1 = ((s8[5505024]{0:T(1024)(128)(4,1)}), s8[1310720]{0:T(1024)(128)(4,1)S(1)}, s32[]{:S(2)}) async-start(s8[5505024]{0:T(1024)(128)(4,1)} %bitcast.173), calls=%async_computation.8 | async-start | bytes 2621440
  217.0 10.5 %slice-start.6 = ((s8[11010048]{0:T(1024)(128)(4,1)}), s8[4194304]{0:T(1024)(128)(4,1)S(1)}, s32[]{:S(2)}) async-start(s8[11010048]{0:T(1024)(128)(4,1)} %bitcast.199), calls=%async_computation.13 | async-start | bytes 8388608
  217.0 10.5 %slice-start.7 = ((s8[11010048]{0:T(1024)(128)(4,1)}), s8[2621440]{0:T(1024)(128)(4,1)S(1)}, s32[]{:S(2)}) async-start(s8[11010048]{0:T(1024)(128)(4,1)} %bitcast.199), calls=%async_computation.14 | async-start | bytes 5242880
  227.5 7.2 copy-start.22
  235.2 8.1 %copy-start.23 = (bf16[16,1024]{1,0:T(8,128)(2,1)S(1)}, bf16[16,1024]{1,0:T(8,128)(2,1)}, u32[]{:S(2)}) copy-start(bf16[16,1024]{1,0:T(8,128)(2,1)} %param.18) | copy-start | bytes 98308
  268.7 10.4 %copy-start.5 = (bf16[2,1536,4,128]{3,1,2,0:T(8,128)(2,1)S(1)}, bf16[2,1536,4,128]{3,1,2,0:T(8,128)(2,1)}, u32[]{:S(2)}) copy-start(bf16[2,1536,4,128]{3,1,2,0:T(8,128)(2,1)} %maximum_maximum_fusion) | copy-start | bytes 9437188
  302.2 8.6 %copy-start.1 = (bf16[4,2,512,1536]{2,3,1,0:T(8,128)(2,1)S(1)}, bf16[4,2,512,1536]{2,3,1,0:T(8,128)(2,1)}, u32[]{:S(2)}) copy-start(bf16[4,2,512,1536]{2,3,1,0:T(8,128)(2,1)} %fusion.3) | copy-start | bytes 37748740
  302.3 8.8 %copy-start.17 = (bf16[512,8,64]{2,0,1:T(8,128)(2,1)S(1)}, bf16[512,8,64]{2,0,1:T(8,128)(2,1)}, u32[]{:S(2)}) copy-start(bf16[512,8,64]{2,0,1:T(8,128)(2,1)} %copy.38) | copy-start | bytes 1572868
  302.3 9.1 %copy-start.18 = (bf16[512,8,64]{2,0,1:T(8,128)(2,1)S(1)}, bf16[512,8,64]{2,0,1:T(8,128)(2,1)}, u32[]{:S(2)}) copy-start(bf16[512,8,64]{2,0,1:T(8,128)(2,1)} %copy.39) | copy-start | bytes 1572868
  311.4 5.3 copy-start.19
  349.0 129.3 %all-reduce.10.cloned.1.call-start = ((), (), s32[]{:S(2)}) async-start(), calls=%async_computation.6 | async-start | bytes 196608 | tf_op jit(solution)/shard_map/psum | solution.py:277
  353.6 29.3 %collective-permute-start.2 = (bf16[2,512,4,128]{3,1,2,0:T(8,128)(2,1)}, bf16[2,512,4,128]{3,1,2,0:T(8,128)(2,1)S(1)}, u32[]{:S(2)}, u32[]{:S(2)}) collective-permute-start(bf16[2,512,4,128]{3,1,2,0:T(8,128)(2,1)} %get-tuple-element.11), channel_id=1, source_target_pairs={{4,0},{8,4},{12,8},{5,1},{9,5},{13,9},{6,2},{10,6},{14,10},{7,3},{... | collective-permute-start | bytes 3145736 | tf_op jit(solution)/shard_map/ppermute | solution.py:18
  359.2 28.5 %copy-start.2 = (f32[1,1536,4,128]{3,1,2,0:T(8,128)S(1)}, f32[1,1536,4,128]{3,1,2,0:T(8,128)}, u32[]{:S(2)}) copy-start(f32[1,1536,4,128]{3,1,2,0:T(8,128)} %convolution_bitcast_fusion.1) | copy-start | bytes 9437188
  359.2 28.5 %copy-start.3 = (f32[1,1536,4,128]{3,1,2,0:T(8,128)S(1)}, f32[1,1536,4,128]{3,1,2,0:T(8,128)}, u32[]{:S(2)}) copy-start(f32[1,1536,4,128]{3,1,2,0:T(8,128)} %convolution_bitcast_fusion) | copy-start | bytes 9437188
  359.2 28.5 %collective-permute-start.3 = (bf16[2,512,4,128]{3,1,2,0:T(8,128)(2,1)S(1)}, bf16[2,512,4,128]{3,1,2,0:T(8,128)(2,1)}, u32[]{:S(2)}, u32[]{:S(2)}) collective-permute-start(bf16[2,512,4,128]{3,1,2,0:T(8,128)(2,1)S(1)} %get-tuple-element.12), channel_id=1, source_target_pairs={{8,0},{12,4},{9,1},{13,5},{10,2},{14,6},{11,3},{15,7},{24,16},{28,... | collective-permute-start | bytes 3145736 | tf_op jit(solution)/shard_map/ppermute | solution.py:18
  391.8 17.9 %slice-start.2 = ((s8[11010048]{0:T(1024)(128)(4,1)}), s8[2621440]{0:T(1024)(128)(4,1)S(1)}, s32[]{:S(2)}) async-start(s8[11010048]{0:T(1024)(128)(4,1)} %bitcast.176), calls=%async_computation.9 | async-start | bytes 5242880
  399.6 10.1 %slice-start.3 = ((s8[11010048]{0:T(1024)(128)(4,1)}), s8[4194304]{0:T(1024)(128)(4,1)S(1)}, s32[]{:S(2)}) async-start(s8[11010048]{0:T(1024)(128)(4,1)} %bitcast.176), calls=%async_computation.10 | async-start | bytes 8388608
  399.6 10.1 %slice-start.4 = ((s8[11010048]{0:T(1024)(128)(4,1)}), s8[4194304]{0:T(1024)(128)(4,1)S(1)}, s32[]{:S(2)}) async-start(s8[11010048]{0:T(1024)(128)(4,1)} %bitcast.176), calls=%async_computation.11 | async-start | bytes 8388608
  399.6 10.1 %copy-start.7 = (bf16[1,512,4,128]{1,3,2,0:T(8,128)(2,1)S(1)}, bf16[1,512,4,128]{1,3,2,0:T(8,128)(2,1)}, u32[]{:S(2)}) copy-start(bf16[1,512,4,128]{1,3,2,0:T(8,128)(2,1)} %copy-done.6) | copy-start | bytes 1572868
  416.1 196.4 %all-reduce.6.cloned.1.call-start = ((), (), s32[]{:S(2)}) async-start(), calls=%async_computation.2 | async-start | bytes 2064384 | tf_op jit(solution)/shard_map/psum | solution.py:275
  420.8 293.5 %reduce-scatter.2.cloned.1.call-start = ((), (), s32[]{:S(2)}) async-start(), calls=%async_computation.1 | async-start | bytes 6881280 | tf_op jit(solution)/shard_map/reduce_scatter | solution.py:293
  (10 other events, 31.1 us)
Sparse Core Ops, SparseCore 0:
  9.6 100.8 all-gather.4
  112.0 100.7 all-gather.6
  349.1 56.8 all-reduce.7
  416.2 62.0 all-reduce.9
  484.7 127.7 all-reduce.5
  615.2 98.9 reduce-scatter.1
where the time goes:
time: 732 us; the launch traced here: 724 us
  waiting for transfers between devices  456 us (62%)
  matrix products  151 us (21%)
  other arithmetic  41.6 us (6%)
  local copies, waits for them, and re-layouts  30.4 us (4%)
  blocking collectives  15.8 us (2%)
  between operations  15.2 us (2%)
  starting transfers between devices  13.8 us (2%)
    psum x1, waiting for transfers between devices, local(): grad_down_qkv = lax.psum(grad_down_part, ('dp', 'context', 'tensor'))  130 us
    reduce_scatter x1, waiting for transfers between devices, local(): lax.psum_scatter((term + jnp.dot(hidden_all, down_factors_all, preferred_...  102 us
    all_gather x1, waiting for transfers between devices, local(): lax.all_gather(tokens[0], 'tensor', axis=0, tiled=True)  96.6 us
    all_gather x1, waiting for transfers between devices, local(): lax.all_gather(output_gradient[0], 'tensor', axis=0, tiled=True)  70.4 us
    psum x1, waiting for transfers between devices, local(): lax.psum(query_up_gradient_piece.astype(jnp.bfloat16), ('dp', 'context'))  41.8 us
    unnamed x71, local copies, waits for them, and re-layouts  16.9 us
    sub x1, matrix products, band_block(): exponent = jnp.exp(scores - row_max)  16.3 us
    psum x1, blocking collectives, local(): factor_value = lax.psum(factor_part.astype(jnp.bfloat16), 'tensor')  15.8 us
  transfers between devices with their start and end apart: 10, of which 7 were waited for; matrix products, arithmetic and copies ran while one was open for 19% of the time, Pallas kernels for 0%

commit v1 on v0

v1 whole, which is shorter than its diff:
```python
import functools

import jax
import jax.numpy as jnp
from jax import lax
from jax.experimental import pallas as pl
from jax.experimental.pallas import tpu as pltpu
from jax.sharding import PartitionSpec as P

HEAD_SIZE = 128
WINDOW = 1024


adapter_scale = 2.0
attn_scale = 168.0 ** (-0.5)
rope_base = 10000.0


def passed_along(block, axis, distance):
    devices = range(lax.axis_size(axis))
    route = [(i - distance, i) for i in devices if i - distance in devices]
    return lax.ppermute(block, axis, route)


def rope_tables(positions, head_width):
    half_width = head_width // 2
    inverse = rope_base ** (-(jnp.arange(half_width, dtype=jnp.float32) * 2.0 / head_width))
    angle = positions[:, None] * inverse[None, :]
    return (jnp.cos(angle), jnp.sin(angle))


NT = (((1,), (1,)), ((), ()))
TN = (((0,), (0,)), ((), ()))
f32 = jnp.float32
bf16 = jnp.bfloat16


def dot(a, b, dims):
    return lax.dot_general(a, b, dims, preferred_element_type=f32)


def turned(x, cosine, sine):
    return x * cosine + pltpu.roll(x, x.shape[-1] // 2, 1) * sine


def rope_query_kernel(x_ref, cos_ref, sin_ref, out_ref):
    out_ref[...] = turned(x_ref[...], cos_ref[...], sin_ref[...]).astype(bf16)


def rope_pair_kernel(k_ref, v_ref, cos_ref, sin_ref, out_ref):
    out_ref[0] = turned(k_ref[...], cos_ref[...], sin_ref[...]).astype(bf16)
    out_ref[1] = v_ref[...].astype(bf16)


def rope_query(x, cosine, sine):
    rows, cols = x.shape
    table = pl.BlockSpec((rows, HEAD_SIZE), lambda h: (0, 0))
    return pl.pallas_call(
        rope_query_kernel,
        grid=(cols // HEAD_SIZE,),
        in_specs=[pl.BlockSpec((rows, HEAD_SIZE), lambda h: (0, h)), table, table],
        out_specs=pl.BlockSpec((rows, HEAD_SIZE), lambda h: (0, h)),
        out_shape=jax.ShapeDtypeStruct((rows, cols), bf16),
        name="rope_query",
        cost_estimate=pl.CostEstimate(flops=4 * rows * cols, bytes_accessed=6 * rows * cols, transcendentals=0),
    )(x, cosine, sine)


def rope_pair(k, v, cosine, sine):
    rows, cols = k.shape
    table = pl.BlockSpec((rows, HEAD_SIZE), lambda h: (0, 0))
    block = pl.BlockSpec((rows, HEAD_SIZE), lambda h: (0, h))
    return pl.pallas_call(
        rope_pair_kernel,
        grid=(cols // HEAD_SIZE,),
        in_specs=[block, block, table, table],
        out_specs=pl.BlockSpec((2, rows, HEAD_SIZE), lambda h: (0, 0, h)),
        out_shape=jax.ShapeDtypeStruct((2, rows, cols), bf16),
        name="rope_pair",
        cost_estimate=pl.CostEstimate(flops=4 * rows * cols, bytes_accessed=12 * rows * cols, transcendentals=0),
    )(k, v, cosine, sine)


def band(block, rows, halo_rows, keys):
    first = max(0, (halo_rows + block * rows - WINDOW + 1) // 128 * 128)
    return first, min(keys, halo_rows + (block + 1) * rows)


def fill(refs, k_buf, v_buf):
    at = 0
    for ref in refs:
        n = ref.shape[1]
        k_buf[at : at + n] = ref[0]
        v_buf[at : at + n] = ref[1]
        at += n


def forward_kernel(halo_rows, group, rows, *refs):
    q_ref, qseg_ref, kseg_ref = refs[:3]
    pair_refs = refs[3:-5]
    w_ref, att_ref, k_buf, v_buf, bias = refs[-5:]
    keys, count = bias.shape
    fill(pair_refs, k_buf, v_buf)

    @pl.when(pl.program_id(0) == 0)
    def _():
        for b in range(count // rows):
            lo, hi = band(b, rows, halo_rows, keys)
            shape = (hi - lo, rows)
            offset = (
                lax.broadcasted_iota(jnp.int32, shape, 1)
                - lax.broadcasted_iota(jnp.int32, shape, 0)
                + (halo_rows + b * rows - lo)
            )
            same = kseg_ref[lo:hi, :] == qseg_ref[:, b * rows : (b + 1) * rows]
            allowed = same & (offset >= 0) & (offset < WINDOW)
            bias[lo:hi, b * rows : (b + 1) * rows] = jnp.where(allowed, 0.0, -1e30)

    for g in range(group):
        for b in range(count // rows):
            lo, hi = band(b, rows, halo_rows, keys)
            here = slice(b * rows, (b + 1) * rows)
            cols = slice(g * HEAD_SIZE, (g + 1) * HEAD_SIZE)
            s = dot(k_buf[lo:hi], q_ref[here, cols], NT) * attn_scale + bias[lo:hi, here]
            p = jnp.exp(s - jnp.max(s, axis=0, keepdims=True))
            w = (p * (1.0 / jnp.sum(p, axis=0, keepdims=True))).astype(bf16)
            w_ref[g, lo:hi, here] = w
            att_ref[here, cols] = dot(v_buf[lo:hi], w, TN).T.astype(bf16)


def attention_forward(queries, pairs, query_seg, key_seg):
    count, q_cols = queries.shape
    kv_cols = pairs[0].shape[2]
    group = q_cols // kv_cols
    keys = count * len(pairs)
    rows = min(256, count)
    halo_rows = keys - count
    q_spec = pl.BlockSpec((count, group * HEAD_SIZE), lambda h: (0, h))
    pair_spec = pl.BlockSpec((2, count, HEAD_SIZE), lambda h: (0, 0, h))
    return pl.pallas_call(
        functools.partial(forward_kernel, halo_rows, group, rows),
        grid=(kv_cols // HEAD_SIZE,),
        in_specs=[
            q_spec,
            pl.BlockSpec((1, count), lambda h: (0, 0)),
            pl.BlockSpec((keys, 1), lambda h: (0, 0)),
        ]
        + [pair_spec] * len(pairs),
        out_specs=[pl.BlockSpec((group, keys, count), lambda h: (h, 0, 0)), q_spec],
        out_shape=[
            jax.ShapeDtypeStruct((q_cols // HEAD_SIZE, keys, count), bf16),
            jax.ShapeDtypeStruct((count, q_cols), bf16),
        ],
        scratch_shapes=[
            pltpu.VMEM((keys, HEAD_SIZE), bf16),
            pltpu.VMEM((keys, HEAD_SIZE), bf16),
            pltpu.VMEM((keys, count), f32),
        ],
        compiler_params=pltpu.CompilerParams(vmem_limit_bytes=48 << 20),
        name="attention_forward",
        cost_estimate=pl.CostEstimate(
            flops=4 * q_cols * count * keys, bytes_accessed=40 << 20, transcendentals=8 * count * keys
        ),
    )(queries, query_seg, key_seg, *pairs)


def backward_kernel(halo_rows, group, rows, n_pairs, *refs):
    q_ref, g_ref, att_ref, w_ref, cos_ref, sin_ref = refs[:6]
    pair_refs = refs[6 : 6 + n_pairs]
    dq_ref, halo_ref, own_ref, k_buf, v_buf, dk_buf, dv_buf = refs[6 + n_pairs :]
    keys = k_buf.shape[0]
    count = q_ref.shape[0]
    half = HEAD_SIZE // 2
    fill(pair_refs, k_buf, v_buf)
    dk_buf[...] = jnp.zeros_like(dk_buf)
    dv_buf[...] = jnp.zeros_like(dv_buf)
    for b in range(count // rows):
        lo, hi = band(b, rows, halo_rows, keys)
        here = slice(b * rows, (b + 1) * rows)
        for h in range(group):
            cols = slice(h * HEAD_SIZE, (h + 1) * HEAD_SIZE)
            g = g_ref[here, cols]
            w = w_ref[h, lo:hi, here]
            row_dot = jnp.sum((g.astype(f32) * att_ref[here, cols].astype(f32)).T, axis=0, keepdims=True)
            gw = dot(v_buf[lo:hi], g, NT)
            ds = (w.astype(f32) * ((gw - row_dot) * attn_scale)).astype(bf16)
            dv_buf[lo:hi] += dot(w, g, (((1,), (0,)), ((), ())))
            dk_buf[lo:hi] += dot(ds, q_ref[here, cols], (((1,), (0,)), ((), ())))
            dq = dot(k_buf[lo:hi], ds, TN).T
            dq_ref[here, cols] = turned(dq, cos_ref[here], -sin_ref[here]).astype(bf16)
    if halo_rows:
        halo_ref[0] = dk_buf[:halo_rows].astype(bf16)
        halo_ref[1] = dv_buf[:halo_rows].astype(bf16)
    own_ref[0] = dk_buf[halo_rows:]
    own_ref[1] = dv_buf[halo_rows:]


def attention_backward(queries, grads, attended, weights, pairs, cosine, sine):
    count, q_cols = queries.shape
    kv_cols = pairs[0].shape[2]
    group = q_cols // kv_cols
    keys = count * len(pairs)
    rows = min(256, count)
    halo_rows = keys - count
    q_spec = pl.BlockSpec((count, group * HEAD_SIZE), lambda h: (0, h))
    pair_spec = pl.BlockSpec((2, count, HEAD_SIZE), lambda h: (0, 0, h))
    table = pl.BlockSpec((count, HEAD_SIZE), lambda h: (0, 0))
    return pl.pallas_call(
        functools.partial(backward_kernel, halo_rows, group, rows, len(pairs)),
        grid=(kv_cols // HEAD_SIZE,),
        in_specs=[
            q_spec,
            q_spec,
            q_spec,
            pl.BlockSpec((group, keys, count), lambda h: (h, 0, 0)),
            table,
            table,
        ]
        + [pair_spec] * len(pairs),
        out_specs=[
            q_spec,
            pl.BlockSpec((2, halo_rows, HEAD_SIZE), lambda h: (0, 0, h)),
            pair_spec,
        ],
        out_shape=[
            jax.ShapeDtypeStruct((count, q_cols), bf16),
            jax.ShapeDtypeStruct((2, halo_rows, kv_cols), bf16),
            jax.ShapeDtypeStruct((2, count, kv_cols), f32),
        ],
        scratch_shapes=[
            pltpu.VMEM((keys, HEAD_SIZE), bf16),
            pltpu.VMEM((keys, HEAD_SIZE), bf16),
            pltpu.VMEM((keys, HEAD_SIZE), f32),
            pltpu.VMEM((keys, HEAD_SIZE), f32),
        ],
        compiler_params=pltpu.CompilerParams(vmem_limit_bytes=48 << 20),
        name="attention_backward",
        cost_estimate=pl.CostEstimate(
            flops=8 * q_cols * count * keys, bytes_accessed=20 << 20, transcendentals=0
        ),
    )(queries, grads, attended, weights, cosine, sine, *pairs)


def combine_kernel(own_ref, cos_ref, sin_ref, *refs):
    dk_ref, dv_ref = refs[-2:]
    dk, dv = own_ref[0], own_ref[1]
    for ref in refs[:-2]:
        dk = dk + ref[0].astype(f32)
        dv = dv + ref[1].astype(f32)
    dk_ref[...] = turned(dk, cos_ref[...], -sin_ref[...]).astype(bf16)
    dv_ref[...] = dv.astype(bf16)


def combine(own, shares, cosine, sine):
    _, count, kv_cols = own.shape
    pair_spec = pl.BlockSpec((2, count, HEAD_SIZE), lambda h: (0, 0, h))
    table = pl.BlockSpec((count, HEAD_SIZE), lambda h: (0, 0))
    out = pl.BlockSpec((count, HEAD_SIZE), lambda h: (0, h))
    return pl.pallas_call(
        combine_kernel,
        grid=(kv_cols // HEAD_SIZE,),
        in_specs=[pair_spec, table, table] + [pair_spec] * len(shares),
        out_specs=[out, out],
        out_shape=[jax.ShapeDtypeStruct((count, kv_cols), bf16)] * 2,
        name="combine_pairs",
        cost_estimate=pl.CostEstimate(flops=8 * count * kv_cols, bytes_accessed=20 * count * kv_cols, transcendentals=0),
    )(own, cosine, sine, *shares)


def term_kernel(first_ref, dk_ref, dv_ref, hid_ref, kv_ref, down_ref, out_ref):
    total = first_ref[...] + dot(dk_ref[...], kv_ref[0], NT)
    total = total + dot(dv_ref[...], kv_ref[1], NT)
    total = total + dot(hid_ref[...], down_ref[...], (((1,), (0,)), ((), ())))
    out_ref[...] = total.astype(bf16)


def term_sum(first, dk, dv, hidden, kv_weight, down):
    count, width = first.shape
    tile = next(t for t in (768, 384, 256, 128, width) if width % t == 0)
    whole = lambda a: pl.BlockSpec(a.shape, lambda i: (0, 0))
    block = pl.BlockSpec((count, tile), lambda i: (0, i))
    return pl.pallas_call(
        term_kernel,
        grid=(width // tile,),
        in_specs=[
            block,
            whole(dk),
            whole(dv),
            whole(hidden),
            pl.BlockSpec((2, tile, kv_weight.shape[2]), lambda i: (0, i, 0)),
            pl.BlockSpec((down.shape[0], tile), lambda i: (0, i)),
        ],
        out_specs=block,
        out_shape=jax.ShapeDtypeStruct((count, width), bf16),
        compiler_params=pltpu.CompilerParams(vmem_limit_bytes=48 << 20),
        name="input_term",
        cost_estimate=pl.CostEstimate(
            flops=4 * count * width * dk.shape[1], bytes_accessed=28 << 20, transcendentals=0
        ),
    )(first, dk, dv, hidden, kv_weight, down)


def shifted(block, axis, distance):
    n = lax.axis_size(axis)
    return lax.ppermute(block, axis, [(i, (i + distance) % n) for i in range(n)])


def summed_pairwise(block, axis):
    n = lax.axis_size(axis)
    if n & (n - 1):
        return lax.psum(block, axis)
    step = 1
    while step < n:
        other = lax.ppermute(block, axis, [(i, i ^ step) for i in range(n)])
        block = (block.astype(f32) + other.astype(f32)).astype(bf16)
        step *= 2
    return block


def scattered_rows(block, axis):
    n, me = lax.axis_size(axis), lax.axis_index(axis)
    blocks = block.reshape(n, block.shape[0] // n, block.shape[1])
    total = lax.dynamic_index_in_dim(blocks, me, 0, keepdims=False).astype(f32)
    for d in range(1, n):
        part = lax.dynamic_index_in_dim(blocks, (me + d) % n, 0, keepdims=False)
        total = total + shifted(part, axis, d).astype(f32)
    return total


def gathered_rows(block, axis):
    n, me = lax.axis_size(axis), lax.axis_index(axis)
    parts = jnp.stack([block] + [shifted(block, axis, d) for d in range(1, n)], 0)
    order = (me - jnp.arange(n)) % n
    return jnp.take(parts, order, axis=0).reshape(n * block.shape[0], block.shape[1])


def local(
    tokens,
    output_gradient,
    document_index,
    query_weight,
    key_value_weight,
    output_weight,
    adapter_down_projections,
    adapter_up_query,
    adapter_up_key_value,
    adapter_down_output,
    adapter_up_output,
):
    tensor_size = lax.axis_size("tensor")
    context_at = lax.axis_index("context")
    local_count = tokens.shape[1]
    width = tokens.shape[2]
    shard_len = local_count * tensor_size
    halo_count = (WINDOW - 1) // shard_len + 1
    rank = adapter_down_projections.shape[1]
    gathered = lax.all_gather(tokens[0], "tensor", axis=0, tiled=True)
    incoming = lax.all_gather(output_gradient[0], "tensor", axis=0, tiled=True)
    positions = (context_at * shard_len + jnp.arange(shard_len, dtype=jnp.int32)).astype(f32)
    cosine, sine = rope_tables(positions, HEAD_SIZE)
    cosine = jnp.concatenate([cosine, cosine], 1)
    sine = jnp.concatenate([-sine, sine], 1)
    segment_row = document_index[0]
    segment_pad = jnp.concatenate(
        [jnp.full((halo_count * shard_len,), -1, jnp.int32), segment_row], 0
    )
    key_seg = lax.dynamic_slice_in_dim(
        segment_pad, context_at * shard_len, (halo_count + 1) * shard_len, 0
    )
    query_seg = lax.dynamic_slice_in_dim(segment_row, context_at * shard_len, shard_len, 0)

    down_all = adapter_down_projections.reshape(3 * rank, width)
    adapted = jnp.einsum("ja,ma->jm", gathered, down_all, preferred_element_type=f32).astype(bf16)
    adapted_query = adapted[:, :rank]
    adapted_key = adapted[:, rank : 2 * rank]
    adapted_value = adapted[:, 2 * rank :]

    def projected(weight, low, up):
        return jnp.dot(gathered, weight, preferred_element_type=f32) + adapter_scale * jnp.dot(
            low, up, preferred_element_type=f32
        )

    key_linear = projected(key_value_weight[0], adapted_key, adapter_up_key_value[0])
    value_linear = projected(key_value_weight[1], adapted_value, adapter_up_key_value[1])
    pair_local = rope_pair(key_linear, value_linear, cosine, sine)
    earlier = [
        passed_along(pair_local, "context", distance) for distance in range(halo_count, 0, -1)
    ]
    queries = rope_query(
        projected(query_weight, adapted_query, adapter_up_query), cosine, sine
    )
    pairs = earlier + [pair_local]
    weights, attended = attention_forward(queries, pairs, query_seg[None, :], key_seg[:, None])
    factor = jnp.einsum(
        "kn,pn->kp", attended, adapter_down_output, preferred_element_type=f32
    ).astype(bf16)

    incoming, weights, attended, factor = lax.optimization_barrier(
        (incoming, weights, attended, factor)
    )
    up_gradient = (
        adapter_scale
        * jnp.einsum("ja,ma->jm", incoming, adapter_up_output, preferred_element_type=f32)
    ).astype(bf16)
    grad_attended = (
        jnp.einsum("td,hd->th", incoming, output_weight, preferred_element_type=f32)
        + jnp.dot(up_gradient, adapter_down_output, preferred_element_type=f32)
    ).astype(bf16)
    grad_query, grad_halo, grad_own = attention_backward(
        queries, grad_attended, attended, weights, pairs, cosine, sine
    )
    shares = [
        passed_along(
            lax.slice_in_dim(
                grad_halo,
                (halo_count - distance) * shard_len,
                (halo_count - distance + 1) * shard_len,
                axis=1,
            ),
            "context",
            -distance,
        )
        for distance in range(1, halo_count + 1)
    ]
    first_term = jnp.einsum("th,dh->td", grad_query, query_weight, preferred_element_type=f32)
    query_hidden = jnp.einsum(
        "kn,pn->kp", grad_query, adapter_up_query, preferred_element_type=f32
    )
    grad_key, grad_value = combine(grad_own, shares, cosine, sine)
    key_hidden = jnp.einsum(
        "kn,pn->kp", grad_key, adapter_up_key_value[0], preferred_element_type=f32
    )
    value_hidden = jnp.einsum(
        "kn,pn->kp", grad_value, adapter_up_key_value[1], preferred_element_type=f32
    )
    hidden = (
        adapter_scale * jnp.concatenate([query_hidden, key_hidden, value_hidden], 1)
    ).astype(bf16)
    term = term_sum(first_term, grad_key, grad_value, hidden, key_value_weight, down_all)
    grad_input = lax.psum_scatter(term, "tensor", scatter_dimension=0, tiled=True)[None]

    def over_tokens(low, grads):
        return jnp.einsum("tr,th->rh", low, grads, preferred_element_type=f32)

    wide = jnp.concatenate(
        [over_tokens(hidden, gathered), adapter_scale * over_tokens(factor, incoming)], 0
    ).astype(bf16)
    narrow = jnp.concatenate(
        [
            adapter_scale * over_tokens(adapted_query, grad_query),
            adapter_scale * over_tokens(adapted_key, grad_key),
            adapter_scale * over_tokens(adapted_value, grad_value),
            over_tokens(up_gradient, attended),
        ],
        1,
    ).astype(bf16)
    mine = scattered_rows(wide, "tensor").astype(bf16)
    size = mine.size
    flat = jnp.concatenate([mine.reshape(-1, 128), narrow.reshape(-1, 128)], 0)
    flat = summed_pairwise(summed_pairwise(flat, "context"), "dp")
    wide_sum = gathered_rows(flat[: size // 128].reshape(mine.shape), "tensor").astype(f32)
    narrow_sum = flat[size // 128 :].reshape(narrow.shape).astype(f32)
    q_cols, kv_cols = adapter_up_query.shape[1], adapter_up_key_value.shape[2]
    return (
        grad_input,
        wide_sum[: 3 * rank].reshape(3, rank, width),
        narrow_sum[:, :q_cols],
        jnp.stack(
            [
                narrow_sum[:, q_cols : q_cols + kv_cols],
                narrow_sum[:, q_cols + kv_cols : q_cols + 2 * kv_cols],
            ],
            0,
        ),
        narrow_sum[:, q_cols + 2 * kv_cols :],
        wide_sum[3 * rank :],
    )


def solution(mesh):
    in_specs = (
        P("dp", ("context", "tensor"), None),
        P("dp", ("context", "tensor"), None),
        P("dp", None),
        P(None, "tensor"),
        P(None, None, "tensor"),
        P("tensor", None),
        P(),
        P(None, "tensor"),
        P(None, None, "tensor"),
        P(None, "tensor"),
        P(),
    )
    out_specs = (
        P("dp", ("context", "tensor"), None),
        P(),
        P(None, "tensor"),
        P(None, None, "tensor"),
        P(None, "tensor"),
        P(),
    )
    return jax.shard_map(local, mesh=mesh, in_specs=in_specs, out_specs=out_specs, check_vma=False)
```

time: 732 us -> 436 us (0.60)
  waiting for transfers between devices: 456 us -> 251 us
  matrix products: 151 us -> 65 us
  Pallas kernels: 0 us -> 64.1 us
  other arithmetic: 41.6 us -> 3.34 us
  blocking collectives: 15.8 us -> 0 us
  local copies, waits for them, and re-layouts: 30.4 us -> 15.2 us
  starting transfers between devices: 13.8 us -> 21.9 us
    psum x3 -> x0, waiting for transfers between devices: 172 us -> none  [the longest x1 130 us: local(): grad_down_qkv = lax.psum(grad_down_part, ('dp', 'context', 'tensor'))]
    dot_general x29 -> x21, matrix products: 135 us -> 65 us  [the longest x3 18.5 us: projected(): jnp.dot(gathered, weight, preferred_element_type=f32)]
    reduce_scatter x1, waiting for transfers between devices: 102 us -> 32.2 us  [local(): lax.psum_scatter(term, 'tensor', scatter_dimension=0, tiled=True)[None]]
    ppermute x0 -> x9, waiting for transfers between devices: none -> 65.3 us  [the longest x6 49.7 us: shifted(): lax.ppermute(block, axis, [(i, (i + distance) % n) for i in range(n)])]
    pallas_call x0 -> x6, Pallas kernels: none -> 64.1 us  [the longest x1 20.6 us: attention_forward(): pl.pallas_call(functools.partial(forward_kernel, halo_rows, group, rows),...]
    all_gather x2, waiting for transfers between devices: 167 us -> 117 us  [the longest x1 97.1 us: local(): gathered = lax.all_gather(tokens[0], 'tensor', axis=0, tiled=True)]
    ppermute x4, waiting for transfers between devices: 13.9 us -> 34.7 us  [passed_along(): return lax.ppermute(block, axis, route)]
    convert_element_type x6 -> x7, other arithmetic: 17.3 us -> 0.51 us  [the longest x3 0.22 us: summed_pairwise(): block = (block.astype(f32) + other.astype(f32)).astype(bf16)]
  transfers between devices with their start and end apart: 10 -> 16, of which waited for: 7 -> 16; matrix products, arithmetic and copies ran while one was open for 19% -> 13% of each run, Pallas kernels for 0% -> 7%
where the time goes in v1:
time: 436 us; the launch traced here: 434 us
  waiting for transfers between devices  251 us (58%)
  matrix products  65 us (15%)
  Pallas kernels  64.1 us (15%)
  starting transfers between devices  21.9 us (5%)
  local copies, waits for them, and re-layouts  15.2 us (3%)
  between operations  14.2 us (3%)
    all_gather x1, waiting for transfers between devices, local(): gathered = lax.all_gather(tokens[0], 'tensor', axis=0, tiled=True)  97.1 us
    ppermute x6, waiting for transfers between devices, shifted(): lax.ppermute(block, axis, [(i, (i + distance) % n) for i in range(n)])  49.7 us
    ppermute x4, waiting for transfers between devices, passed_along(): return lax.ppermute(block, axis, route)  34.7 us
    reduce_scatter x1, waiting for transfers between devices, local(): lax.psum_scatter(term, 'tensor', scatter_dimension=0, tiled=True)[None]  32.2 us
    pallas_call x1, Pallas kernels, attention_forward(): pl.pallas_call(functools.partial(forward_kernel, halo_rows, group, rows),...  20.6 us
    all_gather x1, waiting for transfers between devices, local(): incoming = lax.all_gather(output_gradient[0], 'tensor', axis=0, tiled=True)  20 us
    dot_general x3, matrix products, projected(): jnp.dot(gathered, weight, preferred_element_type=f32)  18.5 us
    ppermute x3, waiting for transfers between devices, summed_pairwise(): other = lax.ppermute(block, axis, [(i, i ^ step) for i in range(n)])  15.6 us
  transfers between devices with their start and end apart: 16, of which 16 were waited for; matrix products, arithmetic and copies ran while one was open for 13% of the time, Pallas kernels for 7%

profile of v1, /device:TPU:9, one launch (start us, length us, event | category | flops | bytes accessed | tf_op | source)
XLA Modules:
  0.0 434.5 jit_solution(3685197023715423063)
XLA Ops:
  13.3 97.1 %all-gather.5.cloned.1.call-done = bf16[1,512,5376]{2,1,0:T(8,128)(2,1)} async-done(((bf16[1,128,5376]{2,1,0:T(8,128)(2,1)}), bf16[1,512,5376]{2,1,0:T(8,128)(2,1)}) %all-gather.5.cloned.1.call-update) | async-done | bytes 5505040 | tf_op jit(solution)/shard_map/all_gather | solution.py:357
  110.5 4.4 %fusion.16 = bf16[512,48]{0,1:T(8,128)(2,1)S(1)} fusion(bf16[48,5376]{1,0:T(8,128)(2,1)S(1)} %bitcast.82, bf16[1,512,5376]{2,1,0:T(8,128)(2,1)} %all-gather.5.cloned.1.call-done), kind=kOutput, calls=%fused_computation.23 | convolution fusion | flops 264265728 | bytes 6070272 | tf_op jit(solution)/shard_map/ja,ma->jm/dot_general | solution.py:373
  114.9 5.2 %fusion.3 = f32[512,512]{1,0:T(8,128)S(1)} fusion(bf16[1,512,5376]{2,1,0:T(8,128)(2,1)S(1)} %copy-done.15, bf16[2,5376,512]{2,1,0:T(8,128)(2,1)} %kv_ref.1), kind=kOutput, calls=%fused_computation.6 | convolution fusion | flops 2818572288 | bytes 12058624 | tf_op jit(solution)/shard_map/dot_general | solution.py:379
  121.5 3.0 fusion.1
  125.9 4.0 rope_pair.1.refs_5_.refs_8_
  129.9 3.9 collective-permute-start.1
  136.1 10.3 %fusion.10 = f32[512,1024]{1,0:T(8,128)S(1)} fusion(bf16[5376,1024]{1,0:T(8,128)(2,1)} %param.14, bf16[1,512,5376]{2,1,0:T(8,128)(2,1)} %all-gather.5.cloned.1.call-done), kind=kOutput, calls=%fused_computation.13 | convolution fusion | flops 5637144576 | bytes 18612224 | tf_op jit(solution)/shard_map/dot_general | solution.py:379
  148.2 6.0 %rope_query.1.refs_0_ = bf16[512,1024]{1,0:T(8,128)(2,1)} custom-call(f32[512,1024]{1,0:T(8,128)} %multiply_add_fusion.x_ref, f32[512,128]{1,0:T(8,128)} %get-tuple-element.40.cos_ref.refs_4_, f32[512,128]{1,0:T(8,128)} %get-tuple-element.41.sin_ref.refs_5_), custom_call_target="tpu_custom_call" | custom-call | flops 2097152 | bytes 3145728 | tf_op jit(solution)/shard_map/rope_query/pallas_call | solution.py:58
  155.4 12.8 %collective-permute-done.refs_3_.refs_6_ = bf16[2,512,512]{2,1,0:T(8,128)(2,1)} collective-permute-done((bf16[2,512,512]{2,1,0:T(8,128)(2,1)}, bf16[2,512,512]{2,1,0:T(8,128)(2,1)}, u32[]{:S(2)}, u32[]{:S(2)}) %collective-permute-start) | collective-permute-done | bytes 1048608 | tf_op jit(solution)/shard_map/ppermute | solution.py:22
  171.9 20.6 %attention_forward.1 = (bf16[8,1536,512]{2,1,0:T(8,128)(2,1)}, bf16[512,1024]{1,0:T(8,128)(2,1)S(1)}) custom-call(bf16[512,1024]{1,0:T(8,128)(2,1)S(1)} %copy-done.10, s32[1,512]{1,0:T(1,128)S(1)} %constant_dynamic-slice_fusion.refs_1_, s32[1536,1]{1,0:T(8,128)S(1)} %copy-done.12, bf16[2,512,512]{2,1,0:T(8,128)(2,1)} %collective-permute-done.refs_3_.refs_6_, ...), custom_call_target="tpu_custom_call" | custom-call | flops 3221225472 | bytes 41943040 | tf_op jit(solution)/shard_map/attention_forward/pallas_call | solution.py:140
  192.8 20.0 %all-gather.7.cloned.1.call-done = bf16[1,512,5376]{2,1,0:T(8,128)(2,1)} async-done(((bf16[1,128,5376]{2,1,0:T(8,128)(2,1)}), bf16[1,512,5376]{2,1,0:T(8,128)(2,1)}) %all-gather.7.cloned.1.call-update) | async-done | bytes 5505040 | tf_op jit(solution)/shard_map/all_gather | solution.py:358
  212.8 4.2 fusion.20
  217.1 8.8 %fusion.49 = f32[512,1024]{1,0:T(8,128)S(1)} fusion(bf16[512,5376]{1,0:T(8,128)(2,1)S(1)} %bitcast.86, bf16[1024,5376]{1,0:T(8,128)(2,1)} %param.16), kind=kOutput, calls=%fused_computation.97 | convolution fusion | flops 5637144576 | bytes 18612224 | tf_op jit(solution)/shard_map/td,hd->th/dot_general | solution.py:406
  226.3 14.7 %attention_backward.1 = (bf16[512,1024]{1,0:T(8,128)(2,1)S(1)}, bf16[2,1024,512]{2,1,0:T(8,128)(2,1)}, f32[2,512,512]{2,1,0:T(8,128)}) custom-call(bf16[512,1024]{1,0:T(8,128)(2,1)S(1)} %copy-done.11, bf16[512,1024]{1,0:T(8,128)(2,1)S(1)} %add_convert_fusion.refs_1_, bf16[512,1024]{1,0:T(8,128)(2,1)S(1)} %get-tuple-element.20.refs_2_, ...), custom_call_target="tpu_custom_call" | custom-call | flops 6442450944 | bytes 20971520 | tf_op jit(solution)/shard_map/attention_backward/pallas_call | solution.py:208
  246.8 12.7 %fusion.50.first_ref = f32[512,5376]{1,0:T(8,128)} fusion(bf16[512,1024]{1,0:T(8,128)(2,1)S(1)} %get-tuple-element.22, bf16[5376,1024]{1,0:T(8,128)(2,1)} %param.14), kind=kOutput, calls=%fused_computation.98 | convolution fusion | flops 5637144576 | bytes 23068672 | tf_op jit(solution)/shard_map/th,dh->td/dot_general | solution.py:425
  259.5 9.7 %collective-permute-done.3.refs_1_ = bf16[2,512,512]{2,1,0:T(8,128)(2,1)} collective-permute-done((bf16[2,512,512]{2,1,0:T(8,128)(2,1)S(1)}, bf16[2,512,512]{2,1,0:T(8,128)(2,1)}, u32[]{:S(2)}, u32[]{:S(2)}) %collective-permute-start.3) | collective-permute-done | bytes 1048608 | tf_op jit(solution)/shard_map/ppermute | solution.py:22
  269.2 11.9 %collective-permute-done.2.refs_0_ = bf16[2,512,512]{2,1,0:T(8,128)(2,1)} collective-permute-done((bf16[2,512,512]{2,1,0:T(8,128)(2,1)S(1)}, bf16[2,512,512]{2,1,0:T(8,128)(2,1)}, u32[]{:S(2)}, u32[]{:S(2)}) %collective-permute-start.2) | collective-permute-done | bytes 1048608 | tf_op jit(solution)/shard_map/ppermute | solution.py:22
  281.2 4.5 %combine_pairs.1 = (bf16[512,512]{1,0:T(8,128)(2,1)}, bf16[512,512]{1,0:T(8,128)(2,1)}) custom-call(f32[2,512,512]{2,1,0:T(8,128)} %get-tuple-element.23.own_ref, f32[512,128]{1,0:T(8,128)} %get-tuple-element.40.cos_ref.refs_4_, f32[512,128]{1,0:T(8,128)} %get-tuple-element.41.sin_ref.refs_5_, bf16[2,512,512]{2,1,0:T(8,128)(2,1)} %collective-permute-done.2.refs_0_, ...), custom_call_target="tpu_custom_call" | custom-call | flops 2097152 | bytes 5242880 | tf_op jit(solution)/shard_map/combine_pairs/pallas_call | solution.py:259
  290.5 14.4 %input_term.1 = bf16[512,5376]{1,0:T(8,128)(2,1)} custom-call(f32[512,5376]{1,0:T(8,128)} %fusion.50.first_ref, bf16[512,512]{1,0:T(8,128)(2,1)S(1)} %copy-done.4, bf16[512,512]{1,0:T(8,128)(2,1)S(1)} %copy-done.2, bf16[512,48]{1,0:T(8,128)(2,1)S(1)} %multiply_convert_fusion.hid_ref, bf16[2,5376,512]{2,1,0:T(8,128)(2,1)} %kv_ref.1, bf16[48,5376]{1,0:T(8,128)(2,1)S(1)} %bitcast.83), custom_call_target="tpu_custom_call" | custom-call | flops 5637144576 | bytes 29360128 | tf_op jit(solution)/shard_map/input_term/pallas_call | solution.py:282
  305.5 3.4 fusion
  308.9 3.8 convolution_convert_fusion
  312.8 3.2 collective-permute-start.4
  318.7 8.9 %collective-permute-done.4 = bf16[16,5376]{1,0:T(8,128)(2,1)S(1)} collective-permute-done((bf16[16,5376]{1,0:T(8,128)(2,1)S(1)}, bf16[16,5376]{1,0:T(8,128)(2,1)S(1)}, u32[]{:S(2)}, u32[]{:S(2)}) %collective-permute-start.4) | collective-permute-done | bytes 172064 | tf_op jit(solution)/shard_map/ppermute | solution.py:305
  327.6 3.2 collective-permute-done.6
  330.9 12.1 %collective-permute-done.5 = bf16[16,5376]{1,0:T(8,128)(2,1)S(1)} collective-permute-done((bf16[16,5376]{1,0:T(8,128)(2,1)S(1)}, bf16[16,5376]{1,0:T(8,128)(2,1)S(1)}, u32[]{:S(2)}, u32[]{:S(2)}) %collective-permute-start.5) | collective-permute-done | bytes 172064 | tf_op jit(solution)/shard_map/ppermute | solution.py:305
  345.1 8.0 %collective-permute-done.8 = bf16[1056,128]{1,0:T(8,128)(2,1)S(1)} collective-permute-done((bf16[1056,128]{1,0:T(8,128)(2,1)S(1)}, bf16[1056,128]{1,0:T(8,128)(2,1)S(1)}, u32[]{:S(2)}, u32[]{:S(2)}) %collective-permute-start.8) | collective-permute-done | bytes 270368 | tf_op jit(solution)/shard_map/ppermute | solution.py:314
  354.5 6.0 %collective-permute-done.9 = bf16[1056,128]{1,0:T(8,128)(2,1)S(1)} collective-permute-done((bf16[1056,128]{1,0:T(8,128)(2,1)S(1)}, bf16[1056,128]{1,0:T(8,128)(2,1)S(1)}, u32[]{:S(2)}, u32[]{:S(2)}) %collective-permute-start.9) | collective-permute-done | bytes 270368 | tf_op jit(solution)/shard_map/ppermute | solution.py:314
  361.1 2.9 collective-permute-start.11
  367.7 8.5 %collective-permute-done.12 = bf16[16,5376]{1,0:T(8,128)(2,1)S(1)} collective-permute-done((bf16[16,5376]{1,0:T(8,128)(2,1)S(1)}, bf16[16,5376]{1,0:T(8,128)(2,1)S(1)}, u32[]{:S(2)}, u32[]{:S(2)}) %collective-permute-start.12) | collective-permute-done | bytes 172064 | tf_op jit(solution)/shard_map/ppermute | solution.py:305
  376.1 5.7 %collective-permute-done.11 = bf16[16,5376]{1,0:T(8,128)(2,1)S(1)} collective-permute-done((bf16[16,5376]{1,0:T(8,128)(2,1)S(1)}, bf16[16,5376]{1,0:T(8,128)(2,1)S(1)}, u32[]{:S(2)}, u32[]{:S(2)}) %collective-permute-start.11) | collective-permute-done | bytes 172064 | tf_op jit(solution)/shard_map/ppermute | solution.py:305
  381.9 11.3 %collective-permute-done.10 = bf16[16,5376]{1,0:T(8,128)(2,1)S(1)} collective-permute-done((bf16[16,5376]{1,0:T(8,128)(2,1)S(1)}, bf16[16,5376]{1,0:T(8,128)(2,1)S(1)}, u32[]{:S(2)}, u32[]{:S(2)}) %collective-permute-start.10) | collective-permute-done | bytes 172064 | tf_op jit(solution)/shard_map/ppermute | solution.py:305
  395.8 32.2 %reduce-scatter.2.cloned.1.call-done = bf16[128,5376]{1,0:T(8,128)(2,1)} async-done(((bf16[512,5376]{1,0:T(8,128)(2,1)}), bf16[128,5376]{1,0:T(8,128)(2,1)}) %reduce-scatter.2.cloned.1.call-update) | async-done | bytes 1376272 | tf_op jit(solution)/shard_map/reduce_scatter | solution.py:440
  (117 shorter events, 42.7 us)
Async XLA Ops:
  7.2 205.6 %copy-start = (bf16[16,5376]{1,0:T(8,128)(2,1)S(1)}, bf16[16,5376]{1,0:T(8,128)(2,1)}, u32[]{:S(2)}) copy-start(bf16[16,5376]{1,0:T(8,128)(2,1)} %param.21) | copy-start | bytes 516100
  7.2 103.3 %copy-start.8 = (bf16[3,16,5376]{2,1,0:T(8,128)(2,1)S(1)}, bf16[3,16,5376]{2,1,0:T(8,128)(2,1)}, u32[]{:S(2)}) copy-start(bf16[3,16,5376]{2,1,0:T(8,128)(2,1)} %param.17) | copy-start | bytes 1548292
  7.2 103.3 %all-gather.5.cloned.1.call-start = ((), (), s32[]{:S(2)}) async-start(), calls=%async_computation.2 | async-start | bytes 6881280 | tf_op jit(solution)/shard_map/all_gather | solution.py:357
  7.9 204.9 %all-gather.7.cloned.1.call-start = ((), (), s32[]{:S(2)}) async-start(), calls=%async_computation.3 | async-start | bytes 6881280 | tf_op jit(solution)/shard_map/all_gather | solution.py:358
  8.7 419.3 %reduce-scatter.2.cloned.1.call-start = ((), (), s32[]{:S(2)}) async-start(), calls=%async_computation.1 | async-start | bytes 6881280 | tf_op jit(solution)/shard_map/reduce_scatter | solution.py:440
  110.5 4.4 %copy-start.15 = (bf16[1,512,5376]{2,1,0:T(8,128)(2,1)S(1)}, bf16[1,512,5376]{2,1,0:T(8,128)(2,1)}, u32[]{:S(2)}) copy-start(bf16[1,512,5376]{2,1,0:T(8,128)(2,1)} %all-gather.5.cloned.1.call-done) | copy-start | bytes 16515076
  110.5 11.0 %slice-start = ((s8[11010048]{0:T(1024)(128)(4,1)}), s8[4194304]{0:T(1024)(128)(4,1)S(1)}, s32[]{:S(2)}) async-start(s8[11010048]{0:T(1024)(128)(4,1)} %bitcast.87), calls=%async_computation.4 | async-start | bytes 8388608
  114.9 5.3 %copy-start.19 = (bf16[2,16,512]{2,1,0:T(8,128)(2,1)S(1)}, bf16[2,16,512]{2,1,0:T(8,128)(2,1)}, u32[]{:S(2)}) copy-start(bf16[2,16,512]{2,1,0:T(8,128)(2,1)} %param.19) | copy-start | bytes 98308
  114.9 6.6 %slice-start.1 = ((s8[11010048]{0:T(1024)(128)(4,1)}), s8[4194304]{0:T(1024)(128)(4,1)S(1)}, s32[]{:S(2)}) async-start(s8[11010048]{0:T(1024)(128)(4,1)} %bitcast.87), calls=%async_computation.5 | async-start | bytes 8388608
  114.9 6.6 %slice-start.2 = ((s8[11010048]{0:T(1024)(128)(4,1)}), s8[2621440]{0:T(1024)(128)(4,1)S(1)}, s32[]{:S(2)}) async-start(s8[11010048]{0:T(1024)(128)(4,1)} %bitcast.87), calls=%async_computation.6 | async-start | bytes 5242880
  129.9 16.5 %copy-start.18 = (bf16[16,1024]{1,0:T(8,128)(2,1)S(1)}, bf16[16,1024]{1,0:T(8,128)(2,1)}, u32[]{:S(2)}) copy-start(bf16[16,1024]{1,0:T(8,128)(2,1)} %param.18) | copy-start | bytes 98308
  129.9 24.6 %collective-permute-start.1 = (bf16[2,512,512]{2,1,0:T(8,128)(2,1)}, bf16[2,512,512]{2,1,0:T(8,128)(2,1)S(1)}, u32[]{:S(2)}, u32[]{:S(2)}) collective-permute-start(bf16[2,512,512]{2,1,0:T(8,128)(2,1)} %rope_pair.1.refs_5_.refs_8_), channel_id=1, source_target_pairs={{0,4},{4,8},{8,12},{1,5},{5,9},{9,13},{2,6},{6,10},{10,14},{3,7},{... | collective-permute-start | bytes 3145736 | tf_op jit(solution)/shard_map/ppermute | solution.py:22
  133.7 34.5 %collective-permute-start = (bf16[2,512,512]{2,1,0:T(8,128)(2,1)}, bf16[2,512,512]{2,1,0:T(8,128)(2,1)}, u32[]{:S(2)}, u32[]{:S(2)}) collective-permute-start(bf16[2,512,512]{2,1,0:T(8,128)(2,1)} %rope_pair.1.refs_5_.refs_8_), channel_id=1, source_target_pairs={{0,8},{4,12},{1,9},{5,13},{2,10},{6,14},{3,11},{7,15},{16,24},{20,... | collective-permute-start | bytes 3145736 | tf_op jit(solution)/shard_map/ppermute | solution.py:22
  146.4 21.9 %copy-start.9 = (bf16[2,512,512]{2,1,0:T(8,128)(2,1)S(1)}, bf16[2,512,512]{2,1,0:T(8,128)(2,1)}, u32[]{:S(2)}) copy-start(bf16[2,512,512]{2,1,0:T(8,128)(2,1)} %rope_pair.1.refs_5_.refs_8_) | copy-start | bytes 3145732
  148.2 44.2 %copy-start.17 = (bf16[16,1024]{1,0:T(8,128)(2,1)S(1)}, bf16[16,1024]{1,0:T(8,128)(2,1)}, u32[]{:S(2)}) copy-start(bf16[16,1024]{1,0:T(8,128)(2,1)} %param.20) | copy-start | bytes 98308
  217.0 9.3 %copy-start.6 = (f32[512,128]{1,0:T(8,128)S(1)}, f32[512,128]{1,0:T(8,128)}, u32[]{:S(2)}) copy-start(f32[512,128]{1,0:T(8,128)} %get-tuple-element.40.cos_ref.refs_4_) | copy-start | bytes 786436
  217.0 9.3 %copy-start.7 = (f32[512,128]{1,0:T(8,128)S(1)}, f32[512,128]{1,0:T(8,128)}, u32[]{:S(2)}) copy-start(f32[512,128]{1,0:T(8,128)} %get-tuple-element.41.sin_ref.refs_5_) | copy-start | bytes 786436
  217.0 9.3 %copy-start.11 = (bf16[512,1024]{1,0:T(8,128)(2,1)S(1)}, bf16[512,1024]{1,0:T(8,128)(2,1)}, u32[]{:S(2)}) copy-start(bf16[512,1024]{1,0:T(8,128)(2,1)} %rope_query.1.refs_0_) | copy-start | bytes 3145732
  243.0 26.2 %collective-permute-start.3 = (bf16[2,512,512]{2,1,0:T(8,128)(2,1)S(1)}, bf16[2,512,512]{2,1,0:T(8,128)(2,1)}, u32[]{:S(2)}, u32[]{:S(2)}) collective-permute-start(bf16[2,512,512]{2,1,0:T(8,128)(2,1)S(1)} %get-tuple-element.28), channel_id=1, source_target_pairs={{8,0},{12,4},{9,1},{13,5},{10,2},{14,6},{11,3},{15,7},{24,16},{28,... | collective-permute-start | bytes 3145736 | tf_op jit(solution)/shard_map/ppermute | solution.py:22
  244.3 36.8 %collective-permute-start.2 = (bf16[2,512,512]{2,1,0:T(8,128)(2,1)S(1)}, bf16[2,512,512]{2,1,0:T(8,128)(2,1)}, u32[]{:S(2)}, u32[]{:S(2)}) collective-permute-start(bf16[2,512,512]{2,1,0:T(8,128)(2,1)S(1)} %get-tuple-element.29), channel_id=1, source_target_pairs={{4,0},{8,4},{12,8},{5,1},{9,5},{13,9},{6,2},{10,6},{14,10},{7,3},{... | collective-permute-start | bytes 3145736 | tf_op jit(solution)/shard_map/ppermute | solution.py:22
  308.9 9.4 %copy-start.5 = (bf16[512,512]{1,0:T(8,128)(2,1)S(1)}, bf16[512,512]{1,0:T(8,128)(2,1)}, u32[]{:S(2)}) copy-start(bf16[512,512]{1,0:T(8,128)(2,1)} %get-tuple-element.25.dk_ref) | copy-start | bytes 1572868
  308.9 9.5 %copy-start.3 = (bf16[512,512]{1,0:T(8,128)(2,1)S(1)}, bf16[512,512]{1,0:T(8,128)(2,1)}, u32[]{:S(2)}) copy-start(bf16[512,512]{1,0:T(8,128)(2,1)} %get-tuple-element.26.dv_ref) | copy-start | bytes 1572868
  312.8 14.8 %collective-permute-start.4 = (bf16[16,5376]{1,0:T(8,128)(2,1)S(1)}, bf16[16,5376]{1,0:T(8,128)(2,1)S(1)}, u32[]{:S(2)}, u32[]{:S(2)}) collective-permute-start(bf16[16,5376]{1,0:T(8,128)(2,1)S(1)} %get-tuple-element.30), channel_id=1, source_target_pairs={{0,1},{1,2},{2,3},{3,0},{4,5},{5,6},{6,7},{7,4},{8,9},{9,10},{10,1... | collective-permute-start | bytes 516104 | tf_op jit(solution)/shard_map/ppermute | solution.py:305
  316.1 14.8 %collective-permute-start.6 = (bf16[16,5376]{1,0:T(8,128)(2,1)S(1)}, bf16[16,5376]{1,0:T(8,128)(2,1)S(1)}, u32[]{:S(2)}, u32[]{:S(2)}) collective-permute-start(bf16[16,5376]{1,0:T(8,128)(2,1)S(1)} %get-tuple-element.31), channel_id=1, source_target_pairs={{0,3},{1,0},{2,1},{3,2},{4,7},{5,4},{6,5},{7,6},{8,11},{9,8},{10,9... | collective-permute-start | bytes 516104 | tf_op jit(solution)/shard_map/ppermute | solution.py:305
  316.2 26.7 %collective-permute-start.5 = (bf16[16,5376]{1,0:T(8,128)(2,1)S(1)}, bf16[16,5376]{1,0:T(8,128)(2,1)S(1)}, u32[]{:S(2)}, u32[]{:S(2)}) collective-permute-start(bf16[16,5376]{1,0:T(8,128)(2,1)S(1)} %get-tuple-element.32), channel_id=1, source_target_pairs={{0,2},{1,3},{2,0},{3,1},{4,6},{5,7},{6,4},{7,5},{8,10},{9,11},{10,... | collective-permute-start | bytes 516104 | tf_op jit(solution)/shard_map/ppermute | solution.py:305
  343.3 1.6 collective-permute-start.7
  345.0 8.1 %collective-permute-start.8 = (bf16[1056,128]{1,0:T(8,128)(2,1)S(1)}, bf16[1056,128]{1,0:T(8,128)(2,1)S(1)}, u32[]{:S(2)}, u32[]{:S(2)}) collective-permute-start(bf16[1056,128]{1,0:T(8,128)(2,1)S(1)} %add_convert_fusion.3), channel_id=1, source_target_pairs={{0,8},{4,12},{8,0},{12,4},{1,9},{5,13},{9,1},{13,5},{2,10},{6,14},... | collective-permute-start | bytes 811016 | tf_op jit(solution)/shard_map/ppermute | solution.py:314
  353.1 74.9 %copy-start.1 = (bf16[16,5376]{1,0:T(8,128)(2,1)S(1)}, bf16[16,5376]{1,0:T(8,128)(2,1)}, u32[]{:S(2)}) copy-start(bf16[16,5376]{1,0:T(8,128)(2,1)} %param.21) | copy-start | bytes 516100
  353.2 7.3 %collective-permute-start.9 = (bf16[1056,128]{1,0:T(8,128)(2,1)S(1)}, bf16[1056,128]{1,0:T(8,128)(2,1)S(1)}, u32[]{:S(2)}, u32[]{:S(2)}) collective-permute-start(bf16[1056,128]{1,0:T(8,128)(2,1)S(1)} %add_convert_fusion.2), channel_id=1, source_target_pairs={{0,16},{16,0},{1,17},{17,1},{2,18},{18,2},{3,19},{19,3},{4,20},{20... | collective-permute-start | bytes 811016 | tf_op jit(solution)/shard_map/ppermute | solution.py:314
  361.0 15.1 %collective-permute-start.12 = (bf16[16,5376]{1,0:T(8,128)(2,1)S(1)}, bf16[16,5376]{1,0:T(8,128)(2,1)S(1)}, u32[]{:S(2)}, u32[]{:S(2)}) collective-permute-start(bf16[16,5376]{1,0:T(8,128)(2,1)S(1)} %reshape.107), channel_id=1, source_target_pairs={{0,3},{1,0},{2,1},{3,2},{4,7},{5,4},{6,5},{7,6},{8,11},{9,8},{10,9... | collective-permute-start | bytes 516104 | tf_op jit(solution)/shard_map/ppermute | solution.py:305
  361.1 20.8 %collective-permute-start.11 = (bf16[16,5376]{1,0:T(8,128)(2,1)S(1)}, bf16[16,5376]{1,0:T(8,128)(2,1)S(1)}, u32[]{:S(2)}, u32[]{:S(2)}) collective-permute-start(bf16[16,5376]{1,0:T(8,128)(2,1)S(1)} %reshape.107), channel_id=1, source_target_pairs={{0,2},{1,3},{2,0},{3,1},{4,6},{5,7},{6,4},{7,5},{8,10},{9,11},{10,... | collective-permute-start | bytes 516104 | tf_op jit(solution)/shard_map/ppermute | solution.py:305
  364.0 29.1 %collective-permute-start.10 = (bf16[16,5376]{1,0:T(8,128)(2,1)S(1)}, bf16[16,5376]{1,0:T(8,128)(2,1)S(1)}, u32[]{:S(2)}, u32[]{:S(2)}) collective-permute-start(bf16[16,5376]{1,0:T(8,128)(2,1)S(1)} %reshape.107), channel_id=1, source_target_pairs={{0,1},{1,2},{2,3},{3,0},{4,5},{5,6},{6,7},{7,4},{8,9},{9,10},{10,1... | collective-permute-start | bytes 516104 | tf_op jit(solution)/shard_map/ppermute | solution.py:305
  (7 other events, 10.9 us)
Sparse Core Ops, SparseCore 0:
  9.6 100.8 all-gather.4
  112.0 100.7 all-gather.6
  305.0 122.8 reduce-scatter.1

commit v2 on v1

--- a/solution.py
+++ b/solution.py
@@ -195,32 +195,37 @@
     own_ref[1] = dv_buf[halo_rows:]
 
 
-def attention_backward(queries, grads, attended, weights, pairs, cosine, sine):
+def attention_backward(queries, grads, attended, weights, pairs, cosine, sine, part, parts):
     count, q_cols = queries.shape
     kv_cols = pairs[0].shape[2]
     group = q_cols // kv_cols
+    q_cols, kv_cols = q_cols // parts, kv_cols // parts
+    heads = kv_cols // HEAD_SIZE
+    first = part * heads
     keys = count * len(pairs)
     rows = min(256, count)
     halo_rows = keys - count
-    q_spec = pl.BlockSpec((count, group * HEAD_SIZE), lambda h: (0, h))
-    pair_spec = pl.BlockSpec((2, count, HEAD_SIZE), lambda h: (0, 0, h))
+    q_in = pl.BlockSpec((count, group * HEAD_SIZE), lambda h: (0, h + first))
+    q_out = pl.BlockSpec((count, group * HEAD_SIZE), lambda h: (0, h))
+    pair_in = pl.BlockSpec((2, count, HEAD_SIZE), lambda h: (0, 0, h + first))
+    pair_out = pl.BlockSpec((2, count, HEAD_SIZE), lambda h: (0, 0, h))
     table = pl.BlockSpec((count, HEAD_SIZE), lambda h: (0, 0))
     return pl.pallas_call(
         functools.partial(backward_kernel, halo_rows, group, rows, len(pairs)),
-        grid=(kv_cols // HEAD_SIZE,),
+        grid=(heads,),
         in_specs=[
-            q_spec,
-            q_spec,
-            q_spec,
-            pl.BlockSpec((group, keys, count), lambda h: (h, 0, 0)),
+            q_in,
+            q_in,
+            q_in,
+            pl.BlockSpec((group, keys, count), lambda h: (h + first, 0, 0)),
             table,
             table,
         ]
-        + [pair_spec] * len(pairs),
+        + [pair_in] * len(pairs),
         out_specs=[
-            q_spec,
+            q_out,
             pl.BlockSpec((2, halo_rows, HEAD_SIZE), lambda h: (0, 0, h)),
-            pair_spec,
+            pair_out,
         ],
         out_shape=[
             jax.ShapeDtypeStruct((count, q_cols), bf16),
@@ -267,42 +272,55 @@
     )(own, cosine, sine, *shares)
 
 
-def term_kernel(first_ref, dk_ref, dv_ref, hid_ref, kv_ref, down_ref, out_ref):
-    total = first_ref[...] + dot(dk_ref[...], kv_ref[0], NT)
-    total = total + dot(dv_ref[...], kv_ref[1], NT)
-    total = total + dot(hid_ref[...], down_ref[...], (((1,), (0,)), ((), ())))
+def term_kernel(parts, *refs):
+    first_ref, hid_ref, kv_ref, down_ref = refs[:4]
+    out_ref = refs[-1]
+    total = first_ref[...] + dot(hid_ref[...], down_ref[...], TN)
+    cols = kv_ref.shape[2] // parts
+    for p in range(parts):
+        here = slice(p * cols, (p + 1) * cols)
+        total = total + dot(refs[4 + p][...], kv_ref[0, :, here], NT)
+        total = total + dot(refs[4 + parts + p][...], kv_ref[1, :, here], NT)
     out_ref[...] = total.astype(bf16)
 
 
 def term_sum(first, dk, dv, hidden, kv_weight, down):
     count, width = first.shape
-    tile = next(t for t in (768, 384, 256, 128, width) if width % t == 0)
+    tile = next(t for t in (896, 768, 384, 256, 128, width) if width % t == 0)
     whole = lambda a: pl.BlockSpec(a.shape, lambda i: (0, 0))
-    block = pl.BlockSpec((count, tile), lambda i: (0, i))
-    return pl.pallas_call(
-        term_kernel,
+    return pl.pallas_call(
+        functools.partial(term_kernel, len(dk)),
         grid=(width // tile,),
         in_specs=[
-            block,
-            whole(dk),
-            whole(dv),
+            pl.BlockSpec((count, tile), lambda i: (0, i)),
             whole(hidden),
             pl.BlockSpec((2, tile, kv_weight.shape[2]), lambda i: (0, i, 0)),
             pl.BlockSpec((down.shape[0], tile), lambda i: (0, i)),
-        ],
-        out_specs=block,
+        ]
+        + [whole(a) for a in dk + dv],
+        out_specs=pl.BlockSpec((count, tile), lambda i: (0, i)),
         out_shape=jax.ShapeDtypeStruct((count, width), bf16),
         compiler_params=pltpu.CompilerParams(vmem_limit_bytes=48 << 20),
         name="input_term",
         cost_estimate=pl.CostEstimate(
-            flops=4 * count * width * dk.shape[1], bytes_accessed=28 << 20, transcendentals=0
+            flops=4 * count * width * kv_weight.shape[2],
+            bytes_accessed=28 * width * count // 5,
+            transcendentals=0,
         ),
-    )(first, dk, dv, hidden, kv_weight, down)
-
-
-def shifted(block, axis, distance):
-    n = lax.axis_size(axis)
-    return lax.ppermute(block, axis, [(i, (i + distance) % n) for i in range(n)])
+    )(first, hidden, kv_weight, down, *dk, *dv)
+
+
+def after(block, *others):
+    anywhere = pl.BlockSpec(memory_space=pl.ANY)
+    return pl.pallas_call(
+        lambda *refs: None,
+        in_specs=[anywhere] * (1 + len(others)),
+        out_specs=anywhere,
+        out_shape=jax.ShapeDtypeStruct(block.shape, block.dtype),
+        input_output_aliases={0: 0},
+        name="after",
+        cost_estimate=pl.CostEstimate(flops=0, bytes_accessed=0, transcendentals=0),
+    )(block, *others)
 
 
 def summed_pairwise(block, axis):
@@ -319,19 +337,31 @@
 
 def scattered_rows(block, axis):
     n, me = lax.axis_size(axis), lax.axis_index(axis)
-    blocks = block.reshape(n, block.shape[0] // n, block.shape[1])
-    total = lax.dynamic_index_in_dim(blocks, me, 0, keepdims=False).astype(f32)
-    for d in range(1, n):
-        part = lax.dynamic_index_in_dim(blocks, (me + d) % n, 0, keepdims=False)
-        total = total + shifted(part, axis, d).astype(f32)
-    return total
+    if n & (n - 1):
+        return lax.psum_scatter(block, axis, scatter_dimension=0, tiled=True)
+    step = n // 2
+    while step:
+        halves = block.reshape(2, block.shape[0] // 2, block.shape[1])
+        bit = (me // step) % 2
+        keep = jnp.where(bit == 0, halves[0], halves[1])
+        give = jnp.where(bit == 0, halves[1], halves[0])
+        got = lax.ppermute(give, axis, [(i, i ^ step) for i in range(n)])
+        block = (keep.astype(f32) + got.astype(f32)).astype(bf16)
+        step //= 2
+    return block
 
 
 def gathered_rows(block, axis):
     n, me = lax.axis_size(axis), lax.axis_index(axis)
-    parts = jnp.stack([block] + [shifted(block, axis, d) for d in range(1, n)], 0)
-    order = (me - jnp.arange(n)) % n
-    return jnp.take(parts, order, axis=0).reshape(n * block.shape[0], block.shape[1])
+    if n & (n - 1):
+        return lax.all_gather(block, axis, axis=0, tiled=True)
+    step = 1
+    while step < n:
+        got = lax.ppermute(block, axis, [(i, i ^ step) for i in range(n)])
+        first = (me // step) % 2 == 0
+        block = jnp.concatenate([jnp.where(first, block, got), jnp.where(first, got, block)], 0)
+        step *= 2
+    return block
 
 
 def local(
@@ -406,55 +436,78 @@
         jnp.einsum("td,hd->th", incoming, output_weight, preferred_element_type=f32)
         + jnp.dot(up_gradient, adapter_down_output, preferred_element_type=f32)
     ).astype(bf16)
-    grad_query, grad_halo, grad_own = attention_backward(
-        queries, grad_attended, attended, weights, pairs, cosine, sine
-    )
-    shares = [
-        passed_along(
-            lax.slice_in_dim(
-                grad_halo,
-                (halo_count - distance) * shard_len,
-                (halo_count - distance + 1) * shard_len,
-                axis=1,
-            ),
-            "context",
-            -distance,
+    kv_heads = key_value_weight.shape[2] // HEAD_SIZE
+    parts = 2 if kv_heads % 2 == 0 else 1
+    grad_queries, owns, arrivals = [], [], []
+    for part in range(parts):
+        grad_part, grad_halo, grad_own = attention_backward(
+            queries, grad_attended, attended, weights, pairs, cosine, sine, part, parts
         )
-        for distance in range(1, halo_count + 1)
-    ]
+        grad_queries.append(grad_part)
+        owns.append(grad_own)
+        arrivals.append(
+            [
+                passed_along(
+                    lax.slice_in_dim(
+                        grad_halo,
+                        (halo_count - distance) * shard_len,
+                        (halo_count - distance + 1) * shard_len,
+                        axis=1,
+                    ),
+                    "context",
+                    -distance,
+                )
+                for distance in range(1, halo_count + 1)
+            ]
+        )
+    grad_query = jnp.concatenate(grad_queries, 1)
     first_term = jnp.einsum("th,dh->td", grad_query, query_weight, preferred_element_type=f32)
-    query_hidden = jnp.einsum(
-        "kn,pn->kp", grad_query, adapter_up_query, preferred_element_type=f32
-    )
-    grad_key, grad_value = combine(grad_own, shares, cosine, sine)
-    key_hidden = jnp.einsum(
-        "kn,pn->kp", grad_key, adapter_up_key_value[0], preferred_element_type=f32
-    )
-    value_hidden = jnp.einsum(
-        "kn,pn->kp", grad_value, adapter_up_key_value[1], preferred_element_type=f32
-    )
+    grad_keys, grad_values = [], []
+    for own, shares in zip(owns, arrivals):
+        grad_key, grad_value = combine(own, shares, cosine, sine)
+        grad_keys.append(grad_key)
+        grad_values.append(grad_value)
+
+    def lowered(up, grads):
+        ups = jnp.split(up, len(grads), 1)
+        return sum(
+            jnp.einsum("pn,kn->pk", u, g, preferred_element_type=f32) for u, g in zip(ups, grads)
+        )
+
     hidden = (
-        adapter_scale * jnp.concatenate([query_hidden, key_hidden, value_hidden], 1)
+        adapter_scale
+        * jnp.concatenate(
+            [
+                lowered(adapter_up_query, [grad_query]),
+                lowered(adapter_up_key_value[0], grad_keys),
+                lowered(adapter_up_key_value[1], grad_values),
+            ],
+            0,
+        )
     ).astype(bf16)
-    term = term_sum(first_term, grad_key, grad_value, hidden, key_value_weight, down_all)
+    term = term_sum(first_term, grad_keys, grad_values, hidden, key_value_weight, down_all)
     grad_input = lax.psum_scatter(term, "tensor", scatter_dimension=0, tiled=True)[None]
 
     def over_tokens(low, grads):
         return jnp.einsum("tr,th->rh", low, grads, preferred_element_type=f32)
 
-    wide = jnp.concatenate(
-        [over_tokens(hidden, gathered), adapter_scale * over_tokens(factor, incoming)], 0
+    low_rows = jnp.concatenate([hidden, (adapter_scale * factor.astype(f32)).astype(bf16).T], 0)
+    low_rows = after(low_rows, term)
+    mine_low = scattered_rows(low_rows, "tensor")
+    row_at = lax.axis_index("tensor") * mine_low.shape[0] + jnp.arange(mine_low.shape[0])
+    from_tokens = (row_at < 3 * rank)[:, None]
+    zero = jnp.zeros_like(mine_low)
+    mine = (
+        jnp.dot(jnp.where(from_tokens, mine_low, zero), gathered, preferred_element_type=f32)
+        + jnp.dot(jnp.where(from_tokens, zero, mine_low), incoming, preferred_element_type=f32)
     ).astype(bf16)
     narrow = jnp.concatenate(
-        [
-            adapter_scale * over_tokens(adapted_query, grad_query),
-            adapter_scale * over_tokens(adapted_key, grad_key),
-            adapter_scale * over_tokens(adapted_value, grad_value),
-            over_tokens(up_gradient, attended),
-        ],
+        [adapter_scale * over_tokens(adapted_query, grad_query)]
+        + [adapter_scale * over_tokens(adapted_key, g) for g in grad_keys]
+        + [adapter_scale * over_tokens(adapted_value, g) for g in grad_values]
+        + [over_tokens(up_gradient, attended)],
         1,
     ).astype(bf16)
-    mine = scattered_rows(wide, "tensor").astype(bf16)
     size = mine.size
     flat = jnp.concatenate([mine.reshape(-1, 128), narrow.reshape(-1, 128)], 0)
     flat = summed_pairwise(summed_pairwise(flat, "context"), "dp")

time: 436 us -> 430 us (0.986)
  waiting for transfers between devices: 251 us -> 221 us
  starting transfers between devices: 21.9 us -> 34.8 us
    reduce_scatter x1, waiting for transfers between devices: 32.2 us -> 16.5 us  [local(): lax.psum_scatter(term, 'tensor', scatter_dimension=0, tiled=True)[None]]
    ppermute x4 -> x6, waiting for transfers between devices: 34.7 us -> 23.1 us  [passed_along(): return lax.ppermute(block, axis, route)]
    ppermute x3, starting transfers between devices: 1.23 us -> 12 us  [summed_pairwise(): other = lax.ppermute(block, axis, [(i, i ^ step) for i in range(n)])]
    dot_general x3 -> x7, matrix products: 2.94 us -> 12.3 us  [the longest x5 4.88 us: lowered(): jnp.einsum('pn,kn->pk', u, g, preferred_element_type=f32)]
    dot_general x6, matrix products: 8.1 us -> 1.11 us  [over_tokens(): return jnp.einsum('tr,th->rh', low, grads, preferred_element_type=f32)]
    unnamed x47 -> x76, local copies, waits for them, and re-layouts: 6.77 us -> 11.9 us
    ppermute x4 -> x6, starting transfers between devices: 9.92 us -> 12.4 us  [passed_along(): return lax.ppermute(block, axis, route)]
    pallas_call x1 -> x2, Pallas kernels: 14.7 us -> 16.4 us  [attention_backward(): pl.pallas_call(functools.partial(backward_kernel, halo_rows, group, rows,...]
  transfers between devices with their start and end apart: 16 -> 16, of which waited for: 16 -> 14; matrix products, arithmetic and copies ran while one was open for 13% -> 15% of each run, Pallas kernels for 7% -> 8%
where the time goes in v2:
time: 430 us; the launch traced here: 429 us
  waiting for transfers between devices  221 us (51%)
  matrix products  67.4 us (16%)
  Pallas kernels  65.9 us (15%)
  starting transfers between devices  34.8 us (8%)
  local copies, waits for them, and re-layouts  18.6 us (4%)
  between operations  14.3 us (3%)
  other arithmetic  6.77 us (2%)
    all_gather x1, waiting for transfers between devices, local(): gathered = lax.all_gather(tokens[0], 'tensor', axis=0, tiled=True)  96.4 us
    ppermute x2, waiting for transfers between devices, gathered_rows(): got = lax.ppermute(block, axis, [(i, i ^ step) for i in range(n)])  46.8 us
    ppermute x6, waiting for transfers between devices, passed_along(): return lax.ppermute(block, axis, route)  23.1 us
    all_gather x1, waiting for transfers between devices, local(): incoming = lax.all_gather(output_gradient[0], 'tensor', axis=0, tiled=True)  20.1 us
    pallas_call x1, Pallas kernels, attention_forward(): pl.pallas_call(functools.partial(forward_kernel, halo_rows, group, rows),...  20 us
    dot_general x3, matrix products, projected(): jnp.dot(gathered, weight, preferred_element_type=f32)  18.5 us
    reduce_scatter x1, waiting for transfers between devices, local(): lax.psum_scatter(term, 'tensor', scatter_dimension=0, tiled=True)[None]  16.5 us
    pallas_call x2, Pallas kernels, attention_backward(): pl.pallas_call(functools.partial(backward_kernel, halo_rows, group, rows,...  16.4 us
  transfers between devices with their start and end apart: 16, of which 14 were waited for; matrix products, arithmetic and copies ran while one was open for 15% of the time, Pallas kernels for 8%

profile of v2, /device:TPU:9, one launch (start us, length us, event | category | flops | bytes accessed | tf_op | source)
XLA Modules:
  0.0 429.0 jit_solution(8693006340319422091)
XLA Ops:
  14.0 96.4 %all-gather.5.cloned.1.call-done = bf16[1,512,5376]{2,1,0:T(8,128)(2,1)} async-done(((bf16[1,128,5376]{2,1,0:T(8,128)(2,1)}), bf16[1,512,5376]{2,1,0:T(8,128)(2,1)}) %all-gather.5.cloned.1.call-update) | async-done | bytes 5505040 | tf_op jit(solution)/shard_map/all_gather | solution.py:387
  110.5 4.4 %fusion.16 = bf16[512,48]{0,1:T(8,128)(2,1)S(1)} fusion(bf16[48,5376]{1,0:T(8,128)(2,1)S(1)} %bitcast.69, bf16[1,512,5376]{2,1,0:T(8,128)(2,1)} %all-gather.5.cloned.1.call-done), kind=kOutput, calls=%fused_computation.21 | convolution fusion | flops 264265728 | bytes 6070272 | tf_op jit(solution)/shard_map/ja,ma->jm/dot_general | solution.py:403
  114.9 5.2 %fusion.1 = f32[512,512]{1,0:T(8,128)S(1)} fusion(bf16[1,512,5376]{2,1,0:T(8,128)(2,1)S(1)} %copy-done.24, bf16[2,5376,512]{2,1,0:T(8,128)(2,1)} %refs_2_.1), kind=kOutput, calls=%fused_computation.2 | convolution fusion | flops 2818572288 | bytes 12058624 | tf_op jit(solution)/shard_map/dot_general | solution.py:409
  121.6 3.0 fusion.3
  125.9 4.0 rope_pair.1.refs_5_.refs_8_
  129.9 3.4 collective-permute-start
  133.2 2.1 collective-permute-start.1
  135.4 10.3 %fusion.10 = f32[512,1024]{1,0:T(8,128)S(1)} fusion(bf16[5376,1024]{1,0:T(8,128)(2,1)} %param.14, bf16[1,512,5376]{2,1,0:T(8,128)(2,1)} %all-gather.5.cloned.1.call-done), kind=kOutput, calls=%fused_computation.11 | convolution fusion | flops 5637144576 | bytes 18612224 | tf_op jit(solution)/shard_map/dot_general | solution.py:409
  147.5 6.0 %rope_query.1.refs_0_ = bf16[512,1024]{1,0:T(8,128)(2,1)} custom-call(f32[512,1024]{1,0:T(8,128)} %multiply_add_fusion.x_ref, f32[512,128]{1,0:T(8,128)} %get-tuple-element.55.cos_ref.refs_4_, f32[512,128]{1,0:T(8,128)} %get-tuple-element.56.sin_ref.refs_5_), custom_call_target="tpu_custom_call" | custom-call | flops 2097152 | bytes 3145728 | tf_op jit(solution)/shard_map/rope_query/pallas_call | solution.py:58
  155.3 12.4 %collective-permute-done.1.refs_4_.refs_7_ = bf16[2,512,512]{2,1,0:T(8,128)(2,1)S(1)} collective-permute-done((bf16[2,512,512]{2,1,0:T(8,128)(2,1)}, bf16[2,512,512]{2,1,0:T(8,128)(2,1)S(1)}, u32[]{:S(2)}, u32[]{:S(2)}) %collective-permute-start.1) | collective-permute-done | bytes 1048608 | tf_op jit(solution)/shard_map/ppermute | solution.py:22
  172.3 20.0 %attention_forward.1 = (bf16[8,1536,512]{2,1,0:T(8,128)(2,1)}, bf16[512,1024]{1,0:T(8,128)(2,1)S(1)}) custom-call(bf16[512,1024]{1,0:T(8,128)(2,1)S(1)} %copy-done.6, s32[1,512]{1,0:T(1,128)S(1)} %constant_dynamic-slice_fusion.refs_1_, s32[1536,1]{1,0:T(8,128)S(1)} %copy-done.23, bf16[2,512,512]{2,1,0:T(8,128)(2,1)S(1)} %collective-permute-done.refs_3_.refs_6_, ...), custom_call_target="tpu_custom_call" | custom-call | flops 3221225472 | bytes 41943040 | tf_op jit(solution)/shard_map/attention_forward/pallas_call | solution.py:140
  192.7 20.1 %all-gather.7.cloned.1.call-done = bf16[1,512,5376]{2,1,0:T(8,128)(2,1)} async-done(((bf16[1,128,5376]{2,1,0:T(8,128)(2,1)}), bf16[1,512,5376]{2,1,0:T(8,128)(2,1)}) %all-gather.7.cloned.1.call-update) | async-done | bytes 5505040 | tf_op jit(solution)/shard_map/all_gather | solution.py:388
  212.8 11.5 %fusion.62 = f32[512,1024]{1,0:T(8,128)S(1)} fusion(bf16[512,5376]{1,0:T(8,128)(2,1)} %bitcast.71, bf16[1024,5376]{1,0:T(8,128)(2,1)} %param.16), kind=kOutput, calls=%fused_computation.112 | convolution fusion | flops 5637144576 | bytes 18612224 | tf_op jit(solution)/shard_map/td,hd->th/dot_general | solution.py:436
  226.4 8.3 %attention_backward.2 = (bf16[512,512]{1,0:T(8,128)(2,1)S(1)}, bf16[2,1024,256]{2,1,0:T(8,128)(2,1)S(1)}, f32[2,512,256]{2,1,0:T(8,128)S(1)}) custom-call(bf16[512,1024]{1,0:T(8,128)(2,1)S(1)} %copy-done.7, bf16[512,1024]{1,0:T(8,128)(2,1)S(1)} %add_convert_fusion.refs_1_, bf16[512,1024]{1,0:T(8,128)(2,1)} %copy-done.1, ...), custom_call_target="tpu_custom_call" | custom-call | flops 3221225472 | bytes 20971520 | tf_op jit(solution)/shard_map/attention_backward/pallas_call | solution.py:213
  235.8 8.1 %attention_backward.3 = (bf16[512,512]{1,0:T(8,128)(2,1)S(1)}, bf16[2,1024,256]{2,1,0:T(8,128)(2,1)S(1)}, f32[2,512,256]{2,1,0:T(8,128)S(1)}) custom-call(bf16[512,1024]{1,0:T(8,128)(2,1)S(1)} %copy-done.7, bf16[512,1024]{1,0:T(8,128)(2,1)S(1)} %add_convert_fusion.refs_1_, bf16[512,1024]{1,0:T(8,128)(2,1)} %copy-done.1, ...), custom_call_target="tpu_custom_call" | custom-call | flops 3221225472 | bytes 20971520 | tf_op jit(solution)/shard_map/attention_backward/pallas_call | solution.py:213
  245.0 2.4 collective-permute-start.4
  248.8 12.7 %fusion.63.refs_0_ = f32[512,5376]{1,0:T(8,128)} fusion(bf16[512,1024]{1,0:T(8,128)(2,1)S(1)} %constant_dynamic-update-slice_fusion, bf16[5376,1024]{1,0:T(8,128)(2,1)} %param.14), kind=kOutput, calls=%fused_computation.113 | convolution fusion | flops 5637144576 | bytes 23068672 | tf_op jit(solution)/shard_map/th,dh->td/dot_general | solution.py:464
  266.9 2.6 combine_pairs.3
  270.7 6.2 %collective-permute-done.2.refs_0_ = bf16[2,512,256]{2,1,0:T(8,128)(2,1)S(1)} collective-permute-done((bf16[2,512,256]{2,1,0:T(8,128)(2,1)}, bf16[2,512,256]{2,1,0:T(8,128)(2,1)S(1)}, u32[]{:S(2)}, u32[]{:S(2)}) %collective-permute-start.2) | collective-permute-done | bytes 524320 | tf_op jit(solution)/shard_map/ppermute | solution.py:22
  276.8 2.7 collective-permute-done.3.refs_1_
  280.3 2.6 combine_pairs.2
  290.1 14.3 %input_term.1.refs_1_ = bf16[512,5376]{1,0:T(8,128)(2,1)} custom-call(f32[512,5376]{1,0:T(8,128)} %fusion.63.refs_0_, bf16[48,512]{1,0:T(8,128)(2,1)S(1)} %fusion.33.refs_1_, bf16[2,5376,512]{2,1,0:T(8,128)(2,1)} %refs_2_.1, bf16[48,5376]{1,0:T(8,128)(2,1)S(1)} %bitcast.70, bf16[512,256]{1,0:T(8,128)(2,1)S(1)} %copy-done.17, ...), custom_call_target="tpu_custom_call" | custom-call | flops 5637144576 | bytes 15414067 | tf_op jit(solution)/shard_map/input_term/pallas_call | solution.py:291
  311.0 3.1 collective-permute-start.7
  315.6 4.0 fusion.36
  319.6 3.4 fusion
  323.4 10.7 %collective-permute-start.8 = (bf16[1056,128]{1,0:T(8,128)(2,1)S(1)}, bf16[1056,128]{1,0:T(8,128)(2,1)S(1)}, u32[]{:S(2)}, u32[]{:S(2)}) collective-permute-start(bf16[1056,128]{1,0:T(8,128)(2,1)S(1)} %constant_dynamic-update-slice_fusion.2), channel_id=1, source_target_pairs={{0,4},{4,0},{8,12},{12,8},{1,5},{5,1},{9,13},{13,9},{2,6},{6,2},{1... | collective-permute-start | bytes 811016 | tf_op jit(solution)/shard_map/ppermute | solution.py:332
  335.3 7.8 %collective-permute-done.9 = bf16[1056,128]{1,0:T(8,128)(2,1)S(1)} collective-permute-done((bf16[1056,128]{1,0:T(8,128)(2,1)S(1)}, bf16[1056,128]{1,0:T(8,128)(2,1)S(1)}, u32[]{:S(2)}, u32[]{:S(2)}) %collective-permute-start.9) | collective-permute-done | bytes 270368 | tf_op jit(solution)/shard_map/ppermute | solution.py:332
  344.5 5.8 %collective-permute-done.10 = bf16[1056,128]{1,0:T(8,128)(2,1)S(1)} collective-permute-done((bf16[1056,128]{1,0:T(8,128)(2,1)S(1)}, bf16[1056,128]{1,0:T(8,128)(2,1)S(1)}, u32[]{:S(2)}, u32[]{:S(2)}) %collective-permute-start.10) | collective-permute-done | bytes 270368 | tf_op jit(solution)/shard_map/ppermute | solution.py:332
  350.6 5.0 %collective-permute-start.11 = (bf16[16,5376]{1,0:T(8,128)(2,1)S(1)}, bf16[16,5376]{1,0:T(8,128)(2,1)S(1)}, u32[]{:S(2)}, u32[]{:S(2)}) collective-permute-start(bf16[16,5376]{1,0:T(8,128)(2,1)S(1)} %reshape.60), channel_id=1, source_target_pairs={{0,1},{1,0},{2,3},{3,2},{4,5},{5,4},{6,7},{7,6},{8,9},{9,8},{10,11... | collective-permute-start | bytes 516104 | tf_op jit(solution)/shard_map/ppermute | solution.py:360
  355.7 14.8 %collective-permute-done.11 = bf16[16,5376]{1,0:T(8,128)(2,1)S(1)} collective-permute-done((bf16[16,5376]{1,0:T(8,128)(2,1)S(1)}, bf16[16,5376]{1,0:T(8,128)(2,1)S(1)}, u32[]{:S(2)}, u32[]{:S(2)}) %collective-permute-start.11) | collective-permute-done | bytes 172064 | tf_op jit(solution)/shard_map/ppermute | solution.py:360
  371.9 32.0 %collective-permute-done.12 = bf16[32,5376]{1,0:T(8,128)(2,1)S(1)} collective-permute-done((bf16[32,5376]{1,0:T(8,128)(2,1)S(1)}, bf16[32,5376]{1,0:T(8,128)(2,1)S(1)}, u32[]{:S(2)}, u32[]{:S(2)}) %collective-permute-start.12) | collective-permute-done | bytes 344096 | tf_op jit(solution)/shard_map/ppermute | solution.py:360
  405.9 16.5 %reduce-scatter.2.cloned.1.call-done = bf16[128,5376]{1,0:T(8,128)(2,1)} async-done(((bf16[512,5376]{1,0:T(8,128)(2,1)}), bf16[128,5376]{1,0:T(8,128)(2,1)}) %reduce-scatter.2.cloned.1.call-update) | async-done | bytes 1376272 | tf_op jit(solution)/shard_map/reduce_scatter | solution.py:489
  (152 shorter events, 52.7 us)
Async XLA Ops:
  7.2 217.2 %copy-start = (bf16[16,5376]{1,0:T(8,128)(2,1)S(1)}, bf16[16,5376]{1,0:T(8,128)(2,1)}, u32[]{:S(2)}) copy-start(bf16[16,5376]{1,0:T(8,128)(2,1)} %param.21) | copy-start | bytes 516100
  7.2 6.2 %copy-start.32 = (bf16[2,16,512]{2,1,0:T(8,128)(2,1)S(1)}, bf16[2,16,512]{2,1,0:T(8,128)(2,1)}, u32[]{:S(2)}) copy-start(bf16[2,16,512]{2,1,0:T(8,128)(2,1)} %param.19) | copy-start | bytes 98308
  7.2 103.3 %copy-start.19 = (bf16[3,16,5376]{2,1,0:T(8,128)(2,1)S(1)}, bf16[3,16,5376]{2,1,0:T(8,128)(2,1)}, u32[]{:S(2)}) copy-start(bf16[3,16,5376]{2,1,0:T(8,128)(2,1)} %param.17) | copy-start | bytes 1548292
  7.2 103.3 %all-gather.5.cloned.1.call-start = ((), (), s32[]{:S(2)}) async-start(), calls=%async_computation.2 | async-start | bytes 6881280 | tf_op jit(solution)/shard_map/all_gather | solution.py:387
  7.9 204.9 %all-gather.7.cloned.1.call-start = ((), (), s32[]{:S(2)}) async-start(), calls=%async_computation.3 | async-start | bytes 6881280 | tf_op jit(solution)/shard_map/all_gather | solution.py:388
  8.7 413.8 %reduce-scatter.2.cloned.1.call-start = ((), (), s32[]{:S(2)}) async-start(), calls=%async_computation.1 | async-start | bytes 6881280 | tf_op jit(solution)/shard_map/reduce_scatter | solution.py:489
  110.5 11.1 %slice-start = ((s8[11010048]{0:T(1024)(128)(4,1)}), s8[4194304]{0:T(1024)(128)(4,1)S(1)}, s32[]{:S(2)}) async-start(s8[11010048]{0:T(1024)(128)(4,1)} %bitcast.74), calls=%async_computation.4 | async-start | bytes 8388608
  114.9 6.7 %slice-start.1 = ((s8[11010048]{0:T(1024)(128)(4,1)}), s8[4194304]{0:T(1024)(128)(4,1)S(1)}, s32[]{:S(2)}) async-start(s8[11010048]{0:T(1024)(128)(4,1)} %bitcast.74), calls=%async_computation.5 | async-start | bytes 8388608
  114.9 6.7 %slice-start.2 = ((s8[11010048]{0:T(1024)(128)(4,1)}), s8[2621440]{0:T(1024)(128)(4,1)S(1)}, s32[]{:S(2)}) async-start(s8[11010048]{0:T(1024)(128)(4,1)} %bitcast.74), calls=%async_computation.6 | async-start | bytes 5242880
  129.9 15.8 %copy-start.31 = (bf16[16,1024]{1,0:T(8,128)(2,1)S(1)}, bf16[16,1024]{1,0:T(8,128)(2,1)}, u32[]{:S(2)}) copy-start(bf16[16,1024]{1,0:T(8,128)(2,1)} %param.18) | copy-start | bytes 98308
  129.9 25.4 %collective-permute-start = (bf16[2,512,512]{2,1,0:T(8,128)(2,1)}, bf16[2,512,512]{2,1,0:T(8,128)(2,1)S(1)}, u32[]{:S(2)}, u32[]{:S(2)}) collective-permute-start(bf16[2,512,512]{2,1,0:T(8,128)(2,1)} %rope_pair.1.refs_5_.refs_8_), channel_id=1, source_target_pairs={{0,8},{4,12},{1,9},{5,13},{2,10},{6,14},{3,11},{7,15},{16,24},{20,... | collective-permute-start | bytes 3145736 | tf_op jit(solution)/shard_map/ppermute | solution.py:22
  133.2 34.4 %collective-permute-start.1 = (bf16[2,512,512]{2,1,0:T(8,128)(2,1)}, bf16[2,512,512]{2,1,0:T(8,128)(2,1)S(1)}, u32[]{:S(2)}, u32[]{:S(2)}) collective-permute-start(bf16[2,512,512]{2,1,0:T(8,128)(2,1)} %rope_pair.1.refs_5_.refs_8_), channel_id=1, source_target_pairs={{0,4},{4,8},{8,12},{1,5},{5,9},{9,13},{2,6},{6,10},{10,14},{3,7},{... | collective-permute-start | bytes 3145736 | tf_op jit(solution)/shard_map/ppermute | solution.py:22
  145.7 23.0 %copy-start.5 = (bf16[2,512,512]{2,1,0:T(8,128)(2,1)S(1)}, bf16[2,512,512]{2,1,0:T(8,128)(2,1)}, u32[]{:S(2)}) copy-start(bf16[2,512,512]{2,1,0:T(8,128)(2,1)} %rope_pair.1.refs_5_.refs_8_) | copy-start | bytes 3145732
  147.5 44.9 %copy-start.30 = (bf16[16,1024]{1,0:T(8,128)(2,1)S(1)}, bf16[16,1024]{1,0:T(8,128)(2,1)}, u32[]{:S(2)}) copy-start(bf16[16,1024]{1,0:T(8,128)(2,1)} %param.20) | copy-start | bytes 98308
  155.3 37.0 %copy-start.8 = (bf16[2,512,512]{2,1,0:T(8,128)(2,1)}, bf16[2,512,512]{2,1,0:T(8,128)(2,1)S(1)}, u32[]{:S(2)}) copy-start(bf16[2,512,512]{2,1,0:T(8,128)(2,1)S(1)} %collective-permute-done.refs_3_.refs_6_) | copy-start | bytes 3145732
  192.3 32.0 %copy-start.1 = (bf16[512,1024]{1,0:T(8,128)(2,1)}, bf16[512,1024]{1,0:T(8,128)(2,1)S(1)}, u32[]{:S(2)}) copy-start(bf16[512,1024]{1,0:T(8,128)(2,1)S(1)} %get-tuple-element.25.refs_2_) | copy-start | bytes 3145732
  212.8 11.6 %copy-start.25 = (bf16[1,512,5376]{2,1,0:T(8,128)(2,1)S(1)}, bf16[1,512,5376]{2,1,0:T(8,128)(2,1)}, u32[]{:S(2)}) copy-start(bf16[1,512,5376]{2,1,0:T(8,128)(2,1)} %all-gather.7.cloned.1.call-done) | copy-start | bytes 16515076
  234.7 9.2 %copy-start.21 = (f32[2,512,256]{2,1,0:T(8,128)}, f32[2,512,256]{2,1,0:T(8,128)S(1)}, u32[]{:S(2)}) copy-start(f32[2,512,256]{2,1,0:T(8,128)S(1)} %get-tuple-element.29.own_ref) | copy-start | bytes 3145732
  245.0 20.9 %collective-permute-start.4 = (bf16[2,512,256]{2,1,0:T(8,128)(2,1)S(1)}, bf16[2,512,256]{2,1,0:T(8,128)(2,1)S(1)}, u32[]{:S(2)}, u32[]{:S(2)}) collective-permute-start(bf16[2,512,256]{2,1,0:T(8,128)(2,1)S(1)} %get-tuple-element.41), channel_id=1, source_target_pairs={{4,0},{8,4},{12,8},{5,1},{9,5},{13,9},{6,2},{10,6},{14,10},{7,3},{... | collective-permute-start | bytes 1572872 | tf_op jit(solution)/shard_map/ppermute | solution.py:22
  247.4 18.5 %collective-permute-start.5 = (bf16[2,512,256]{2,1,0:T(8,128)(2,1)S(1)}, bf16[2,512,256]{2,1,0:T(8,128)(2,1)S(1)}, u32[]{:S(2)}, u32[]{:S(2)}) collective-permute-start(bf16[2,512,256]{2,1,0:T(8,128)(2,1)S(1)} %get-tuple-element.40), channel_id=1, source_target_pairs={{8,0},{12,4},{9,1},{13,5},{10,2},{14,6},{11,3},{15,7},{24,16},{28,... | collective-permute-start | bytes 1572872 | tf_op jit(solution)/shard_map/ppermute | solution.py:22
  261.4 24.9 %copy-start.20 = (bf16[3,16,5376]{2,1,0:T(8,128)(2,1)S(1)}, bf16[3,16,5376]{2,1,0:T(8,128)(2,1)}, u32[]{:S(2)}) copy-start(bf16[3,16,5376]{2,1,0:T(8,128)(2,1)} %param.17) | copy-start | bytes 1548292
  261.7 15.1 %collective-permute-start.2 = (bf16[2,512,256]{2,1,0:T(8,128)(2,1)}, bf16[2,512,256]{2,1,0:T(8,128)(2,1)S(1)}, u32[]{:S(2)}, u32[]{:S(2)}) collective-permute-start(bf16[2,512,256]{2,1,0:T(8,128)(2,1)} %get-tuple-element.39), channel_id=1, source_target_pairs={{4,0},{8,4},{12,8},{5,1},{9,5},{13,9},{6,2},{10,6},{14,10},{7,3},{... | collective-permute-start | bytes 1572872 | tf_op jit(solution)/shard_map/ppermute | solution.py:22
  263.6 15.9 %collective-permute-start.3 = (bf16[2,512,256]{2,1,0:T(8,128)(2,1)S(1)}, bf16[2,512,256]{2,1,0:T(8,128)(2,1)S(1)}, u32[]{:S(2)}, u32[]{:S(2)}) collective-permute-start(bf16[2,512,256]{2,1,0:T(8,128)(2,1)S(1)} %get-tuple-element.38), channel_id=1, source_target_pairs={{8,0},{12,4},{9,1},{13,5},{10,2},{14,6},{11,3},{15,7},{24,16},{28,... | collective-permute-start | bytes 1572872 | tf_op jit(solution)/shard_map/ppermute | solution.py:22
  304.5 4.7 %copy-start.12 = (bf16[512,256]{1,0:T(8,128)(2,1)S(1)}, bf16[512,256]{1,0:T(8,128)(2,1)}, u32[]{:S(2)}) copy-start(bf16[512,256]{1,0:T(8,128)(2,1)} %get-tuple-element.36.refs_7_) | copy-start | bytes 786436
  304.5 9.7 %copy-start.2 = (bf16[512,1024]{1,0:T(8,128)(2,1)S(1)}, bf16[512,1024]{1,0:T(8,128)(2,1)}, u32[]{:S(2)}) copy-start(bf16[512,1024]{1,0:T(8,128)(2,1)} %copy-done.1) | copy-start | bytes 3145732
  306.6 3.7 collective-permute-start.6
  311.0 4.6 %collective-permute-start.7 = (bf16[16,512]{1,0:T(8,128)(2,1)S(1)}, bf16[16,512]{1,0:T(8,128)(2,1)S(1)}, u32[]{:S(2)}, u32[]{:S(2)}) collective-permute-start(bf16[16,512]{1,0:T(8,128)(2,1)S(1)} %broadcast_select_fusion.5), channel_id=1, source_target_pairs={{0,1},{1,0},{2,3},{3,2},{4,5},{5,4},{6,7},{7,6},{8,9},{9,8},{10,11... | collective-permute-start | bytes 49160 | tf_op jit(solution)/shard_map/ppermute | solution.py:348
  323.4 11.8 %collective-permute-start.8 = (bf16[1056,128]{1,0:T(8,128)(2,1)S(1)}, bf16[1056,128]{1,0:T(8,128)(2,1)S(1)}, u32[]{:S(2)}, u32[]{:S(2)}) collective-permute-start(bf16[1056,128]{1,0:T(8,128)(2,1)S(1)} %constant_dynamic-update-slice_fusion.2), channel_id=1, source_target_pairs={{0,4},{4,0},{8,12},{12,8},{1,5},{5,1},{9,13},{13,9},{2,6},{6,2},{1... | collective-permute-start | bytes 811016 | tf_op jit(solution)/shard_map/ppermute | solution.py:332
  335.3 7.9 %collective-permute-start.9 = (bf16[1056,128]{1,0:T(8,128)(2,1)S(1)}, bf16[1056,128]{1,0:T(8,128)(2,1)S(1)}, u32[]{:S(2)}, u32[]{:S(2)}) collective-permute-start(bf16[1056,128]{1,0:T(8,128)(2,1)S(1)} %add_convert_fusion.3), channel_id=1, source_target_pairs={{0,8},{4,12},{8,0},{12,4},{1,9},{5,13},{9,1},{13,5},{2,10},{6,14},... | collective-permute-start | bytes 811016 | tf_op jit(solution)/shard_map/ppermute | solution.py:332
  343.2 7.0 %collective-permute-start.10 = (bf16[1056,128]{1,0:T(8,128)(2,1)S(1)}, bf16[1056,128]{1,0:T(8,128)(2,1)S(1)}, u32[]{:S(2)}, u32[]{:S(2)}) collective-permute-start(bf16[1056,128]{1,0:T(8,128)(2,1)S(1)} %add_convert_fusion.2), channel_id=1, source_target_pairs={{0,16},{16,0},{1,17},{17,1},{2,18},{18,2},{3,19},{19,3},{4,20},{20... | collective-permute-start | bytes 811016 | tf_op jit(solution)/shard_map/ppermute | solution.py:332
  350.6 19.9 %collective-permute-start.11 = (bf16[16,5376]{1,0:T(8,128)(2,1)S(1)}, bf16[16,5376]{1,0:T(8,128)(2,1)S(1)}, u32[]{:S(2)}, u32[]{:S(2)}) collective-permute-start(bf16[16,5376]{1,0:T(8,128)(2,1)S(1)} %reshape.60), channel_id=1, source_target_pairs={{0,1},{1,0},{2,3},{3,2},{4,5},{5,4},{6,7},{7,6},{8,9},{9,8},{10,11... | collective-permute-start | bytes 516104 | tf_op jit(solution)/shard_map/ppermute | solution.py:360
  370.6 33.4 %collective-permute-start.12 = (bf16[32,5376]{1,0:T(8,128)(2,1)S(1)}, bf16[32,5376]{1,0:T(8,128)(2,1)S(1)}, u32[]{:S(2)}, u32[]{:S(2)}) collective-permute-start(bf16[32,5376]{1,0:T(8,128)(2,1)S(1)} %pad_maximum_fusion), channel_id=1, source_target_pairs={{0,2},{1,3},{2,0},{3,1},{4,6},{5,7},{6,4},{7,5},{8,10},{9,11},{10,... | collective-permute-start | bytes 1032200 | tf_op jit(solution)/shard_map/ppermute | solution.py:360
  (21 other events, 38.9 us)
Sparse Core Ops, SparseCore 0:
  9.6 100.8 all-gather.4
  112.0 100.7 all-gather.6
  304.6 117.7 reduce-scatter.1

commit v3 on v1

--- a/solution.py
+++ b/solution.py
@@ -167,7 +167,8 @@
 def backward_kernel(halo_rows, group, rows, n_pairs, *refs):
     q_ref, g_ref, att_ref, w_ref, cos_ref, sin_ref = refs[:6]
     pair_refs = refs[6 : 6 + n_pairs]
-    dq_ref, halo_ref, own_ref, k_buf, v_buf, dk_buf, dv_buf = refs[6 + n_pairs :]
+    dq_ref, *halo_refs = refs[6 + n_pairs : 6 + 2 * n_pairs]
+    own_ref, k_buf, v_buf, dk_buf, dv_buf = refs[6 + 2 * n_pairs :]
     keys = k_buf.shape[0]
     count = q_ref.shape[0]
     half = HEAD_SIZE // 2
@@ -188,9 +189,9 @@
             dk_buf[lo:hi] += dot(ds, q_ref[here, cols], (((1,), (0,)), ((), ())))
             dq = dot(k_buf[lo:hi], ds, TN).T
             dq_ref[here, cols] = turned(dq, cos_ref[here], -sin_ref[here]).astype(bf16)
-    if halo_rows:
-        halo_ref[0] = dk_buf[:halo_rows].astype(bf16)
-        halo_ref[1] = dv_buf[:halo_rows].astype(bf16)
+    for at, halo_ref in enumerate(halo_refs):
+        halo_ref[0] = dk_buf[at * count : (at + 1) * count].astype(bf16)
+        halo_ref[1] = dv_buf[at * count : (at + 1) * count].astype(bf16)
     own_ref[0] = dk_buf[halo_rows:]
     own_ref[1] = dv_buf[halo_rows:]
 
@@ -217,16 +218,10 @@
             table,
         ]
         + [pair_spec] * len(pairs),
-        out_specs=[
-            q_spec,
-            pl.BlockSpec((2, halo_rows, HEAD_SIZE), lambda h: (0, 0, h)),
-            pair_spec,
-        ],
-        out_shape=[
-            jax.ShapeDtypeStruct((count, q_cols), bf16),
-            jax.ShapeDtypeStruct((2, halo_rows, kv_cols), bf16),
-            jax.ShapeDtypeStruct((2, count, kv_cols), f32),
-        ],
+        out_specs=[q_spec] + [pair_spec] * len(pairs),
+        out_shape=[jax.ShapeDtypeStruct((count, q_cols), bf16)]
+        + [jax.ShapeDtypeStruct((2, count, kv_cols), bf16)] * (len(pairs) - 1)
+        + [jax.ShapeDtypeStruct((2, count, kv_cols), f32)],
         scratch_shapes=[
             pltpu.VMEM((keys, HEAD_SIZE), bf16),
             pltpu.VMEM((keys, HEAD_SIZE), bf16),
@@ -241,68 +236,82 @@
     )(queries, grads, attended, weights, cosine, sine, *pairs)
 
 
-def combine_kernel(own_ref, cos_ref, sin_ref, *refs):
-    dk_ref, dv_ref = refs[-2:]
-    dk, dv = own_ref[0], own_ref[1]
-    for ref in refs[:-2]:
-        dk = dk + ref[0].astype(f32)
-        dv = dv + ref[1].astype(f32)
-    dk_ref[...] = turned(dk, cos_ref[...], -sin_ref[...]).astype(bf16)
-    dv_ref[...] = dv.astype(bf16)
-
-
-def combine(own, shares, cosine, sine):
-    _, count, kv_cols = own.shape
-    pair_spec = pl.BlockSpec((2, count, HEAD_SIZE), lambda h: (0, 0, h))
-    table = pl.BlockSpec((count, HEAD_SIZE), lambda h: (0, 0))
-    out = pl.BlockSpec((count, HEAD_SIZE), lambda h: (0, h))
-    return pl.pallas_call(
-        combine_kernel,
-        grid=(kv_cols // HEAD_SIZE,),
-        in_specs=[pair_spec, table, table] + [pair_spec] * len(shares),
-        out_specs=[out, out],
-        out_shape=[jax.ShapeDtypeStruct((count, kv_cols), bf16)] * 2,
-        name="combine_pairs",
-        cost_estimate=pl.CostEstimate(flops=8 * count * kv_cols, bytes_accessed=20 * count * kv_cols, transcendentals=0),
-    )(own, cosine, sine, *shares)
-
-
-def term_kernel(first_ref, dk_ref, dv_ref, hid_ref, kv_ref, down_ref, out_ref):
-    total = first_ref[...] + dot(dk_ref[...], kv_ref[0], NT)
-    total = total + dot(dv_ref[...], kv_ref[1], NT)
-    total = total + dot(hid_ref[...], down_ref[...], (((1,), (0,)), ((), ())))
-    out_ref[...] = total.astype(bf16)
-
-
-def term_sum(first, dk, dv, hidden, kv_weight, down):
+def term_kernel(*refs):
+    first_ref, low_ref, kv_ref, down_ref, up_ref, cos_ref, sin_ref, own_ref = refs[:8]
+    share_refs = refs[8:-4]
+    out_ref, dk_ref, dv_ref, hid_ref = refs[-4:]
+    rank = low_ref.shape[0]
+
+    @pl.when(pl.program_id(0) == 0)
+    def _():
+        for h in range(dk_ref.shape[1] // HEAD_SIZE):
+            cols = slice(h * HEAD_SIZE, (h + 1) * HEAD_SIZE)
+            dk, dv = own_ref[0, :, cols], own_ref[1, :, cols]
+            for ref in share_refs:
+                dk = dk + ref[0, :, cols].astype(f32)
+                dv = dv + ref[1, :, cols].astype(f32)
+            dk_ref[:, cols] = turned(dk, cos_ref[...], -sin_ref[...]).astype(bf16)
+            dv_ref[:, cols] = dv.astype(bf16)
+        hid_ref[:rank] = low_ref[...].astype(bf16)
+        hid_ref[rank : 2 * rank] = (adapter_scale * dot(up_ref[0], dk_ref[...], NT)).astype(bf16)
+        hid_ref[2 * rank :] = (adapter_scale * dot(up_ref[1], dv_ref[...], NT)).astype(bf16)
+
+    out_ref[...] = (
+        dot(dk_ref[...], kv_ref[0], NT)
+        + dot(dv_ref[...], kv_ref[1], NT)
+        + dot(hid_ref[...], down_ref[...], TN)
+        + first_ref[...].astype(f32)
+    ).astype(bf16)
+
+
+def term_sum(first, low, kv_weight, down, up, cosine, sine, own, shares):
     count, width = first.shape
+    kv_cols = own.shape[2]
+    rank = low.shape[0]
     tile = next(t for t in (768, 384, 256, 128, width) if width % t == 0)
-    whole = lambda a: pl.BlockSpec(a.shape, lambda i: (0, 0))
-    block = pl.BlockSpec((count, tile), lambda i: (0, i))
+    whole = lambda a: pl.BlockSpec(a.shape, lambda i: (0,) * len(a.shape))
+    grad = jax.ShapeDtypeStruct((count, kv_cols), bf16)
+    hidden = jax.ShapeDtypeStruct((3 * rank, count), bf16)
     return pl.pallas_call(
         term_kernel,
         grid=(width // tile,),
         in_specs=[
-            block,
-            whole(dk),
-            whole(dv),
+            pl.BlockSpec((count, tile), lambda i: (0, i)),
+            whole(low),
+            pl.BlockSpec((2, tile, kv_cols), lambda i: (0, i, 0)),
+            pl.BlockSpec((down.shape[0], tile), lambda i: (0, i)),
+            whole(up),
+            whole(cosine),
+            whole(sine),
+            whole(own),
+        ]
+        + [whole(a) for a in shares],
+        out_specs=[
+            pl.BlockSpec((count, tile), lambda i: (0, i)),
+            whole(grad),
+            whole(grad),
             whole(hidden),
-            pl.BlockSpec((2, tile, kv_weight.shape[2]), lambda i: (0, i, 0)),
-            pl.BlockSpec((down.shape[0], tile), lambda i: (0, i)),
         ],
-        out_specs=block,
-        out_shape=jax.ShapeDtypeStruct((count, width), bf16),
+        out_shape=[jax.ShapeDtypeStruct((count, width), bf16), grad, grad, hidden],
         compiler_params=pltpu.CompilerParams(vmem_limit_bytes=48 << 20),
         name="input_term",
         cost_estimate=pl.CostEstimate(
-            flops=4 * count * width * dk.shape[1], bytes_accessed=28 << 20, transcendentals=0
+            flops=4 * count * width * kv_cols, bytes_accessed=28 << 20, transcendentals=0
         ),
-    )(first, dk, dv, hidden, kv_weight, down)
-
-
-def shifted(block, axis, distance):
-    n = lax.axis_size(axis)
-    return lax.ppermute(block, axis, [(i, (i + distance) % n) for i in range(n)])
+    )(first, low, kv_weight, down, up, cosine, sine, own, *shares)
+
+
+def after(block, *others):
+    anywhere = pl.BlockSpec(memory_space=pl.ANY)
+    return pl.pallas_call(
+        lambda *refs: None,
+        in_specs=[anywhere] * (1 + len(others)),
+        out_specs=anywhere,
+        out_shape=jax.ShapeDtypeStruct(block.shape, block.dtype),
+        input_output_aliases={0: 0},
+        name="after",
+        cost_estimate=pl.CostEstimate(flops=0, bytes_accessed=0, transcendentals=0),
+    )(block, *others)
 
 
 def summed_pairwise(block, axis):
@@ -319,19 +328,31 @@
 
 def scattered_rows(block, axis):
     n, me = lax.axis_size(axis), lax.axis_index(axis)
-    blocks = block.reshape(n, block.shape[0] // n, block.shape[1])
-    total = lax.dynamic_index_in_dim(blocks, me, 0, keepdims=False).astype(f32)
-    for d in range(1, n):
-        part = lax.dynamic_index_in_dim(blocks, (me + d) % n, 0, keepdims=False)
-        total = total + shifted(part, axis, d).astype(f32)
-    return total
+    if n & (n - 1):
+        return lax.psum_scatter(block, axis, scatter_dimension=0, tiled=True)
+    step = n // 2
+    while step:
+        halves = block.reshape(2, block.shape[0] // 2, block.shape[1])
+        bit = (me // step) % 2
+        keep = jnp.where(bit == 0, halves[0], halves[1])
+        give = jnp.where(bit == 0, halves[1], halves[0])
+        got = lax.ppermute(give, axis, [(i, i ^ step) for i in range(n)])
+        block = (keep.astype(f32) + got.astype(f32)).astype(bf16)
+        step //= 2
+    return block
 
 
 def gathered_rows(block, axis):
     n, me = lax.axis_size(axis), lax.axis_index(axis)
-    parts = jnp.stack([block] + [shifted(block, axis, d) for d in range(1, n)], 0)
-    order = (me - jnp.arange(n)) % n
-    return jnp.take(parts, order, axis=0).reshape(n * block.shape[0], block.shape[1])
+    if n & (n - 1):
+        return lax.all_gather(block, axis, axis=0, tiled=True)
+    step = 1
+    while step < n:
+        got = lax.ppermute(block, axis, [(i, i ^ step) for i in range(n)])
+        first = (me // step) % 2 == 0
+        block = jnp.concatenate([jnp.where(first, block, got), jnp.where(first, got, block)], 0)
+        step *= 2
+    return block
 
 
 def local(
@@ -406,55 +427,52 @@
         jnp.einsum("td,hd->th", incoming, output_weight, preferred_element_type=f32)
         + jnp.dot(up_gradient, adapter_down_output, preferred_element_type=f32)
     ).astype(bf16)
-    grad_query, grad_halo, grad_own = attention_backward(
+    grad_query, *grad_halos, grad_own = attention_backward(
         queries, grad_attended, attended, weights, pairs, cosine, sine
     )
     shares = [
-        passed_along(
-            lax.slice_in_dim(
-                grad_halo,
-                (halo_count - distance) * shard_len,
-                (halo_count - distance + 1) * shard_len,
-                axis=1,
-            ),
-            "context",
-            -distance,
-        )
+        passed_along(grad_halos[halo_count - distance], "context", -distance)
         for distance in range(1, halo_count + 1)
     ]
-    first_term = jnp.einsum("th,dh->td", grad_query, query_weight, preferred_element_type=f32)
-    query_hidden = jnp.einsum(
-        "kn,pn->kp", grad_query, adapter_up_query, preferred_element_type=f32
-    )
-    grad_key, grad_value = combine(grad_own, shares, cosine, sine)
-    key_hidden = jnp.einsum(
-        "kn,pn->kp", grad_key, adapter_up_key_value[0], preferred_element_type=f32
-    )
-    value_hidden = jnp.einsum(
-        "kn,pn->kp", grad_value, adapter_up_key_value[1], preferred_element_type=f32
-    )
-    hidden = (
-        adapter_scale * jnp.concatenate([query_hidden, key_hidden, value_hidden], 1)
-    ).astype(bf16)
-    term = term_sum(first_term, grad_key, grad_value, hidden, key_value_weight, down_all)
+    first_term = jnp.einsum(
+        "th,dh->td", grad_query, query_weight, preferred_element_type=f32
+    ).astype(bf16)
+    query_low = adapter_scale * jnp.einsum(
+        "pn,kn->pk", adapter_up_query, grad_query, preferred_element_type=f32
+    )
+    term, grad_key, grad_value, hidden = term_sum(
+        first_term,
+        query_low,
+        key_value_weight,
+        down_all,
+        adapter_up_key_value,
+        cosine,
+        sine,
+        grad_own,
+        shares,
+    )
     grad_input = lax.psum_scatter(term, "tensor", scatter_dimension=0, tiled=True)[None]
 
     def over_tokens(low, grads):
         return jnp.einsum("tr,th->rh", low, grads, preferred_element_type=f32)
 
-    wide = jnp.concatenate(
-        [over_tokens(hidden, gathered), adapter_scale * over_tokens(factor, incoming)], 0
+    low_rows = jnp.concatenate([hidden, (adapter_scale * factor.astype(f32)).astype(bf16).T], 0)
+    low_rows = after(low_rows, term)
+    mine_low = scattered_rows(low_rows, "tensor")
+    row_at = lax.axis_index("tensor") * mine_low.shape[0] + jnp.arange(mine_low.shape[0])
+    from_tokens = (row_at < 3 * rank)[:, None]
+    zero = jnp.zeros_like(mine_low)
+    mine = (
+        jnp.dot(jnp.where(from_tokens, mine_low, zero), gathered, preferred_element_type=f32)
+        + jnp.dot(jnp.where(from_tokens, zero, mine_low), incoming, preferred_element_type=f32)
     ).astype(bf16)
     narrow = jnp.concatenate(
-        [
-            adapter_scale * over_tokens(adapted_query, grad_query),
-            adapter_scale * over_tokens(adapted_key, grad_key),
-            adapter_scale * over_tokens(adapted_value, grad_value),
-            over_tokens(up_gradient, attended),
-        ],
+        [adapter_scale * over_tokens(adapted_query, grad_query)]
+        + [adapter_scale * over_tokens(adapted_key, grad_key)]
+        + [adapter_scale * over_tokens(adapted_value, grad_value)]
+        + [over_tokens(up_gradient, attended)],
         1,
     ).astype(bf16)
-    mine = scattered_rows(wide, "tensor").astype(bf16)
     size = mine.size
     flat = jnp.concatenate([mine.reshape(-1, 128), narrow.reshape(-1, 128)], 0)
     flat = summed_pairwise(summed_pairwise(flat, "context"), "dp")

time: 436 us -> 416 us (0.954)
  waiting for transfers between devices: 251 us -> 225 us
  starting transfers between devices: 21.9 us -> 38.4 us
  local copies, waits for them, and re-layouts: 15.2 us -> 9.59 us
    reduce_scatter x1, waiting for transfers between devices: 32.2 us -> 16.1 us  [local(): lax.psum_scatter(term, 'tensor', scatter_dimension=0, tiled=True)[None]]
    ppermute x3, starting transfers between devices: 1.23 us -> 13.3 us  [summed_pairwise(): other = lax.ppermute(block, axis, [(i, i ^ step) for i in range(n)])]
    ppermute x4, waiting for transfers between devices: 34.7 us -> 27.2 us  [passed_along(): return lax.ppermute(block, axis, route)]
    dot_general x6 -> x4, matrix products: 8.1 us -> 0.86 us  [over_tokens(): return jnp.einsum('tr,th->rh', low, grads, preferred_element_type=f32)]
    ppermute x6 -> x4, starting transfers between devices: 10.7 us -> 15.8 us  [the longest x2 10.5 us: gathered_rows(): got = lax.ppermute(block, axis, [(i, i ^ step) for i in range(n)])]
    dot_general x3, matrix products: 2.94 us -> 7.59 us  [the longest x1 3.79 us: local(): jnp.dot(jnp.where(from_tokens, mine_low, zero), gathered, preferred_eleme...]
    ppermute x6 -> x4, waiting for transfers between devices: 49.7 us -> 48.1 us  [the longest x2 45.8 us: gathered_rows(): got = lax.ppermute(block, axis, [(i, i ^ step) for i in range(n)])]
  transfers between devices with their start and end apart: 16 -> 14, of which waited for: 16 -> 14; matrix products, arithmetic and copies ran while one was open for 13% -> 14% of each run, Pallas kernels for 7% -> 7%
where the time goes in v3:
time: 416 us; the launch traced here: 415 us
  waiting for transfers between devices  225 us (54%)
  matrix products  61.6 us (15%)
  Pallas kernels  60.4 us (15%)
  starting transfers between devices  38.4 us (9%)
  between operations  14.1 us (3%)
  local copies, waits for them, and re-layouts  9.59 us (2%)
  other arithmetic  6.14 us (1%)
    all_gather x1, waiting for transfers between devices, local(): gathered = lax.all_gather(tokens[0], 'tensor', axis=0, tiled=True)  97.1 us
    ppermute x2, waiting for transfers between devices, gathered_rows(): got = lax.ppermute(block, axis, [(i, i ^ step) for i in range(n)])  45.8 us
    ppermute x4, waiting for transfers between devices, passed_along(): return lax.ppermute(block, axis, route)  27.2 us
    pallas_call x1, Pallas kernels, attention_forward(): pl.pallas_call(functools.partial(forward_kernel, halo_rows, group, rows),...  20.6 us
    all_gather x1, waiting for transfers between devices, local(): incoming = lax.all_gather(output_gradient[0], 'tensor', axis=0, tiled=True)  20.5 us
    dot_general x3, matrix products, projected(): jnp.dot(gathered, weight, preferred_element_type=f32)  18.5 us
    reduce_scatter x1, waiting for transfers between devices, local(): lax.psum_scatter(term, 'tensor', scatter_dimension=0, tiled=True)[None]  16.1 us
    pallas_call x1, Pallas kernels, term_sum(): pl.pallas_call(term_kernel, grid=(width // tile,), in_specs=[pl.BlockSpec...  14.9 us
  transfers between devices with their start and end apart: 14, of which 14 were waited for; matrix products, arithmetic and copies ran while one was open for 14% of the time, Pallas kernels for 7%

profile of v3, /device:TPU:9, one launch (start us, length us, event | category | flops | bytes accessed | tf_op | source)
XLA Modules:
  0.0 415.3 jit_solution(2554627988608408581)
XLA Ops:
  13.4 97.1 %all-gather.5.cloned.1.call-done = bf16[1,512,5376]{2,1,0:T(8,128)(2,1)} async-done(((bf16[1,128,5376]{2,1,0:T(8,128)(2,1)}), bf16[1,512,5376]{2,1,0:T(8,128)(2,1)}) %all-gather.5.cloned.1.call-update) | async-done | bytes 5505040 | tf_op jit(solution)/shard_map/all_gather | solution.py:378
  110.5 4.4 %fusion.16 = bf16[512,48]{0,1:T(8,128)(2,1)S(1)} fusion(bf16[48,5376]{1,0:T(8,128)(2,1)S(1)} %bitcast.59, bf16[1,512,5376]{2,1,0:T(8,128)(2,1)} %all-gather.5.cloned.1.call-done), kind=kOutput, calls=%fused_computation.22 | convolution fusion | flops 264265728 | bytes 6070272 | tf_op jit(solution)/shard_map/ja,ma->jm/dot_general | solution.py:394
  114.9 5.2 %fusion.3 = f32[512,512]{1,0:T(8,128)S(1)} fusion(bf16[1,512,5376]{2,1,0:T(8,128)(2,1)S(1)} %copy-done.12, bf16[2,5376,512]{2,1,0:T(8,128)(2,1)} %refs_2_.1), kind=kOutput, calls=%fused_computation.5 | convolution fusion | flops 2818572288 | bytes 12058624 | tf_op jit(solution)/shard_map/dot_general | solution.py:400
  121.5 3.0 fusion.1
  125.8 4.0 rope_pair.1.refs_5_.refs_8_
  129.8 3.4 collective-permute-start
  133.2 2.1 collective-permute-start.1
  135.3 10.3 %fusion.10 = f32[512,1024]{1,0:T(8,128)S(1)} fusion(bf16[5376,1024]{1,0:T(8,128)(2,1)} %param.14, bf16[1,512,5376]{2,1,0:T(8,128)(2,1)} %all-gather.5.cloned.1.call-done), kind=kOutput, calls=%fused_computation.12 | convolution fusion | flops 5637144576 | bytes 18612224 | tf_op jit(solution)/shard_map/dot_general | solution.py:400
  147.4 6.0 %rope_query.1.refs_0_ = bf16[512,1024]{1,0:T(8,128)(2,1)} custom-call(f32[512,1024]{1,0:T(8,128)} %multiply_add_fusion.x_ref, f32[512,128]{1,0:T(8,128)} %get-tuple-element.45.cos_ref.refs_4_.refs_5_, f32[512,128]{1,0:T(8,128)} %get-tuple-element.46.sin_ref.refs_5_.refs_6_), custom_call_target="tpu_custom_call" | custom-call | flops 2097152 | bytes 3145728 | tf_op jit(solution)/shard_map/rope_query/pallas_call | solution.py:58
  153.5 1.8 collective-permute-done.refs_3_.refs_6_
  156.3 11.4 %collective-permute-done.1.refs_4_.refs_7_ = bf16[2,512,512]{2,1,0:T(8,128)(2,1)} collective-permute-done((bf16[2,512,512]{2,1,0:T(8,128)(2,1)}, bf16[2,512,512]{2,1,0:T(8,128)(2,1)}, u32[]{:S(2)}, u32[]{:S(2)}) %collective-permute-start.1) | collective-permute-done | bytes 1048608 | tf_op jit(solution)/shard_map/ppermute | solution.py:22
  171.3 20.6 %attention_forward.1 = (bf16[8,1536,512]{2,1,0:T(8,128)(2,1)}, bf16[512,1024]{1,0:T(8,128)(2,1)S(1)}) custom-call(bf16[512,1024]{1,0:T(8,128)(2,1)S(1)} %copy-done.6, s32[1,512]{1,0:T(1,128)S(1)} %constant_dynamic-slice_fusion.refs_1_, s32[1536,1]{1,0:T(8,128)S(1)} %copy-done.8, bf16[2,512,512]{2,1,0:T(8,128)(2,1)S(1)} %copy-done.11, ...), custom_call_target="tpu_custom_call" | custom-call | flops 3221225472 | bytes 41943040 | tf_op jit(solution)/shard_map/attention_forward/pallas_call | solution.py:140
  192.2 20.5 %all-gather.7.cloned.1.call-done = bf16[1,512,5376]{2,1,0:T(8,128)(2,1)} async-done(((bf16[1,128,5376]{2,1,0:T(8,128)(2,1)}), bf16[1,512,5376]{2,1,0:T(8,128)(2,1)}) %all-gather.7.cloned.1.call-update) | async-done | bytes 5505040 | tf_op jit(solution)/shard_map/all_gather | solution.py:379
  212.8 11.5 %fusion.46 = f32[512,1024]{1,0:T(8,128)S(1)} fusion(bf16[512,5376]{1,0:T(8,128)(2,1)} %bitcast.61, bf16[1024,5376]{1,0:T(8,128)(2,1)} %param.16), kind=kOutput, calls=%fused_computation.89 | convolution fusion | flops 5637144576 | bytes 18612224 | tf_op jit(solution)/shard_map/td,hd->th/dot_general | solution.py:427
  226.7 14.8 %attention_backward.1 = (bf16[512,1024]{1,0:T(8,128)(2,1)S(1)}, bf16[2,512,512]{2,1,0:T(8,128)(2,1)S(1)}, bf16[2,512,512]{2,1,0:T(8,128)(2,1)S(1)}, f32[2,512,512]{2,1,0:T(8,128)}) custom-call(bf16[512,1024]{1,0:T(8,128)(2,1)S(1)} %copy-done.7, bf16[512,1024]{1,0:T(8,128)(2,1)S(1)} %add_convert_fusion.refs_1_, bf16[512,1024]{1,0:T(8,128)(2,1)} %copy-done.3, ...), custom_call_target="tpu_custom_call" | custom-call | flops 6442450944 | bytes 20971520 | tf_op jit(solution)/shard_map/attention_backward/pallas_call | solution.py:209
  241.8 2.4 collective-permute-start.2
  245.6 11.8 %convolution_convert_fusion.refs_0_ = bf16[512,5376]{1,0:T(8,128)(2,1)} fusion(bf16[512,1024]{1,0:T(8,128)(2,1)S(1)} %get-tuple-element.25, bf16[5376,1024]{1,0:T(8,128)(2,1)} %param.14), kind=kOutput, calls=%fused_computation | convolution fusion | flops 5639897088 | bytes 17563648 | tf_op jit(solution)/shard_map/th,dh->td/dot_general | solution.py:437
  257.4 10.0 %collective-permute-done.2.refs_8_ = bf16[2,512,512]{2,1,0:T(8,128)(2,1)S(1)} collective-permute-done((bf16[2,512,512]{2,1,0:T(8,128)(2,1)S(1)}, bf16[2,512,512]{2,1,0:T(8,128)(2,1)S(1)}, u32[]{:S(2)}, u32[]{:S(2)}) %collective-permute-start.2) | collective-permute-done | bytes 1048608 | tf_op jit(solution)/shard_map/ppermute | solution.py:22
  267.5 4.0 collective-permute-done.3.refs_9_
  271.4 14.9 %input_term.1 = (bf16[512,5376]{1,0:T(8,128)(2,1)}, bf16[512,512]{1,0:T(8,128)(2,1)S(1)}, bf16[512,512]{1,0:T(8,128)(2,1)S(1)}, bf16[48,512]{1,0:T(8,128)(2,1)S(1)}) custom-call(bf16[512,5376]{1,0:T(8,128)(2,1)} %convolution_convert_fusion.refs_0_, f32[16,512]{1,0:T(8,128)S(1)} %fusion.20.refs_1_, bf16[2,5376,512]{2,1,0:T(8,128)(2,1)} %refs_2_.1, ...), custom_call_target="tpu_custom_call" | custom-call | flops 5637144576 | bytes 29360128 | tf_op jit(solution)/shard_map/input_term/pallas_call | solution.py:275
  288.1 2.1 collective-permute-start.4
  292.5 3.2 collective-permute-start.5
  296.9 3.4 fusion.28
  300.3 3.8 fusion
  304.4 12.0 %collective-permute-start.6 = (bf16[1056,128]{1,0:T(8,128)(2,1)S(1)}, bf16[1056,128]{1,0:T(8,128)(2,1)S(1)}, u32[]{:S(2)}, u32[]{:S(2)}) collective-permute-start(bf16[1056,128]{1,0:T(8,128)(2,1)S(1)} %constant_dynamic-update-slice_fusion), channel_id=1, source_target_pairs={{0,4},{4,0},{8,12},{12,8},{1,5},{5,1},{9,13},{13,9},{2,6},{6,2},{1... | collective-permute-start | bytes 811016 | tf_op jit(solution)/shard_map/ppermute | solution.py:323
  317.8 7.8 %collective-permute-done.7 = bf16[1056,128]{1,0:T(8,128)(2,1)S(1)} collective-permute-done((bf16[1056,128]{1,0:T(8,128)(2,1)S(1)}, bf16[1056,128]{1,0:T(8,128)(2,1)S(1)}, u32[]{:S(2)}, u32[]{:S(2)}) %collective-permute-start.7) | collective-permute-done | bytes 270368 | tf_op jit(solution)/shard_map/ppermute | solution.py:323
  326.9 5.8 %collective-permute-done.8 = bf16[1056,128]{1,0:T(8,128)(2,1)S(1)} collective-permute-done((bf16[1056,128]{1,0:T(8,128)(2,1)S(1)}, bf16[1056,128]{1,0:T(8,128)(2,1)S(1)}, u32[]{:S(2)}, u32[]{:S(2)}) %collective-permute-start.8) | collective-permute-done | bytes 270368 | tf_op jit(solution)/shard_map/ppermute | solution.py:323
  333.0 1.9 collective-permute-start.9
  334.9 10.7 %collective-permute-done.9 = bf16[16,5376]{1,0:T(8,128)(2,1)S(1)} collective-permute-done((bf16[16,5376]{1,0:T(8,128)(2,1)S(1)}, bf16[16,5376]{1,0:T(8,128)(2,1)S(1)}, u32[]{:S(2)}, u32[]{:S(2)}) %collective-permute-start.9) | collective-permute-done | bytes 172064 | tf_op jit(solution)/shard_map/ppermute | solution.py:351
  345.7 8.6 %collective-permute-start.10 = (bf16[32,5376]{1,0:T(8,128)(2,1)S(1)}, bf16[32,5376]{1,0:T(8,128)(2,1)S(1)}, u32[]{:S(2)}, u32[]{:S(2)}) collective-permute-start(bf16[32,5376]{1,0:T(8,128)(2,1)S(1)} %pad_maximum_fusion), channel_id=1, source_target_pairs={{0,2},{1,3},{2,0},{3,1},{4,6},{5,7},{6,4},{7,5},{8,10},{9,11},{10,... | collective-permute-start | bytes 1032200 | tf_op jit(solution)/shard_map/ppermute | solution.py:351
  355.6 35.1 %collective-permute-done.10 = bf16[32,5376]{1,0:T(8,128)(2,1)S(1)} collective-permute-done((bf16[32,5376]{1,0:T(8,128)(2,1)S(1)}, bf16[32,5376]{1,0:T(8,128)(2,1)S(1)}, u32[]{:S(2)}, u32[]{:S(2)}) %collective-permute-start.10) | collective-permute-done | bytes 344096 | tf_op jit(solution)/shard_map/ppermute | solution.py:351
  392.7 16.1 %reduce-scatter.2.cloned.1.call-done = bf16[128,5376]{1,0:T(8,128)(2,1)} async-done(((bf16[512,5376]{1,0:T(8,128)(2,1)}), bf16[128,5376]{1,0:T(8,128)(2,1)}) %reduce-scatter.2.cloned.1.call-update) | async-done | bytes 1376272 | tf_op jit(solution)/shard_map/reduce_scatter | solution.py:454
  (98 shorter events, 31.4 us)
Async XLA Ops:
  7.2 217.2 %copy-start = (bf16[16,5376]{1,0:T(8,128)(2,1)S(1)}, bf16[16,5376]{1,0:T(8,128)(2,1)}, u32[]{:S(2)}) copy-start(bf16[16,5376]{1,0:T(8,128)(2,1)} %param.21) | copy-start | bytes 516100
  7.2 103.3 %copy-start.4 = (bf16[3,16,5376]{2,1,0:T(8,128)(2,1)S(1)}, bf16[3,16,5376]{2,1,0:T(8,128)(2,1)}, u32[]{:S(2)}) copy-start(bf16[3,16,5376]{2,1,0:T(8,128)(2,1)} %param.17) | copy-start | bytes 1548292
  7.2 103.3 %all-gather.5.cloned.1.call-start = ((), (), s32[]{:S(2)}) async-start(), calls=%async_computation.2 | async-start | bytes 6881280 | tf_op jit(solution)/shard_map/all_gather | solution.py:378
  7.9 204.9 %all-gather.7.cloned.1.call-start = ((), (), s32[]{:S(2)}) async-start(), calls=%async_computation.3 | async-start | bytes 6881280 | tf_op jit(solution)/shard_map/all_gather | solution.py:379
  8.7 400.1 %reduce-scatter.2.cloned.1.call-start = ((), (), s32[]{:S(2)}) async-start(), calls=%async_computation.1 | async-start | bytes 6881280 | tf_op jit(solution)/shard_map/reduce_scatter | solution.py:454
  110.5 4.4 %copy-start.12 = (bf16[1,512,5376]{2,1,0:T(8,128)(2,1)S(1)}, bf16[1,512,5376]{2,1,0:T(8,128)(2,1)}, u32[]{:S(2)}) copy-start(bf16[1,512,5376]{2,1,0:T(8,128)(2,1)} %all-gather.5.cloned.1.call-done) | copy-start | bytes 16515076
  110.5 11.0 %slice-start = ((s8[11010048]{0:T(1024)(128)(4,1)}), s8[4194304]{0:T(1024)(128)(4,1)S(1)}, s32[]{:S(2)}) async-start(s8[11010048]{0:T(1024)(128)(4,1)} %bitcast.64), calls=%async_computation.4 | async-start | bytes 8388608
  114.9 5.3 %copy-start.9 = (bf16[2,16,512]{2,1,0:T(8,128)(2,1)S(1)}, bf16[2,16,512]{2,1,0:T(8,128)(2,1)}, u32[]{:S(2)}) copy-start(bf16[2,16,512]{2,1,0:T(8,128)(2,1)} %refs_4_.1) | copy-start | bytes 98308
  114.9 6.5 %slice-start.1 = ((s8[11010048]{0:T(1024)(128)(4,1)}), s8[4194304]{0:T(1024)(128)(4,1)S(1)}, s32[]{:S(2)}) async-start(s8[11010048]{0:T(1024)(128)(4,1)} %bitcast.64), calls=%async_computation.5 | async-start | bytes 8388608
  114.9 6.5 %slice-start.2 = ((s8[11010048]{0:T(1024)(128)(4,1)}), s8[2621440]{0:T(1024)(128)(4,1)S(1)}, s32[]{:S(2)}) async-start(s8[11010048]{0:T(1024)(128)(4,1)} %bitcast.64), calls=%async_computation.6 | async-start | bytes 5242880
  129.8 15.8 %copy-start.15 = (bf16[16,1024]{1,0:T(8,128)(2,1)S(1)}, bf16[16,1024]{1,0:T(8,128)(2,1)}, u32[]{:S(2)}) copy-start(bf16[16,1024]{1,0:T(8,128)(2,1)} %param.18) | copy-start | bytes 98308
  129.8 25.4 %collective-permute-start = (bf16[2,512,512]{2,1,0:T(8,128)(2,1)}, bf16[2,512,512]{2,1,0:T(8,128)(2,1)S(1)}, u32[]{:S(2)}, u32[]{:S(2)}) collective-permute-start(bf16[2,512,512]{2,1,0:T(8,128)(2,1)} %rope_pair.1.refs_5_.refs_8_), channel_id=1, source_target_pairs={{0,8},{4,12},{1,9},{5,13},{2,10},{6,14},{3,11},{7,15},{16,24},{20,... | collective-permute-start | bytes 3145736 | tf_op jit(solution)/shard_map/ppermute | solution.py:22
  133.2 34.4 %collective-permute-start.1 = (bf16[2,512,512]{2,1,0:T(8,128)(2,1)}, bf16[2,512,512]{2,1,0:T(8,128)(2,1)}, u32[]{:S(2)}, u32[]{:S(2)}) collective-permute-start(bf16[2,512,512]{2,1,0:T(8,128)(2,1)} %rope_pair.1.refs_5_.refs_8_), channel_id=1, source_target_pairs={{0,4},{4,8},{8,12},{1,5},{5,9},{9,13},{2,6},{6,10},{10,14},{3,7},{... | collective-permute-start | bytes 3145736 | tf_op jit(solution)/shard_map/ppermute | solution.py:22
  145.6 22.0 %copy-start.5 = (bf16[2,512,512]{2,1,0:T(8,128)(2,1)S(1)}, bf16[2,512,512]{2,1,0:T(8,128)(2,1)}, u32[]{:S(2)}) copy-start(bf16[2,512,512]{2,1,0:T(8,128)(2,1)} %rope_pair.1.refs_5_.refs_8_) | copy-start | bytes 3145732
  147.4 44.4 %copy-start.14 = (bf16[16,1024]{1,0:T(8,128)(2,1)S(1)}, bf16[16,1024]{1,0:T(8,128)(2,1)}, u32[]{:S(2)}) copy-start(bf16[16,1024]{1,0:T(8,128)(2,1)} %param.20) | copy-start | bytes 98308
  167.7 1.2 copy-start.6
  168.9 1.1 copy-start.8
  170.0 1.2 copy-start.11
  191.9 34.5 %copy-start.3 = (bf16[512,1024]{1,0:T(8,128)(2,1)}, bf16[512,1024]{1,0:T(8,128)(2,1)S(1)}, u32[]{:S(2)}) copy-start(bf16[512,1024]{1,0:T(8,128)(2,1)S(1)} %get-tuple-element.23.refs_2_) | copy-start | bytes 3145732
  212.8 11.6 %copy-start.13 = (bf16[1,512,5376]{2,1,0:T(8,128)(2,1)S(1)}, bf16[1,512,5376]{2,1,0:T(8,128)(2,1)}, u32[]{:S(2)}) copy-start(bf16[1,512,5376]{2,1,0:T(8,128)(2,1)} %all-gather.7.cloned.1.call-done) | copy-start | bytes 16515076
  224.3 2.3 copy-start.1
  224.4 2.3 copy-start.2
  224.4 2.3 copy-start.7
  241.8 25.6 %collective-permute-start.2 = (bf16[2,512,512]{2,1,0:T(8,128)(2,1)S(1)}, bf16[2,512,512]{2,1,0:T(8,128)(2,1)S(1)}, u32[]{:S(2)}, u32[]{:S(2)}) collective-permute-start(bf16[2,512,512]{2,1,0:T(8,128)(2,1)S(1)} %get-tuple-element.27), channel_id=1, source_target_pairs={{4,0},{8,4},{12,8},{5,1},{9,5},{13,9},{6,2},{10,6},{14,10},{7,3},{... | collective-permute-start | bytes 3145736 | tf_op jit(solution)/shard_map/ppermute | solution.py:22
  244.3 27.1 %collective-permute-start.3 = (bf16[2,512,512]{2,1,0:T(8,128)(2,1)S(1)}, bf16[2,512,512]{2,1,0:T(8,128)(2,1)S(1)}, u32[]{:S(2)}, u32[]{:S(2)}) collective-permute-start(bf16[2,512,512]{2,1,0:T(8,128)(2,1)S(1)} %get-tuple-element.28), channel_id=1, source_target_pairs={{8,0},{12,4},{9,1},{13,5},{10,2},{14,6},{11,3},{15,7},{24,16},{28,... | collective-permute-start | bytes 3145736 | tf_op jit(solution)/shard_map/ppermute | solution.py:22
  288.1 3.7 collective-permute-start.4
  292.5 4.3 %collective-permute-start.5 = (bf16[16,512]{1,0:T(8,128)(2,1)S(1)}, bf16[16,512]{1,0:T(8,128)(2,1)S(1)}, u32[]{:S(2)}, u32[]{:S(2)}) collective-permute-start(bf16[16,512]{1,0:T(8,128)(2,1)S(1)} %broadcast_select_fusion.5), channel_id=1, source_target_pairs={{0,1},{1,0},{2,3},{3,2},{4,5},{5,4},{6,7},{7,6},{8,9},{9,8},{10,11... | collective-permute-start | bytes 49160 | tf_op jit(solution)/shard_map/ppermute | solution.py:339
  304.4 13.2 %collective-permute-start.6 = (bf16[1056,128]{1,0:T(8,128)(2,1)S(1)}, bf16[1056,128]{1,0:T(8,128)(2,1)S(1)}, u32[]{:S(2)}, u32[]{:S(2)}) collective-permute-start(bf16[1056,128]{1,0:T(8,128)(2,1)S(1)} %constant_dynamic-update-slice_fusion), channel_id=1, source_target_pairs={{0,4},{4,0},{8,12},{12,8},{1,5},{5,1},{9,13},{13,9},{2,6},{6,2},{1... | collective-permute-start | bytes 811016 | tf_op jit(solution)/shard_map/ppermute | solution.py:323
  317.7 7.9 %collective-permute-start.7 = (bf16[1056,128]{1,0:T(8,128)(2,1)S(1)}, bf16[1056,128]{1,0:T(8,128)(2,1)S(1)}, u32[]{:S(2)}, u32[]{:S(2)}) collective-permute-start(bf16[1056,128]{1,0:T(8,128)(2,1)S(1)} %add_convert_fusion.3), channel_id=1, source_target_pairs={{0,8},{4,12},{8,0},{12,4},{1,9},{5,13},{9,1},{13,5},{2,10},{6,14},... | collective-permute-start | bytes 811016 | tf_op jit(solution)/shard_map/ppermute | solution.py:323
  325.6 7.0 %collective-permute-start.8 = (bf16[1056,128]{1,0:T(8,128)(2,1)S(1)}, bf16[1056,128]{1,0:T(8,128)(2,1)S(1)}, u32[]{:S(2)}, u32[]{:S(2)}) collective-permute-start(bf16[1056,128]{1,0:T(8,128)(2,1)S(1)} %add_convert_fusion.2), channel_id=1, source_target_pairs={{0,16},{16,0},{1,17},{17,1},{2,18},{18,2},{3,19},{19,3},{4,20},{20... | collective-permute-start | bytes 811016 | tf_op jit(solution)/shard_map/ppermute | solution.py:323
  333.0 12.6 %collective-permute-start.9 = (bf16[16,5376]{1,0:T(8,128)(2,1)S(1)}, bf16[16,5376]{1,0:T(8,128)(2,1)S(1)}, u32[]{:S(2)}, u32[]{:S(2)}) collective-permute-start(bf16[16,5376]{1,0:T(8,128)(2,1)S(1)} %reshape.60), channel_id=1, source_target_pairs={{0,1},{1,0},{2,3},{3,2},{4,5},{5,4},{6,7},{7,6},{8,9},{9,8},{10,11... | collective-permute-start | bytes 516104 | tf_op jit(solution)/shard_map/ppermute | solution.py:351
  345.7 45.0 %collective-permute-start.10 = (bf16[32,5376]{1,0:T(8,128)(2,1)S(1)}, bf16[32,5376]{1,0:T(8,128)(2,1)S(1)}, u32[]{:S(2)}, u32[]{:S(2)}) collective-permute-start(bf16[32,5376]{1,0:T(8,128)(2,1)S(1)} %pad_maximum_fusion), channel_id=1, source_target_pairs={{0,2},{1,3},{2,0},{3,1},{4,6},{5,7},{6,4},{7,5},{8,10},{9,11},{10,... | collective-permute-start | bytes 1032200 | tf_op jit(solution)/shard_map/ppermute | solution.py:351
  (1 other events, 1.0 us)
Sparse Core Ops, SparseCore 0:
  9.6 100.8 all-gather.4
  112.0 100.7 all-gather.6
  286.5 122.2 reduce-scatter.1

commit v4 on v3

--- a/solution.py
+++ b/solution.py
@@ -344,15 +344,29 @@
 
 def gathered_rows(block, axis):
     n, me = lax.axis_size(axis), lax.axis_index(axis)
-    if n & (n - 1):
-        return lax.all_gather(block, axis, axis=0, tiled=True)
-    step = 1
-    while step < n:
-        got = lax.ppermute(block, axis, [(i, i ^ step) for i in range(n)])
-        first = (me // step) % 2 == 0
-        block = jnp.concatenate([jnp.where(first, block, got), jnp.where(first, got, block)], 0)
-        step *= 2
-    return block
+    lower, higher = [], []
+    up = down = block
+    for t in range(1, n):
+        up = lax.ppermute(up, axis, [(i, i + 1) for i in range(t - 1, n - 1)])
+        down = lax.ppermute(down, axis, [(i, i - 1) for i in range(1, n - t + 1)])
+        lower.append(up)
+        higher.append(down)
+    rows = block.shape[0]
+    line = jnp.concatenate(lower[::-1] + [block] + higher, 0)
+    return lax.dynamic_slice_in_dim(line, (n - 1 - me) * rows, n * rows, 0)
+
+
+def returned_shares(halos):
+    n = lax.axis_size("context")
+    if len(halos) != 2:
+        count = len(halos)
+        sent = [halos[count - d] for d in range(1, count + 1)]
+        return [passed_along(b, "context", -d) for d, b in enumerate(sent, 1)], sent[0]
+    far, near = halos
+    relayed = lax.ppermute(far, "context", [(i, i - 1) for i in range(3, n, 2)])
+    direct = lax.ppermute(far, "context", [(i, i - 2) for i in range(2, n, 2)])
+    near = (near.astype(f32) + relayed.astype(f32)).astype(bf16)
+    return [lax.ppermute(near, "context", [(i, i - 1) for i in range(1, n)]), direct], near
 
 
 def local(
@@ -430,10 +444,8 @@
     grad_query, *grad_halos, grad_own = attention_backward(
         queries, grad_attended, attended, weights, pairs, cosine, sine
     )
-    shares = [
-        passed_along(grad_halos[halo_count - distance], "context", -distance)
-        for distance in range(1, halo_count + 1)
-    ]
+    shares, last_sent = returned_shares(grad_halos)
+    grad_query = after(grad_query, last_sent)
     first_term = jnp.einsum(
         "th,dh->td", grad_query, query_weight, preferred_element_type=f32
     ).astype(bf16)

time: 416 us -> 406 us (0.976); the launches traced: 415 us -> 401 us
  waiting for transfers between devices: 225 us -> 208 us
    ppermute x4 -> x2, waiting for transfers between devices: 27.2 us -> 13.2 us  [passed_along(): return lax.ppermute(block, axis, route)]
    ppermute x2 -> x9, starting transfers between devices: 10.5 us -> 21.6 us  [the longest x3 8.13 us: gathered_rows(): down = lax.ppermute(down, axis, [(i, i - 1) for i in range(1, n - t + 1)])]
    ppermute x3, starting transfers between devices: 13.3 us -> 2.68 us  [summed_pairwise(): other = lax.ppermute(block, axis, [(i, i ^ step) for i in range(n)])]
    ppermute x4 -> x2, starting transfers between devices: 9.19 us -> 5.46 us  [passed_along(): return lax.ppermute(block, axis, route)]
    ppermute x2 -> x9, waiting for transfers between devices: 45.8 us -> 45.6 us  [the longest x3 24.2 us: gathered_rows(): down = lax.ppermute(down, axis, [(i, i - 1) for i in range(1, n - t + 1)])]
  transfers between devices with their start and end apart: 14 -> 19, of which waited for: 14 -> 15; matrix products, arithmetic and copies ran while one was open for 14% -> 16% of each run, Pallas kernels for 7% -> 8%
where the time goes in v4:
time: 406 us; the launch traced here: 401 us
  waiting for transfers between devices  208 us (51%)
  matrix products  63.8 us (16%)
  Pallas kernels  60.5 us (15%)
  starting transfers between devices  35.1 us (9%)
  between operations  14.2 us (3%)
  local copies, waits for them, and re-layouts  11.4 us (3%)
  other arithmetic  7.73 us (2%)
    all_gather x1, waiting for transfers between devices, local(): gathered = lax.all_gather(tokens[0], 'tensor', axis=0, tiled=True)  97.1 us
    ppermute x3, waiting for transfers between devices, gathered_rows(): down = lax.ppermute(down, axis, [(i, i - 1) for i in range(1, n - t + 1)])  24.2 us
    pallas_call x1, Pallas kernels, attention_forward(): pl.pallas_call(functools.partial(forward_kernel, halo_rows, group, rows),...  20.6 us
    all_gather x1, waiting for transfers between devices, local(): incoming = lax.all_gather(output_gradient[0], 'tensor', axis=0, tiled=True)  20.5 us
    dot_general x3, matrix products, projected(): jnp.dot(gathered, weight, preferred_element_type=f32)  18.5 us
    ppermute x3, waiting for transfers between devices, gathered_rows(): up = lax.ppermute(up, axis, [(i, i + 1) for i in range(t - 1, n - 1)])  15.2 us
    pallas_call x1, Pallas kernels, term_sum(): pl.pallas_call(term_kernel, grid=(width // tile,), in_specs=[pl.BlockSpec...  15.2 us
    pallas_call x1, Pallas kernels, attention_backward(): pl.pallas_call(functools.partial(backward_kernel, halo_rows, group, rows,...  14.7 us
  transfers between devices with their start and end apart: 19, of which 15 were waited for; matrix products, arithmetic and copies ran while one was open for 16% of the time, Pallas kernels for 8%

profile of v4, /device:TPU:9, one launch (start us, length us, event | category | flops | bytes accessed | tf_op | source)
XLA Modules:
  0.0 401.0 jit_solution(6408664037074916113)
XLA Ops:
  13.4 97.1 %all-gather.5.cloned.1.call-done = bf16[1,512,5376]{2,1,0:T(8,128)(2,1)} async-done(((bf16[1,128,5376]{2,1,0:T(8,128)(2,1)}), bf16[1,512,5376]{2,1,0:T(8,128)(2,1)}) %all-gather.5.cloned.1.call-update) | async-done | bytes 5505040 | tf_op jit(solution)/shard_map/all_gather | solution.py:392
  110.5 4.4 %fusion.16 = bf16[512,48]{0,1:T(8,128)(2,1)S(1)} fusion(bf16[48,5376]{1,0:T(8,128)(2,1)S(1)} %bitcast.59, bf16[1,512,5376]{2,1,0:T(8,128)(2,1)} %all-gather.5.cloned.1.call-done), kind=kOutput, calls=%fused_computation.23 | convolution fusion | flops 264265728 | bytes 6070272 | tf_op jit(solution)/shard_map/ja,ma->jm/dot_general | solution.py:408
  114.9 5.2 %fusion.3 = f32[512,512]{1,0:T(8,128)S(1)} fusion(bf16[1,512,5376]{2,1,0:T(8,128)(2,1)S(1)} %copy-done.14, bf16[2,5376,512]{2,1,0:T(8,128)(2,1)} %refs_2_.1), kind=kOutput, calls=%fused_computation.5 | convolution fusion | flops 2818572288 | bytes 12058624 | tf_op jit(solution)/shard_map/dot_general | solution.py:414
  121.5 3.0 fusion.1
  125.8 4.0 %rope_pair.1.refs_5_.refs_8_ = bf16[2,512,512]{2,1,0:T(8,128)(2,1)} custom-call(f32[512,512]{1,0:T(8,128)} %fusion.15.k_ref, f32[512,512]{1,0:T(8,128)} %fusion.14.v_ref, f32[512,128]{1,0:T(8,128)} %get-tuple-element.41.cos_ref.refs_4_.refs_5_, f32[512,128]{1,0:T(8,128)} %get-tuple-element.42.sin_ref.refs_5_.refs_6_), custom_call_target="tpu_custom_call" | custom-call | flops 1048576 | bytes 3145728 | tf_op jit(solution)/shard_map/rope_pair/pallas_call | solution.py:73
  129.9 3.4 collective-permute-start
  133.2 2.1 collective-permute-start.1
  135.3 10.3 %fusion.10 = f32[512,1024]{1,0:T(8,128)S(1)} fusion(bf16[5376,1024]{1,0:T(8,128)(2,1)} %param.14, bf16[1,512,5376]{2,1,0:T(8,128)(2,1)} %all-gather.5.cloned.1.call-done), kind=kOutput, calls=%fused_computation.12 | convolution fusion | flops 5637144576 | bytes 18612224 | tf_op jit(solution)/shard_map/dot_general | solution.py:414
  147.4 6.0 %rope_query.1.refs_0_ = bf16[512,1024]{1,0:T(8,128)(2,1)} custom-call(f32[512,1024]{1,0:T(8,128)} %multiply_add_fusion.x_ref, f32[512,128]{1,0:T(8,128)} %get-tuple-element.41.cos_ref.refs_4_.refs_5_, f32[512,128]{1,0:T(8,128)} %get-tuple-element.42.sin_ref.refs_5_.refs_6_), custom_call_target="tpu_custom_call" | custom-call | flops 2097152 | bytes 3145728 | tf_op jit(solution)/shard_map/rope_query/pallas_call | solution.py:58
  156.3 11.4 %collective-permute-done.1.refs_4_.refs_7_ = bf16[2,512,512]{2,1,0:T(8,128)(2,1)} collective-permute-done((bf16[2,512,512]{2,1,0:T(8,128)(2,1)}, bf16[2,512,512]{2,1,0:T(8,128)(2,1)}, u32[]{:S(2)}, u32[]{:S(2)}) %collective-permute-start.1) | collective-permute-done | bytes 1048608 | tf_op jit(solution)/shard_map/ppermute | solution.py:22
  171.3 20.6 %attention_forward.1 = (bf16[8,1536,512]{2,1,0:T(8,128)(2,1)}, bf16[512,1024]{1,0:T(8,128)(2,1)S(1)}) custom-call(bf16[512,1024]{1,0:T(8,128)(2,1)S(1)} %copy-done.8, s32[1,512]{1,0:T(1,128)S(1)} %constant_dynamic-slice_fusion.refs_1_, s32[1536,1]{1,0:T(8,128)S(1)} %copy-done.10, bf16[2,512,512]{2,1,0:T(8,128)(2,1)S(1)} %copy-done.13, ...), custom_call_target="tpu_custom_call" | custom-call | flops 3221225472 | bytes 41943040 | tf_op jit(solution)/shard_map/attention_forward/pallas_call | solution.py:140
  192.3 20.5 %all-gather.7.cloned.1.call-done = bf16[1,512,5376]{2,1,0:T(8,128)(2,1)} async-done(((bf16[1,128,5376]{2,1,0:T(8,128)(2,1)}), bf16[1,512,5376]{2,1,0:T(8,128)(2,1)}) %all-gather.7.cloned.1.call-update) | async-done | bytes 5505040 | tf_op jit(solution)/shard_map/all_gather | solution.py:393
  212.8 11.6 %fusion.46 = f32[512,1024]{1,0:T(8,128)S(1)} fusion(bf16[512,5376]{1,0:T(8,128)(2,1)} %bitcast.61, bf16[1024,5376]{1,0:T(8,128)(2,1)} %param.16), kind=kOutput, calls=%fused_computation.91 | convolution fusion | flops 5637144576 | bytes 18612224 | tf_op jit(solution)/shard_map/td,hd->th/dot_general | solution.py:441
  226.4 14.7 %attention_backward.1 = (bf16[512,1024]{1,0:T(8,128)(2,1)S(1)}, bf16[2,512,512]{2,1,0:T(8,128)(2,1)}, bf16[2,512,512]{2,1,0:T(8,128)(2,1)S(1)}, f32[2,512,512]{2,1,0:T(8,128)}) custom-call(bf16[512,1024]{1,0:T(8,128)(2,1)S(1)} %copy-done.9, bf16[512,1024]{1,0:T(8,128)(2,1)S(1)} %add_convert_fusion.1.refs_1_, bf16[512,1024]{1,0:T(8,128)(2,1)} %copy-done.4, ...), custom_call_target="tpu_custom_call" | custom-call | flops 6442450944 | bytes 20971520 | tf_op jit(solution)/shard_map/attention_backward/pallas_call | solution.py:209
  245.9 2.5 add_convert_fusion.refs_1_
  253.6 12.0 %convolution_convert_fusion.refs_0_ = bf16[512,5376]{1,0:T(8,128)(2,1)} fusion(bf16[512,1024]{1,0:T(8,128)(2,1)} %after.2, bf16[5376,1024]{1,0:T(8,128)(2,1)} %param.14), kind=kOutput, calls=%fused_computation | convolution fusion | flops 5639897088 | bytes 17563648 | tf_op jit(solution)/shard_map/th,dh->td/dot_general | solution.py:449
  265.6 6.2 %collective-permute-done.3.refs_8_ = bf16[2,512,512]{2,1,0:T(8,128)(2,1)S(1)} collective-permute-done((bf16[2,512,512]{2,1,0:T(8,128)(2,1)}, bf16[2,512,512]{2,1,0:T(8,128)(2,1)S(1)}, u32[]{:S(2)}, u32[]{:S(2)}) %collective-permute-start.3) | collective-permute-done | bytes 1048608 | tf_op jit(solution)/shard_map/ppermute | solution.py:369
  271.7 15.2 %input_term.1 = (bf16[512,5376]{1,0:T(8,128)(2,1)}, bf16[512,512]{1,0:T(8,128)(2,1)S(1)}, bf16[512,512]{1,0:T(8,128)(2,1)S(1)}, bf16[48,512]{1,0:T(8,128)(2,1)S(1)}) custom-call(bf16[512,5376]{1,0:T(8,128)(2,1)} %convolution_convert_fusion.refs_0_, f32[16,512]{1,0:T(8,128)S(1)} %fusion.20.refs_1_, bf16[2,5376,512]{2,1,0:T(8,128)(2,1)} %refs_2_.1, ...), custom_call_target="tpu_custom_call" | custom-call | flops 5637144576 | bytes 29360128 | tf_op jit(solution)/shard_map/input_term/pallas_call | solution.py:275
  292.8 3.2 collective-permute-start.6
  297.9 3.4 fusion.28
  301.3 3.4 fusion
  308.1 6.8 %collective-permute-done.8 = bf16[1056,128]{1,0:T(8,128)(2,1)S(1)} collective-permute-done((bf16[1056,128]{1,0:T(8,128)(2,1)S(1)}, bf16[1056,128]{1,0:T(8,128)(2,1)S(1)}, u32[]{:S(2)}, u32[]{:S(2)}) %collective-permute-start.8) | collective-permute-done | bytes 270368 | tf_op jit(solution)/shard_map/ppermute | solution.py:323
  316.2 6.1 %collective-permute-done.9 = bf16[1056,128]{1,0:T(8,128)(2,1)S(1)} collective-permute-done((bf16[1056,128]{1,0:T(8,128)(2,1)S(1)}, bf16[1056,128]{1,0:T(8,128)(2,1)S(1)}, u32[]{:S(2)}, u32[]{:S(2)}) %collective-permute-start.9) | collective-permute-done | bytes 270368 | tf_op jit(solution)/shard_map/ppermute | solution.py:323
  322.6 3.0 collective-permute-start.10
  325.6 4.0 %collective-permute-start.13 = (bf16[16,5376]{1,0:T(8,128)(2,1)S(1)}, bf16[16,5376]{1,0:T(8,128)(2,1)S(1)}, u32[]{:S(2)}, u32[]{:S(2)}) collective-permute-start(bf16[16,5376]{1,0:T(8,128)(2,1)S(1)} %reshape.60), channel_id=1, source_target_pairs={{1,0},{2,1},{3,2},{5,4},{6,5},{7,6},{9,8},{10,9},{11,10},{13,12},{... | collective-permute-start | bytes 516104 | tf_op jit(solution)/shard_map/ppermute | solution.py:351
  329.7 7.5 %collective-permute-done.10 = bf16[16,5376]{1,0:T(8,128)(2,1)S(1)} collective-permute-done((bf16[16,5376]{1,0:T(8,128)(2,1)S(1)}, bf16[16,5376]{1,0:T(8,128)(2,1)S(1)}, u32[]{:S(2)}, u32[]{:S(2)}) %collective-permute-start.10) | collective-permute-done | bytes 172064 | tf_op jit(solution)/shard_map/ppermute | solution.py:350
  337.1 4.2 %collective-permute-start.11 = (bf16[16,5376]{1,0:T(8,128)(2,1)S(1)}, bf16[16,5376]{1,0:T(8,128)(2,1)S(1)}, u32[]{:S(2)}, u32[]{:S(2)}) collective-permute-start(bf16[16,5376]{1,0:T(8,128)(2,1)S(1)} %collective-permute-done.10), channel_id=1, source_target_pairs={{1,2},{2,3},{5,6},{6,7},{9,10},{10,11},{13,14},{14,15},{17,18},{18... | collective-permute-start | bytes 516104 | tf_op jit(solution)/shard_map/ppermute | solution.py:350
  342.0 2.8 collective-permute-start.14
  344.8 7.7 %collective-permute-done.11 = bf16[16,5376]{1,0:T(8,128)(2,1)S(1)} collective-permute-done((bf16[16,5376]{1,0:T(8,128)(2,1)S(1)}, bf16[16,5376]{1,0:T(8,128)(2,1)S(1)}, u32[]{:S(2)}, u32[]{:S(2)}) %collective-permute-start.11) | collective-permute-done | bytes 172064 | tf_op jit(solution)/shard_map/ppermute | solution.py:350
  353.9 9.2 %collective-permute-done.14 = bf16[16,5376]{1,0:T(8,128)(2,1)S(1)} collective-permute-done((bf16[16,5376]{1,0:T(8,128)(2,1)S(1)}, bf16[16,5376]{1,0:T(8,128)(2,1)S(1)}, u32[]{:S(2)}, u32[]{:S(2)}) %collective-permute-start.14) | collective-permute-done | bytes 172064 | tf_op jit(solution)/shard_map/ppermute | solution.py:351
  364.5 15.0 %collective-permute-done.15 = bf16[16,5376]{1,0:T(8,128)(2,1)S(1)} collective-permute-done((bf16[16,5376]{1,0:T(8,128)(2,1)S(1)}, bf16[16,5376]{1,0:T(8,128)(2,1)S(1)}, u32[]{:S(2)}, u32[]{:S(2)}) %collective-permute-start.15) | collective-permute-done | bytes 172064 | tf_op jit(solution)/shard_map/ppermute | solution.py:351
  381.4 13.0 %reduce-scatter.2.cloned.1.call-done = bf16[128,5376]{1,0:T(8,128)(2,1)} async-done(((bf16[512,5376]{1,0:T(8,128)(2,1)}), bf16[128,5376]{1,0:T(8,128)(2,1)}) %reduce-scatter.2.cloned.1.call-update) | async-done | bytes 1376272 | tf_op jit(solution)/shard_map/reduce_scatter | solution.py:466
  (118 shorter events, 47.4 us)
Async XLA Ops:
  7.2 217.2 %copy-start = (bf16[16,5376]{1,0:T(8,128)(2,1)S(1)}, bf16[16,5376]{1,0:T(8,128)(2,1)}, u32[]{:S(2)}) copy-start(bf16[16,5376]{1,0:T(8,128)(2,1)} %param.21) | copy-start | bytes 516100
  7.2 103.3 %copy-start.6 = (bf16[3,16,5376]{2,1,0:T(8,128)(2,1)S(1)}, bf16[3,16,5376]{2,1,0:T(8,128)(2,1)}, u32[]{:S(2)}) copy-start(bf16[3,16,5376]{2,1,0:T(8,128)(2,1)} %param.17) | copy-start | bytes 1548292
  7.2 103.3 %all-gather.5.cloned.1.call-start = ((), (), s32[]{:S(2)}) async-start(), calls=%async_computation.2 | async-start | bytes 6881280 | tf_op jit(solution)/shard_map/all_gather | solution.py:392
  7.9 204.9 %all-gather.7.cloned.1.call-start = ((), (), s32[]{:S(2)}) async-start(), calls=%async_computation.3 | async-start | bytes 6881280 | tf_op jit(solution)/shard_map/all_gather | solution.py:393
  8.7 385.8 %reduce-scatter.2.cloned.1.call-start = ((), (), s32[]{:S(2)}) async-start(), calls=%async_computation.1 | async-start | bytes 6881280 | tf_op jit(solution)/shard_map/reduce_scatter | solution.py:466
  110.5 4.4 %copy-start.14 = (bf16[1,512,5376]{2,1,0:T(8,128)(2,1)S(1)}, bf16[1,512,5376]{2,1,0:T(8,128)(2,1)}, u32[]{:S(2)}) copy-start(bf16[1,512,5376]{2,1,0:T(8,128)(2,1)} %all-gather.5.cloned.1.call-done) | copy-start | bytes 16515076
  110.5 11.0 %slice-start = ((s8[11010048]{0:T(1024)(128)(4,1)}), s8[4194304]{0:T(1024)(128)(4,1)S(1)}, s32[]{:S(2)}) async-start(s8[11010048]{0:T(1024)(128)(4,1)} %bitcast.64), calls=%async_computation.4 | async-start | bytes 8388608
  114.9 5.3 %copy-start.11 = (bf16[2,16,512]{2,1,0:T(8,128)(2,1)S(1)}, bf16[2,16,512]{2,1,0:T(8,128)(2,1)}, u32[]{:S(2)}) copy-start(bf16[2,16,512]{2,1,0:T(8,128)(2,1)} %refs_4_.1) | copy-start | bytes 98308
  114.9 6.5 %slice-start.1 = ((s8[11010048]{0:T(1024)(128)(4,1)}), s8[4194304]{0:T(1024)(128)(4,1)S(1)}, s32[]{:S(2)}) async-start(s8[11010048]{0:T(1024)(128)(4,1)} %bitcast.64), calls=%async_computation.5 | async-start | bytes 8388608
  114.9 6.5 %slice-start.2 = ((s8[11010048]{0:T(1024)(128)(4,1)}), s8[2621440]{0:T(1024)(128)(4,1)S(1)}, s32[]{:S(2)}) async-start(s8[11010048]{0:T(1024)(128)(4,1)} %bitcast.64), calls=%async_computation.6 | async-start | bytes 5242880
  129.9 15.8 %copy-start.17 = (bf16[16,1024]{1,0:T(8,128)(2,1)S(1)}, bf16[16,1024]{1,0:T(8,128)(2,1)}, u32[]{:S(2)}) copy-start(bf16[16,1024]{1,0:T(8,128)(2,1)} %param.18) | copy-start | bytes 98308
  129.9 25.4 %collective-permute-start = (bf16[2,512,512]{2,1,0:T(8,128)(2,1)}, bf16[2,512,512]{2,1,0:T(8,128)(2,1)S(1)}, u32[]{:S(2)}, u32[]{:S(2)}) collective-permute-start(bf16[2,512,512]{2,1,0:T(8,128)(2,1)} %rope_pair.1.refs_5_.refs_8_), channel_id=1, source_target_pairs={{0,8},{4,12},{1,9},{5,13},{2,10},{6,14},{3,11},{7,15},{16,24},{20,... | collective-permute-start | bytes 3145736 | tf_op jit(solution)/shard_map/ppermute | solution.py:22
  133.2 34.4 %collective-permute-start.1 = (bf16[2,512,512]{2,1,0:T(8,128)(2,1)}, bf16[2,512,512]{2,1,0:T(8,128)(2,1)}, u32[]{:S(2)}, u32[]{:S(2)}) collective-permute-start(bf16[2,512,512]{2,1,0:T(8,128)(2,1)} %rope_pair.1.refs_5_.refs_8_), channel_id=1, source_target_pairs={{0,4},{4,8},{8,12},{1,5},{5,9},{9,13},{2,6},{6,10},{10,14},{3,7},{... | collective-permute-start | bytes 3145736 | tf_op jit(solution)/shard_map/ppermute | solution.py:22
  145.6 22.0 %copy-start.7 = (bf16[2,512,512]{2,1,0:T(8,128)(2,1)S(1)}, bf16[2,512,512]{2,1,0:T(8,128)(2,1)}, u32[]{:S(2)}) copy-start(bf16[2,512,512]{2,1,0:T(8,128)(2,1)} %rope_pair.1.refs_5_.refs_8_) | copy-start | bytes 3145732
  147.4 44.5 %copy-start.16 = (bf16[16,1024]{1,0:T(8,128)(2,1)S(1)}, bf16[16,1024]{1,0:T(8,128)(2,1)}, u32[]{:S(2)}) copy-start(bf16[16,1024]{1,0:T(8,128)(2,1)} %param.20) | copy-start | bytes 98308
  191.9 32.5 %copy-start.4 = (bf16[512,1024]{1,0:T(8,128)(2,1)}, bf16[512,1024]{1,0:T(8,128)(2,1)S(1)}, u32[]{:S(2)}) copy-start(bf16[512,1024]{1,0:T(8,128)(2,1)S(1)} %get-tuple-element.23.refs_2_) | copy-start | bytes 3145732
  212.8 11.6 %copy-start.15 = (bf16[1,512,5376]{2,1,0:T(8,128)(2,1)S(1)}, bf16[1,512,5376]{2,1,0:T(8,128)(2,1)}, u32[]{:S(2)}) copy-start(bf16[1,512,5376]{2,1,0:T(8,128)(2,1)} %all-gather.7.cloned.1.call-done) | copy-start | bytes 16515076
  226.4 19.2 %copy-start.5 = (bf16[512,1024]{1,0:T(8,128)(2,1)S(1)}, bf16[512,1024]{1,0:T(8,128)(2,1)}, u32[]{:S(2)}) copy-start(bf16[512,1024]{1,0:T(8,128)(2,1)} %copy-done.4) | copy-start | bytes 3145732
  242.1 3.8 collective-permute-start.2
  243.8 21.8 %collective-permute-start.4 = (bf16[2,512,512]{2,1,0:T(8,128)(2,1)}, bf16[2,512,512]{2,1,0:T(8,128)(2,1)}, u32[]{:S(2)}, u32[]{:S(2)}) collective-permute-start(bf16[2,512,512]{2,1,0:T(8,128)(2,1)} %get-tuple-element.27), channel_id=1, source_target_pairs={{8,0},{9,1},{10,2},{11,3},{24,16},{25,17},{26,18},{27,19}} | collective-permute-start | bytes 3145736 | tf_op jit(solution)/shard_map/ppermute | solution.py:367
  248.4 23.3 %collective-permute-start.3 = (bf16[2,512,512]{2,1,0:T(8,128)(2,1)}, bf16[2,512,512]{2,1,0:T(8,128)(2,1)S(1)}, u32[]{:S(2)}, u32[]{:S(2)}) collective-permute-start(bf16[2,512,512]{2,1,0:T(8,128)(2,1)} %add_convert_fusion.refs_1_), channel_id=1, source_target_pairs={{4,0},{8,4},{12,8},{5,1},{9,5},{13,9},{6,2},{10,6},{14,10},{7,3},{... | collective-permute-start | bytes 3145736 | tf_op jit(solution)/shard_map/ppermute | solution.py:369
  288.4 3.7 collective-permute-start.5
  292.8 5.1 %collective-permute-start.6 = (bf16[16,512]{1,0:T(8,128)(2,1)S(1)}, bf16[16,512]{1,0:T(8,128)(2,1)S(1)}, u32[]{:S(2)}, u32[]{:S(2)}) collective-permute-start(bf16[16,512]{1,0:T(8,128)(2,1)S(1)} %broadcast_select_fusion.1), channel_id=1, source_target_pairs={{0,1},{1,0},{2,3},{3,2},{4,5},{5,4},{6,7},{7,6},{8,9},{9,8},{10,11... | collective-permute-start | bytes 49160 | tf_op jit(solution)/shard_map/ppermute | solution.py:339
  305.1 1.6 collective-permute-start.7
  306.8 8.1 %collective-permute-start.8 = (bf16[1056,128]{1,0:T(8,128)(2,1)S(1)}, bf16[1056,128]{1,0:T(8,128)(2,1)S(1)}, u32[]{:S(2)}, u32[]{:S(2)}) collective-permute-start(bf16[1056,128]{1,0:T(8,128)(2,1)S(1)} %add_convert_fusion.4), channel_id=1, source_target_pairs={{0,8},{4,12},{8,0},{12,4},{1,9},{5,13},{9,1},{13,5},{2,10},{6,14},... | collective-permute-start | bytes 811016 | tf_op jit(solution)/shard_map/ppermute | solution.py:323
  315.0 7.3 %collective-permute-start.9 = (bf16[1056,128]{1,0:T(8,128)(2,1)S(1)}, bf16[1056,128]{1,0:T(8,128)(2,1)S(1)}, u32[]{:S(2)}, u32[]{:S(2)}) collective-permute-start(bf16[1056,128]{1,0:T(8,128)(2,1)S(1)} %add_convert_fusion.3), channel_id=1, source_target_pairs={{0,16},{16,0},{1,17},{17,1},{2,18},{18,2},{3,19},{19,3},{4,20},{20... | collective-permute-start | bytes 811016 | tf_op jit(solution)/shard_map/ppermute | solution.py:323
  322.6 14.5 %collective-permute-start.10 = (bf16[16,5376]{1,0:T(8,128)(2,1)S(1)}, bf16[16,5376]{1,0:T(8,128)(2,1)S(1)}, u32[]{:S(2)}, u32[]{:S(2)}) collective-permute-start(bf16[16,5376]{1,0:T(8,128)(2,1)S(1)} %reshape.60), channel_id=1, source_target_pairs={{0,1},{1,2},{2,3},{4,5},{5,6},{6,7},{8,9},{9,10},{10,11},{12,13},{... | collective-permute-start | bytes 516104 | tf_op jit(solution)/shard_map/ppermute | solution.py:350
  325.6 16.5 %collective-permute-start.13 = (bf16[16,5376]{1,0:T(8,128)(2,1)S(1)}, bf16[16,5376]{1,0:T(8,128)(2,1)S(1)}, u32[]{:S(2)}, u32[]{:S(2)}) collective-permute-start(bf16[16,5376]{1,0:T(8,128)(2,1)S(1)} %reshape.60), channel_id=1, source_target_pairs={{1,0},{2,1},{3,2},{5,4},{6,5},{7,6},{9,8},{10,9},{11,10},{13,12},{... | collective-permute-start | bytes 516104 | tf_op jit(solution)/shard_map/ppermute | solution.py:351
  337.1 15.4 %collective-permute-start.11 = (bf16[16,5376]{1,0:T(8,128)(2,1)S(1)}, bf16[16,5376]{1,0:T(8,128)(2,1)S(1)}, u32[]{:S(2)}, u32[]{:S(2)}) collective-permute-start(bf16[16,5376]{1,0:T(8,128)(2,1)S(1)} %collective-permute-done.10), channel_id=1, source_target_pairs={{1,2},{2,3},{5,6},{6,7},{9,10},{10,11},{13,14},{14,15},{17,18},{18... | collective-permute-start | bytes 516104 | tf_op jit(solution)/shard_map/ppermute | solution.py:350
  342.0 21.1 %collective-permute-start.14 = (bf16[16,5376]{1,0:T(8,128)(2,1)S(1)}, bf16[16,5376]{1,0:T(8,128)(2,1)S(1)}, u32[]{:S(2)}, u32[]{:S(2)}) collective-permute-start(bf16[16,5376]{1,0:T(8,128)(2,1)S(1)} %collective-permute-done.13), channel_id=1, source_target_pairs={{1,0},{2,1},{5,4},{6,5},{9,8},{10,9},{13,12},{14,13},{17,16},{18,1... | collective-permute-start | bytes 516104 | tf_op jit(solution)/shard_map/ppermute | solution.py:351
  352.6 11.8 %collective-permute-start.12 = (bf16[16,5376]{1,0:T(8,128)(2,1)S(1)}, bf16[16,5376]{1,0:T(8,128)(2,1)S(1)}, u32[]{:S(2)}, u32[]{:S(2)}) collective-permute-start(bf16[16,5376]{1,0:T(8,128)(2,1)S(1)} %collective-permute-done.11), channel_id=1, source_target_pairs={{2,3},{6,7},{10,11},{14,15},{18,19},{22,23},{26,27},{30,31}} | collective-permute-start | bytes 516104 | tf_op jit(solution)/shard_map/ppermute | solution.py:350
  363.1 16.4 %collective-permute-start.15 = (bf16[16,5376]{1,0:T(8,128)(2,1)S(1)}, bf16[16,5376]{1,0:T(8,128)(2,1)S(1)}, u32[]{:S(2)}, u32[]{:S(2)}) collective-permute-start(bf16[16,5376]{1,0:T(8,128)(2,1)S(1)} %collective-permute-done.14), channel_id=1, source_target_pairs={{1,0},{5,4},{9,8},{13,12},{17,16},{21,20},{25,24},{29,28}} | collective-permute-start | bytes 516104 | tf_op jit(solution)/shard_map/ppermute | solution.py:351
  (8 other events, 11.7 us)
Sparse Core Ops, SparseCore 0:
  9.6 100.8 all-gather.4
  112.0 100.7 all-gather.6
  287.1 107.3 reduce-scatter.1
